TPU v7x, 32 devices: a whole 2x2x4 slice. The times are simulated.
32 devices in a mesh: dp: 8 (over z, y), tensor: 4 (over x, core).
Axes of the slice: x: 2, y: 2, z: 4, core: 2. Of those that a mesh axis runs over, the one named last changes fastest.
Arguments:
- tokens: bfloat16 [16384, 1120], P(('dp', 'tensor')), may hold values from -6 to 6
- cotangent: bfloat16 [16384, 1120], P(('dp', 'tensor')), may hold values from -6 to 6
- ln1_gain: float32 [1120], replicated, may hold values from 0.5 to 1.5
- ln1_bias: float32 [1120], replicated, may hold values from -1.25 to 1.25
- attn_weight: bfloat16 [1120, 3, 1120], P(None, None, 'tensor'), may hold values from -0.1875 to 0.1875
- qv_bias: float32 [2, 1120], P(None, 'tensor'), may hold values from -1.75 to 1.75
- out_weight: bfloat16 [1120, 1120], P('tensor'), may hold values from -0.75 to 0.75
- out_bias: float32 [1120], replicated, may hold values from -1.25 to 1.25
- ln2_gain: float32 [1120], replicated, may hold values from 0.5 to 1.5
- ln2_bias: float32 [1120], replicated, may hold values from -1.25 to 1.25
- up_weight: bfloat16 [1120, 4480], P(None, 'tensor'), may hold values from -0.1875 to 0.1875
- up_bias: float32 [4480], P('tensor'), may hold values from -1.75 to 1.75
- down_weight: bfloat16 [4480, 1120], P('tensor'), may hold values from -0.09375 to 0.09375
- down_bias: float32 [1120], replicated, may hold values from -1.25 to 1.25
- cell_lengths: int32 [8, 11], P('dp'), may hold values from 0 to 1000, as said below
- cell_offsets: int32 [8, 11], P('dp'), may hold values from 0 to 2048, as said below
Outputs:
- layer_out: bfloat16 [16384, 1120], P(('dp', 'tensor'))
- input_grad: bfloat16 [16384, 1120], P(('dp', 'tensor'))
- ln1_gain_grad: float32 [1120], replicated
- ln1_bias_grad: float32 [1120], replicated
- attn_weight_grad: float32 [1120, 3, 1120], P(None, None, 'tensor')
- qv_bias_grad: float32 [2, 1120], P(None, 'tensor')
- out_weight_grad: float32 [1120, 1120], P('tensor')
- out_bias_grad: float32 [1120], replicated
- ln2_gain_grad: float32 [1120], replicated
- ln2_bias_grad: float32 [1120], replicated
- up_weight_grad: float32 [1120, 4480], P(None, 'tensor')
- up_bias_grad: float32 [4480], P('tensor')
- down_weight_grad: float32 [4480, 1120], P('tensor')
- down_bias_grad: float32 [1120], replicated
Inputs may be any that keep to these rules, and one draw needn't show every extreme that they name: `cell_lengths`: in each index of dp the cells are laid out slot by slot in increasing order with gaps of padding; a length 0 marks an empty slot, all later slots are empty too, and every index has an empty slot. Lengths of used slots lie between 200 and 1000, with a heavy tail. `cell_offsets`: A used slot's cell covers slots offset to offset + length - 1 of its index, after the previous cell's end; empty slots have offset 2048.
All inputs are finite; a program needn't handle non-finite values.
Results may differ from a plain program's by a relative error of at most 0.015.
Values may be sent and summed in bfloat16 or wider, within the bound.
No kernel may reach another device: no remote copies, remote signals or barrier semaphores. Data moves between devices by JAX's collectives and lax.ppermute only.
A program may use at most 192 MiB of HBM per device.

v0:
```python
import math

import jax
import jax.numpy as jnp
from jax import lax
from jax.sharding import PartitionSpec as P

HEAD_DIM = 56


big_negative = -1e30
eps_norm = 1e-05


def layer_norm(values, gain, shift):
    center = values - jnp.mean(values, axis=-1, keepdims=True)
    spread = jnp.mean(center * center, axis=-1, keepdims=True)
    return center * lax.rsqrt(spread + eps_norm) * gain + shift


def smooth_gelu(values):
    return jax.nn.gelu(values, approximate=True)


def cell_labels(lengths, offsets, total):
    places = jnp.arange(total, dtype=jnp.int32)[:, None]
    inside = (places >= offsets[None, :]) & (places < offsets[None, :] + lengths[None, :])
    labels = jnp.arange(lengths.shape[0], dtype=jnp.int32)[None, :] + 1
    return jnp.sum(jnp.where(inside, labels, 0), axis=1) - 1


def allowed_keys(cells, start, width):
    total = cells.shape[0]
    query_pos = start + jnp.arange(width, dtype=jnp.int32)
    key_pos = jnp.arange(total, dtype=jnp.int32)
    query_cells = lax.dynamic_slice_in_dim(cells, start, width, 0)
    same = (
        (query_cells[:, None] == cells[None, :])
        & (query_cells[:, None] >= 0)
        & (key_pos[None, :] < query_pos[:, None])
    )
    return same | (key_pos[None, :] == query_pos[:, None])


def block_scores(query_block, key_rows, cells, start, width, scale):
    scores = (
        jnp.einsum("qhe,khe->hqk", query_block, key_rows, preferred_element_type=jnp.float32)
        * scale
    )
    return jnp.where(allowed_keys(cells, start, width)[None], scores, big_negative)


def body(
    tokens,
    cotangent,
    ln1_gain,
    ln1_bias,
    attn_weight,
    qv_bias,
    out_weight,
    out_bias,
    ln2_gain,
    ln2_bias,
    up_weight,
    up_bias,
    down_weight,
    down_bias,
    cell_lengths,
    cell_offsets,
):
    rows = tokens.shape[0]
    total = rows * lax.axis_size("tensor")
    local_width = attn_weight.shape[2]
    head_count = local_width // HEAD_DIM
    scale = 1.0 / math.sqrt(HEAD_DIM)
    block = min(512, total)
    block_count = total // block
    cells = cell_labels(cell_lengths[0], cell_offsets[0], total)
    block_index = jnp.arange(block_count, dtype=jnp.int32)
    x_rows = tokens.astype(jnp.float32)
    h1_rows, norm1_back = jax.vjp(layer_norm, x_rows, ln1_gain, ln1_bias)
    h1_full = lax.all_gather(h1_rows.astype(jnp.bfloat16), "tensor", axis=0, tiled=True)
    mixed = jnp.einsum("td,dke->tke", h1_full, attn_weight, preferred_element_type=jnp.float32)
    query_rows = (
        (mixed[:, 0] + qv_bias[0]).astype(jnp.bfloat16).reshape(total, head_count, HEAD_DIM)
    )
    key_rows = mixed[:, 1].astype(jnp.bfloat16).reshape(total, head_count, HEAD_DIM)
    value_rows = (
        (mixed[:, 2] + qv_bias[1]).astype(jnp.bfloat16).reshape(total, head_count, HEAD_DIM)
    )

    def attend(index):
        start = index * block
        query_block = lax.dynamic_slice_in_dim(query_rows, start, block, 0)
        scores = block_scores(query_block, key_rows, cells, start, block, scale)
        highest = jnp.max(scores, axis=-1, keepdims=True)
        expo = jnp.exp(scores - highest)
        totals = jnp.sum(expo, axis=-1, keepdims=True)
        probs = (expo / totals).astype(jnp.bfloat16)
        result = jnp.einsum("hqk,khe->qhe", probs, value_rows, preferred_element_type=jnp.float32)
        return (result.astype(jnp.bfloat16), (highest + jnp.log(totals))[..., 0])

    attended, log_totals = lax.map(attend, block_index)
    attended = attended.reshape(total, local_width)
    piece = attended
    y1_rows = (
        x_rows
        + lax.psum_scatter(
            jnp.dot(piece, out_weight, preferred_element_type=jnp.float32),
            "tensor",
            scatter_dimension=0,
            tiled=True,
        )
        + out_bias
    )
    h2_rows, norm2_back = jax.vjp(layer_norm, y1_rows, ln2_gain, ln2_bias)
    h2_full = lax.all_gather(h2_rows.astype(jnp.bfloat16), "tensor", axis=0, tiled=True)
    hidden_pre = jnp.dot(h2_full, up_weight, preferred_element_type=jnp.float32) + up_bias
    activated, gelu_back = jax.vjp(smooth_gelu, hidden_pre)
    activated = activated.astype(jnp.bfloat16)
    piece = activated
    layer_out = (
        y1_rows
        + lax.psum_scatter(
            jnp.dot(piece, down_weight, preferred_element_type=jnp.float32).astype(jnp.bfloat16),
            "tensor",
            scatter_dimension=0,
            tiled=True,
        ).astype(jnp.float32)
        + down_bias
    ).astype(jnp.bfloat16)
    grad_full = lax.all_gather(cotangent, "tensor", axis=0, tiled=True)
    down_grad = jnp.einsum("tf,td->fd", activated, grad_full, preferred_element_type=jnp.float32)
    down_bias_grad = jnp.sum(cotangent, axis=0, dtype=jnp.float32)
    act_grad = jnp.einsum("td,fd->tf", grad_full, down_weight, preferred_element_type=jnp.float32)
    pre_grad = gelu_back(act_grad)[0].astype(jnp.bfloat16)
    up_grad = jnp.einsum("td,tf->df", h2_full, pre_grad, preferred_element_type=jnp.float32)
    up_bias_grad = jnp.sum(pre_grad, axis=0, dtype=jnp.float32)
    piece = pre_grad
    h2_grad = lax.psum_scatter(
        jnp.einsum("tf,df->td", piece, up_weight, preferred_element_type=jnp.float32),
        "tensor",
        scatter_dimension=0,
        tiled=True,
    )
    y1_part, gain2_grad, shift2_grad = norm2_back(h2_grad)
    y1_grad = cotangent.astype(jnp.float32) + y1_part
    branch_grad = y1_grad.astype(jnp.bfloat16)
    branch_full = lax.all_gather(branch_grad, "tensor", axis=0, tiled=True)
    out_grad = jnp.einsum("tc,td->cd", attended, branch_full, preferred_element_type=jnp.float32)
    out_bias_grad = jnp.sum(branch_grad, axis=0, dtype=jnp.float32)
    attended_grad = jnp.einsum(
        "td,cd->tc", branch_full, out_weight, preferred_element_type=jnp.float32
    )
    attended_grad = attended_grad.astype(jnp.bfloat16).reshape(total, head_count, HEAD_DIM)

    def attend_back(carry, index):
        key_acc, value_acc = carry
        start = index * block
        query_block = lax.dynamic_slice_in_dim(query_rows, start, block, 0)
        grad_block = lax.dynamic_slice_in_dim(attended_grad, start, block, 0)
        scores = block_scores(query_block, key_rows, cells, start, block, scale)
        probs = jnp.exp(scores - log_totals[index][..., None])
        prob_grad = jnp.einsum(
            "qhe,khe->hqk", grad_block, value_rows, preferred_element_type=jnp.float32
        )
        center = jnp.sum(probs * prob_grad, axis=-1, keepdims=True)
        score_grad = (probs * (prob_grad - center)).astype(jnp.bfloat16)
        query_grad = (
            jnp.einsum("hqk,khe->qhe", score_grad, key_rows, preferred_element_type=jnp.float32)
            * scale
        )
        key_acc = (
            key_acc
            + jnp.einsum(
                "hqk,qhe->khe", score_grad, query_block, preferred_element_type=jnp.float32
            )
            * scale
        )
        value_acc = value_acc + jnp.einsum(
            "hqk,qhe->khe",
            probs.astype(jnp.bfloat16),
            grad_block,
            preferred_element_type=jnp.float32,
        )
        return ((key_acc, value_acc), query_grad.astype(jnp.bfloat16))

    empty = jnp.zeros((total, head_count, HEAD_DIM), jnp.float32)
    (key_acc, value_acc), query_grads = lax.scan(attend_back, (empty, empty), block_index)
    stacked_grad = jnp.stack(
        [
            query_grads.reshape(total, local_width),
            key_acc.reshape(total, local_width).astype(jnp.bfloat16),
            value_acc.reshape(total, local_width).astype(jnp.bfloat16),
        ],
        axis=1,
    )
    attn_grad = jnp.einsum("td,tke->dke", h1_full, stacked_grad, preferred_element_type=jnp.float32)
    qv_grad = jnp.stack(
        [
            jnp.sum(stacked_grad[:, 0], axis=0, dtype=jnp.float32),
            jnp.sum(stacked_grad[:, 2], axis=0, dtype=jnp.float32),
        ]
    )
    piece = stacked_grad
    h1_grad = lax.psum_scatter(
        jnp.einsum("tke,dke->td", piece, attn_weight, preferred_element_type=jnp.float32).astype(
            jnp.bfloat16
        ),
        "tensor",
        scatter_dimension=0,
        tiled=True,
    ).astype(jnp.float32)
    x_part, gain1_grad, shift1_grad = norm1_back(h1_grad)
    input_grad = (y1_grad + x_part).astype(jnp.bfloat16)
    small_grads = jnp.stack(
        [gain1_grad, shift1_grad, gain2_grad, shift2_grad, out_bias_grad, down_bias_grad]
    )
    small_grads = lax.psum(small_grads, "tensor")
    attn_grad, qv_grad, out_grad, small_grads, up_grad, up_bias_grad, down_grad = lax.psum(
        (attn_grad, qv_grad, out_grad, small_grads, up_grad, up_bias_grad, down_grad), "dp"
    )
    return (
        layer_out,
        input_grad,
        small_grads[0],
        small_grads[1],
        attn_grad,
        qv_grad,
        out_grad,
        small_grads[4],
        small_grads[2],
        small_grads[3],
        up_grad,
        up_bias_grad,
        down_grad,
        small_grads[5],
    )


def solution(mesh):
    in_specs = (
        P(("dp", "tensor"), None),
        P(("dp", "tensor"), None),
        P(),
        P(),
        P(None, None, "tensor"),
        P(None, "tensor"),
        P("tensor", None),
        P(),
        P(),
        P(),
        P(None, "tensor"),
        P("tensor"),
        P("tensor", None),
        P(),
        P("dp", None),
        P("dp", None),
    )
    out_specs = (
        P(("dp", "tensor"), None),
        P(("dp", "tensor"), None),
        P(),
        P(),
        P(None, None, "tensor"),
        P(None, "tensor"),
        P("tensor", None),
        P(),
        P(),
        P(),
        P(None, "tensor"),
        P("tensor"),
        P("tensor", None),
        P(),
    )
    return jax.shard_map(body, mesh=mesh, in_specs=in_specs, out_specs=out_specs, check_vma=False)
```

profile of v0, /device:TPU:0, one launch (start us, length us, event | category | flops | bytes accessed | tf_op | source)
XLA Modules:
  0.0 1435.6 jit_solution(2193233268125977223)
XLA Ops:
  13.6 39.2 %all-gather.5.cloned.1.call-done = bf16[2048,1120]{0,1:T(8,128)(2,1)} async-done(((bf16[512,1120]{0,1:T(8,128)(2,1)}), bf16[2048,1120]{0,1:T(8,128)(2,1)}) %all-gather.5.cloned.1.call-update) | async-done | bytes 4587536 | tf_op jit(solution)/shard_map/all_gather | solution.py:82
  52.8 7.2 fusion.51
  64.5 130.2 %while.27 = (s32[]{:T(128)}, bf16[4,512,5,56]{1,3,2,0:T(8,128)(2,1)}, f32[4,5,512]{2,1,0:T(8,128)S(1)}, s32[4]{0:T(128)S(1)}, s32[2048]{0:T(1024)S(1)}, /*index=...) while((s32[]{:T(128)}, ...), condition=%wide.region_6.7_spmd, body=%wide.region_3.6_spmd.sunk | while | flops 1243752960 | bytes 158569728 | solution.py:103
  73.6 7.0 copy-done.2
  86.4 10.6 fusion.134
  106.1 7.0 copy-done.2
  118.9 10.6 fusion.134
  138.6 7.0 copy-done.2
  151.4 10.6 fusion.134
  183.9 10.6 fusion.134
  205.0 76.1 %reduce-scatter.5.cloned.1.call-done = f32[512,1120]{0,1:T(8,128)} async-done(((f32[2048,1120]{0,1:T(8,128)}), f32[512,1120]{0,1:T(8,128)}) %reduce-scatter.5.cloned.1.call-update) | async-done | bytes 2293776 | tf_op jit(solution)/shard_map/reduce_scatter | solution.py:108
  286.3 33.1 %all-gather.9.cloned.1.call-done = bf16[2048,1120]{0,1:T(8,128)(2,1)} async-done(((bf16[512,1120]{0,1:T(8,128)(2,1)}), bf16[2048,1120]{0,1:T(8,128)(2,1)}) %all-gather.9.cloned.1.call-update) | async-done | bytes 4587536 | tf_op jit(solution)/shard_map/all_gather | solution.py:132
  319.4 10.9 fusion.82
  330.3 27.8 %all-gather.7.cloned.1.call-done = bf16[2048,1120]{0,1:T(8,128)(2,1)} async-done(((bf16[512,1120]{0,1:T(8,128)(2,1)}), bf16[2048,1120]{0,1:T(8,128)(2,1)}) %all-gather.7.cloned.1.call-update) | async-done | bytes 4587536 | tf_op jit(solution)/shard_map/all_gather | solution.py:117
  358.1 18.2 %convert_reduce_fusion = (f32[1120]{0:T(1024)}, bf16[2048,1120]{0,1:T(8,128)(2,1)S(1)}, f32[2048,1120]{0,1:T(8,128)}) fusion(f32[2048,1120]{0,1:T(8,128)} %fusion.82, f32[1120]{0:T(1024)S(1)} %copy-done.54, bf16[2048,1120]{0,1:T(8,128)(2,1)} %all-gather.7.cloned.1.call-done, bf16[1120,1120]{1,0:T(8,128)(2,1)S(1)} %copy-done), kind=kOutput, calls=%fused_computation.65 | convolution fusion | flops 5190777856 | bytes 30042880 | tf_op jit(solution)/shard_map/dot_general | solution.py:118
  378.5 8.5 fusion.83
  388.8 10.9 convolution_convert_fusion
  399.8 64.2 %reduce-scatter.9.cloned.1.call-done = f32[512,1120]{0,1:T(8,128)} async-done(((f32[2048,1120]{0,1:T(8,128)}), f32[512,1120]{0,1:T(8,128)}) %reduce-scatter.9.cloned.1.call-update) | async-done | bytes 2293776 | tf_op jit(solution)/shard_map/reduce_scatter | solution.py:140
  467.1 46.9 %reduce-scatter.7.cloned.1.call-done = bf16[512,1120]{0,1:T(8,128)(2,1)} async-done(((bf16[2048,1120]{0,1:T(8,128)(2,1)}), bf16[512,1120]{0,1:T(8,128)(2,1)}) %reduce-scatter.7.cloned.1.call-update) | async-done | bytes 1146896 | tf_op jit(solution)/shard_map/reduce_scatter | solution.py:124
  519.8 36.8 %all-gather.11.cloned.1.call-done = bf16[2048,1120]{0,1:T(8,128)(2,1)} async-done(((bf16[512,1120]{0,1:T(8,128)(2,1)}), bf16[2048,1120]{0,1:T(8,128)(2,1)}) %all-gather.11.cloned.1.call-update) | async-done | bytes 4587536 | tf_op jit(solution)/shard_map/all_gather | solution.py:149
  562.7 305.5 %while.28 = (s32[]{:T(128)}, f32[2048,5,56]{0,2,1:T(8,128)}, f32[2048,5,56]{0,2,1:T(8,128)}, bf16[4,512,5,56]{1,3,2,0:T(8,128)(2,1)}, s32[4]{0:T(128)S(1)}, /*in...) while((s32[]{:T(128)}, f32[2048,5,56]{0,2,1:T(8,128)}, ...), condition=%wide.region_16.17_spmd.clone, body=%wide.region_14.16_spmd.clone.sunk | while | flops 3024099840 | bytes 221509072 | solution.py:189
  568.2 9.8 fusion.144
  578.0 10.3 fusion.147
  588.3 15.9 %multiply_reduce_fusion.5 = (f32[5,512]{1,0:T(8,128)S(1)}, f32[5,512,2048]{2,1,0:T(8,128)}) fusion(f32[5,512,2048]{2,1,0:T(8,128)} %fusion.144, f32[5,512]{1,0:T(8,128)S(1)} %dynamic-slice_bitcast_fusion.2, pred[512,2048]{1,0:T(8,128)(4,1)S(1)} %fusion.145, bf16[2048,5,56]{0,2,1:T(8,128)(2,1)S(1)} %copy-done.11, ...), kind=kOutput, calls=%fused_computation.22.clone.1 | convolution fusion | flops 613414400 | bytes 44451844 | tf_op jit(solution)/shard_map/while/body/eval_jaxpr/qhe,khe->hqk/dot_general | solution.py:164
  604.2 19.1 %multiply_convert_fusion.5 = bf16[5,512,2048]{2,1,0:T(8,128)(2,1)} fusion(f32[5,512,2048]{2,1,0:T(8,128)} %get-tuple-element.373, f32[5,512,2048]{2,1,0:T(8,128)} %fusion.144, f32[5,512]{1,0:T(8,128)S(1)} %get-tuple-element.374, f32[5,512]{1,0:T(8,128)S(1)} %dynamic-slice_bitcast_fusion.2, pred[512,2048]{1,0:T(8,128)(4,1)S(1)} %fusion.145), kind=kLoop, calls=%fused_computation.21.clone.1 | loop fusion | flops 31457280 | bytes 53497856 | tf_op jit(solution)/shard_map/while/body/eval_jaxpr/convert_element_type | solution.py:168
  623.3 8.2 fusion.148
  644.5 9.8 fusion.144
  654.3 10.3 fusion.147
  664.6 15.9 %multiply_reduce_fusion.5 = (f32[5,512]{1,0:T(8,128)S(1)}, f32[5,512,2048]{2,1,0:T(8,128)}) fusion(f32[5,512,2048]{2,1,0:T(8,128)} %fusion.144, f32[5,512]{1,0:T(8,128)S(1)} %dynamic-slice_bitcast_fusion.2, pred[512,2048]{1,0:T(8,128)(4,1)S(1)} %fusion.145, bf16[2048,5,56]{0,2,1:T(8,128)(2,1)S(1)} %copy-done.11, ...), kind=kOutput, calls=%fused_computation.22.clone.1 | convolution fusion | flops 613414400 | bytes 44451844 | tf_op jit(solution)/shard_map/while/body/eval_jaxpr/qhe,khe->hqk/dot_general | solution.py:164
  680.5 19.1 %multiply_convert_fusion.5 = bf16[5,512,2048]{2,1,0:T(8,128)(2,1)} fusion(f32[5,512,2048]{2,1,0:T(8,128)} %get-tuple-element.373, f32[5,512,2048]{2,1,0:T(8,128)} %fusion.144, f32[5,512]{1,0:T(8,128)S(1)} %get-tuple-element.374, f32[5,512]{1,0:T(8,128)S(1)} %dynamic-slice_bitcast_fusion.2, pred[512,2048]{1,0:T(8,128)(4,1)S(1)} %fusion.145), kind=kLoop, calls=%fused_computation.21.clone.1 | loop fusion | flops 31457280 | bytes 53497856 | tf_op jit(solution)/shard_map/while/body/eval_jaxpr/convert_element_type | solution.py:168
  699.6 8.2 fusion.148
  720.8 9.8 fusion.144
  730.6 10.3 fusion.147
  740.9 15.9 %multiply_reduce_fusion.5 = (f32[5,512]{1,0:T(8,128)S(1)}, f32[5,512,2048]{2,1,0:T(8,128)}) fusion(f32[5,512,2048]{2,1,0:T(8,128)} %fusion.144, f32[5,512]{1,0:T(8,128)S(1)} %dynamic-slice_bitcast_fusion.2, pred[512,2048]{1,0:T(8,128)(4,1)S(1)} %fusion.145, bf16[2048,5,56]{0,2,1:T(8,128)(2,1)S(1)} %copy-done.11, ...), kind=kOutput, calls=%fused_computation.22.clone.1 | convolution fusion | flops 613414400 | bytes 44451844 | tf_op jit(solution)/shard_map/while/body/eval_jaxpr/qhe,khe->hqk/dot_general | solution.py:164
  756.8 19.1 %multiply_convert_fusion.5 = bf16[5,512,2048]{2,1,0:T(8,128)(2,1)} fusion(f32[5,512,2048]{2,1,0:T(8,128)} %get-tuple-element.373, f32[5,512,2048]{2,1,0:T(8,128)} %fusion.144, f32[5,512]{1,0:T(8,128)S(1)} %get-tuple-element.374, f32[5,512]{1,0:T(8,128)S(1)} %dynamic-slice_bitcast_fusion.2, pred[512,2048]{1,0:T(8,128)(4,1)S(1)} %fusion.145), kind=kLoop, calls=%fused_computation.21.clone.1 | loop fusion | flops 31457280 | bytes 53497856 | tf_op jit(solution)/shard_map/while/body/eval_jaxpr/convert_element_type | solution.py:168
  775.9 8.2 fusion.148
  797.1 9.8 fusion.144
  806.9 10.3 fusion.147
  817.2 15.9 %multiply_reduce_fusion.5 = (f32[5,512]{1,0:T(8,128)S(1)}, f32[5,512,2048]{2,1,0:T(8,128)}) fusion(f32[5,512,2048]{2,1,0:T(8,128)} %fusion.144, f32[5,512]{1,0:T(8,128)S(1)} %dynamic-slice_bitcast_fusion.2, pred[512,2048]{1,0:T(8,128)(4,1)S(1)} %fusion.145, bf16[2048,5,56]{0,2,1:T(8,128)(2,1)S(1)} %copy-done.11, ...), kind=kOutput, calls=%fused_computation.22.clone.1 | convolution fusion | flops 613414400 | bytes 44451844 | tf_op jit(solution)/shard_map/while/body/eval_jaxpr/qhe,khe->hqk/dot_general | solution.py:164
  833.1 19.1 %multiply_convert_fusion.5 = bf16[5,512,2048]{2,1,0:T(8,128)(2,1)} fusion(f32[5,512,2048]{2,1,0:T(8,128)} %get-tuple-element.373, f32[5,512,2048]{2,1,0:T(8,128)} %fusion.144, f32[5,512]{1,0:T(8,128)S(1)} %get-tuple-element.374, f32[5,512]{1,0:T(8,128)S(1)} %dynamic-slice_bitcast_fusion.2, pred[512,2048]{1,0:T(8,128)(4,1)S(1)} %fusion.145), kind=kLoop, calls=%fused_computation.21.clone.1 | loop fusion | flops 31457280 | bytes 53497856 | tf_op jit(solution)/shard_map/while/body/eval_jaxpr/convert_element_type | solution.py:168
  852.2 8.2 fusion.148
  876.6 8.2 bitcast_convert_fusion
  884.9 11.0 fusion.81
  895.9 13.6 fusion.72
  920.2 11.8 reduce-scatter.11.cloned.1.call-done
  939.2 10.9 psum.56
  950.2 41.0 %all-reduce = (f32[6,1120]{1,0:T(8,128)S(1)}, f32[2,280]{1,0:T(2,128)}, f32[1120]{0:T(1024)}) all-reduce(f32[6,1120]{1,0:T(8,128)S(1)} %psum.56, f32[2,280]{1,0:T(2,128)S(1)} %pad_maximum_fusion.3, f32[1120]{0:T(1024)S(1)} %copy-done.49), channel_id=1, replica_groups=mesh['dp'=8,'tensor'=4] {'dp'}, use_global_device_ids=true, to_apply=%region_27.28 | all-reduce | flops 8400 | bytes 67200 | tf_op jit(solution)/shard_map/psum | solution.py:220
  991.9 424.0 %all-reduce.4.cloned.1.call-done = (f32[1120,3,280]{0,2,1:T(8,128)}, f32[280,1120]{1,0:T(8,128)}, f32[1120,1120]{1,0:T(8,128)}, f32[1120,1120]{1,0:T(8,128)}) async-done(((f32[1120,3,280]{0,2,1:T(8,128)}, f32[280,1120]{1,0:T(8,128)}, f32[1120,1120]{1,0:T(8,128)}, f32[1120,1120]{1,0:T(8,128)}), (f32[1120,3,280]{0,2,1:T(8,128)}, f32[280,1120]{1,0:T(8,128)}, f32[1120,1120]{1,0:T(8,128)}, ...) | async-done | bytes 15052816 | tf_op jit(solution)/shard_map/psum | solution.py:220
  (307 shorter events, 190.1 us)
Async XLA Ops:
  7.2 351.0 %copy-start = (bf16[1120,1120]{1,0:T(8,128)(2,1)S(1)}, bf16[1120,1120]{1,0:T(8,128)(2,1)}, u32[]{:S(2)}) copy-start(bf16[1120,1120]{1,0:T(8,128)(2,1)} %param.30) | copy-start | bytes 7526404
  7.2 45.6 %all-gather.5.cloned.1.call-start = ((), (), s32[]{:S(2)}) async-start(), calls=%async_computation.4 | async-start | bytes 5734400 | tf_op jit(solution)/shard_map/all_gather | solution.py:82
  13.2 267.8 %reduce-scatter.5.cloned.1.call-start = ((), (), s32[]{:S(2)}) async-start(), calls=%async_computation.5 | async-start | bytes 11468800 | tf_op jit(solution)/shard_map/reduce_scatter | solution.py:108
  204.1 76.9 %copy-start.47 = (f32[1120]{0:T(1024)S(1)}, f32[1120]{0:T(1024)}, u32[]{:S(2)}) copy-start(f32[1120]{0:T(1024)} %param.27) | copy-start | bytes 13444
  204.2 115.2 %all-gather.9.cloned.1.call-start = ((), (), s32[]{:S(2)}) async-start(), calls=%async_computation.8 | async-start | bytes 5734400 | tf_op jit(solution)/shard_map/all_gather | solution.py:132
  204.9 153.2 %all-gather.7.cloned.1.call-start = ((), (), s32[]{:S(2)}) async-start(), calls=%async_computation.6 | async-start | bytes 5734400 | tf_op jit(solution)/shard_map/all_gather | solution.py:117
  286.2 71.9 %copy-start.54 = (f32[1120]{0:T(1024)S(1)}, f32[1120]{0:T(1024)}, u32[]{:S(2)}) copy-start(f32[1120]{0:T(1024)} %param.31) | copy-start | bytes 13444
  286.2 177.7 %reduce-scatter.9.cloned.1.call-start = ((), (), s32[]{:S(2)}) async-start(), calls=%async_computation.9 | async-start | bytes 11468800 | tf_op jit(solution)/shard_map/reduce_scatter | solution.py:140
  387.0 126.9 %reduce-scatter.7.cloned.1.call-start = ((), (), s32[]{:S(2)}) async-start(), calls=%async_computation.7 | async-start | bytes 5734400 | tf_op jit(solution)/shard_map/reduce_scatter | solution.py:124
  399.7 64.3 %copy-start.7 = (f32[512,1120]{0,1:T(8,128)S(1)}, f32[512,1120]{0,1:T(8,128)}, u32[]{:S(2)}) copy-start(f32[512,1120]{0,1:T(8,128)} %copy-done.6) | copy-start | bytes 6881284
  399.7 114.2 %copy-start.50 = (f32[1120]{0:T(1024)S(1)}, f32[1120]{0:T(1024)}, u32[]{:S(2)}) copy-start(f32[1120]{0:T(1024)} %param.33) | copy-start | bytes 13444
  399.7 156.9 %all-gather.11.cloned.1.call-start = ((), (), s32[]{:S(2)}) async-start(), calls=%async_computation.10 | async-start | bytes 5734400 | tf_op jit(solution)/shard_map/all_gather | solution.py:149
  519.8 412.3 %reduce-scatter.11.cloned.1.call-start = ((), (), s32[]{:S(2)}) async-start(), calls=%async_computation.11 | async-start | bytes 5734400 | tf_op jit(solution)/shard_map/reduce_scatter | solution.py:206
  519.8 42.9 %copy-start.3 = (bf16[2048,5,56]{0,2,1:T(8,128)(2,1)S(1)}, bf16[2048,5,56]{0,2,1:T(8,128)(2,1)}, u32[]{:S(2)}) copy-start(bf16[2048,5,56]{0,2,1:T(8,128)(2,1)} %get-tuple-element.489) | copy-start | bytes 3440644
  568.2 9.8 copy-start.21
  568.2 9.8 copy-start.23
  578.0 10.3 copy-start.11
  588.3 15.9 %copy-start.22 = (f32[2048,5,56]{0,2,1:T(8,128)}, f32[2048,5,56]{0,2,1:T(8,128)S(1)}, u32[]{:S(2)}) copy-start(f32[2048,5,56]{0,2,1:T(8,128)S(1)} %fusion.147) | copy-start | bytes 6881284 | tf_op jit(solution)/shard_map/while
  623.3 8.2 copy-start.4
  644.5 9.8 copy-start.21
  644.5 9.8 copy-start.23
  654.3 10.3 copy-start.11
  664.6 15.9 %copy-start.22 = (f32[2048,5,56]{0,2,1:T(8,128)}, f32[2048,5,56]{0,2,1:T(8,128)S(1)}, u32[]{:S(2)}) copy-start(f32[2048,5,56]{0,2,1:T(8,128)S(1)} %fusion.147) | copy-start | bytes 6881284 | tf_op jit(solution)/shard_map/while
  699.6 8.2 copy-start.4
  720.8 9.8 copy-start.21
  720.8 9.8 copy-start.23
  730.6 10.3 copy-start.11
  740.9 15.9 %copy-start.22 = (f32[2048,5,56]{0,2,1:T(8,128)}, f32[2048,5,56]{0,2,1:T(8,128)S(1)}, u32[]{:S(2)}) copy-start(f32[2048,5,56]{0,2,1:T(8,128)S(1)} %fusion.147) | copy-start | bytes 6881284 | tf_op jit(solution)/shard_map/while
  775.9 8.2 copy-start.4
  797.1 9.8 copy-start.21
  797.1 9.8 copy-start.23
  806.9 10.3 copy-start.11
  817.2 15.9 %copy-start.22 = (f32[2048,5,56]{0,2,1:T(8,128)}, f32[2048,5,56]{0,2,1:T(8,128)S(1)}, u32[]{:S(2)}) copy-start(f32[2048,5,56]{0,2,1:T(8,128)S(1)} %fusion.147) | copy-start | bytes 6881284 | tf_op jit(solution)/shard_map/while
  852.2 8.2 copy-start.4
  884.9 531.0 %all-reduce.4.cloned.1.call-start = ((), (), s32[]{:S(2)}) async-start(), calls=%async_computation.12 | async-start | bytes 30965760 | tf_op jit(solution)/shard_map/psum | solution.py:220
  884.9 24.7 %slice-start.4 = ((s8[4587520]{0:T(1024)(128)(4,1)}), s8[4194304]{0:T(1024)(128)(4,1)S(1)}, s32[]{:S(2)}) async-start(s8[4587520]{0:T(1024)(128)(4,1)} %bitcast.120), calls=%async_computation.17 | async-start | bytes 8388608
  884.9 27.5 %slice-start.2 = ((s8[4587520]{0:T(1024)(128)(4,1)}), s8[4194304]{0:T(1024)(128)(4,1)S(1)}, s32[]{:S(2)}) async-start(s8[4587520]{0:T(1024)(128)(4,1)} %bitcast.118), calls=%async_computation.15 | async-start | bytes 8388608
  895.9 13.7 copy-start.19
  895.9 13.7 slice-start.5
  895.9 16.5 %slice-start.3 = ((s8[4587520]{0:T(1024)(128)(4,1)}), s8[393216]{0:T(1024)(128)(4,1)S(1)}, s32[]{:S(2)}) async-start(s8[4587520]{0:T(1024)(128)(4,1)} %bitcast.118), calls=%async_computation.16 | async-start | bytes 786432
  919.0 13.0 copy-start.9
  919.1 13.0 copy-start.33
  919.1 13.0 copy-start.35
  919.1 15.2 %copy-start.45 = (f32[512]{0:T(512)S(1)}, f32[512]{0:T(512)}, u32[]{:S(2)}) copy-start(f32[512]{0:T(512)} %copy-done.44) | copy-start | bytes 6148
  919.1 15.2 %copy-start.38 = (f32[512]{0:T(512)S(1)}, f32[512]{0:T(512)}, u32[]{:S(2)}) copy-start(f32[512]{0:T(512)} %copy-done.37) | copy-start | bytes 6148
  920.2 16.7 %copy-start.15 = (bf16[512,1120]{0,1:T(8,128)(2,1)S(1)}, bf16[512,1120]{0,1:T(8,128)(2,1)}, u32[]{:S(2)}) copy-start(bf16[512,1120]{0,1:T(8,128)(2,1)} %param.21) | copy-start | bytes 3440644
  920.2 16.7 %copy-start.43 = (f32[512]{0:T(512)S(1)}, f32[512]{0:T(512)}, u32[]{:S(2)}) copy-start(f32[512]{0:T(512)} %copy-done.42) | copy-start | bytes 6148
  936.9 13.2 copy-start.49
  (48 other events, 159.8 us)
Sparse Core Ops, SparseCore 0:
  13.4 39.3 all-gather.4
  204.3 76.7 reduce-scatter.4
  282.6 36.7 all-gather.8
  321.4 36.7 all-gather.6
  387.2 76.7 reduce-scatter.8
  466.9 46.9 reduce-scatter.6
  519.9 36.7 all-gather.10
  885.0 46.9 reduce-scatter.10
  938.0 477.8 all-reduce.3
where the time goes:
time: 1440 us
  waiting for transfers between devices  761 us (53%)
  matrix products  375 us (26%)
  other arithmetic  149 us (10%)
  local copies, waits for them, and re-layouts  69.5 us (5%)
  blocking collectives  51.9 us (4%)
  between operations  14.9 us (1%)
    psum x1, waiting for transfers between devices, body(): lax.psum((attn_grad, qv_grad, out_grad, small_grads, up_grad, up_bias_gra...  424 us
    convert_element_type x4, other arithmetic, attend_back(): score_grad = (probs * (prob_grad - center)).astype(jnp.bfloat16)  76.5 us
    reduce_scatter x1, waiting for transfers between devices, body(): lax.psum_scatter(jnp.dot(piece, out_weight, preferred_element_type=jnp.fl...  76.1 us
    reduce_scatter x1, waiting for transfers between devices, body(): lax.psum_scatter(jnp.einsum('tf,df->td', piece, up_weight, preferred_elem...  64.2 us
    dot_general x4, matrix products, attend_back(): jnp.einsum('qhe,khe->hqk', grad_block, value_rows, preferred_element_type...  63.7 us
    dot_general x8, matrix products, block_scores(): jnp.einsum('qhe,khe->hqk', query_block, key_rows, preferred_element_type=...  61.4 us
    reduce_scatter x1, waiting for transfers between devices, body(): lax.psum_scatter(jnp.dot(piece, down_weight, preferred_element_type=jnp.f...  46.9 us
    dot_general x4, matrix products, attend(): jnp.einsum('hqk,khe->qhe', probs, value_rows, preferred_element_type=jnp....  42.4 us
  transfers between devices with their start and end apart: 9, of which 9 were waited for; matrix products, arithmetic and copies ran while one was open for 5% of the time, Pallas kernels for 0%

commit v1 on v0

v1 whole, which is shorter than its diff:
```python
import functools
import math

import jax
import jax.numpy as jnp
from jax import lax
from jax.experimental import pallas as pl
from jax.experimental.pallas import tpu as pltpu
from jax.sharding import PartitionSpec as P


HEAD_DIM = 56
BLK = 256
SLOTS = 4
NEG = -1e30
EPS = 1e-05
SCALE = 1.0 / math.sqrt(HEAD_DIM)
SCALE2 = SCALE * math.log2(math.e)
GELU_C = math.sqrt(2.0 / math.pi)
GELU_A = 0.044715
F32 = jnp.float32
BF16 = jnp.bfloat16
NT = ((1,), (1,))
VMEM = 48 << 20


def dot(a, b, dims=((1,), (0,))):
    return lax.dot_general(a, b, (dims, ((), ())), preferred_element_type=F32)


def params():
    return pltpu.CompilerParams(vmem_limit_bytes=VMEM)


def cost(flops, nbytes, trans=0):
    return pl.CostEstimate(flops=int(flops), bytes_accessed=int(nbytes), transcendentals=int(trans))


def fold(v):
    total = v[:, :128]
    for at in range(128, v.shape[1], 128):
        total = total + v[:, at : at + 128]
    return total


def normal(x):
    center = x - jnp.mean(x, axis=0, keepdims=True)
    root = lax.rsqrt(jnp.mean(center * center, axis=0, keepdims=True) + EPS)
    return center * root, root


def qkv_kernel(heads, a_ref, b_ref, w_ref, vec_ref, bias_ref, *rest):
    x_out, h_out, q_out, kn_out, vn_out = rest[-5:]
    x = jnp.concatenate([a_ref[...], b_ref[...]], axis=1)
    x_out[...] = x
    n, _ = normal(x.astype(F32))
    h = (n * vec_ref[:, 0:1] + vec_ref[:, 1:2]).astype(BF16)
    h_out[...] = h
    width = heads * HEAD_DIM
    for part in range(3):
        r = dot(w_ref[part], h)
        if part != 1:
            r = r + bias_ref[part]
        r = r.astype(BF16)
        r = r.reshape(heads, HEAD_DIM, r.shape[1])
        q_out[part * heads : (part + 1) * heads] = r
        if part > 0:
            out = kn_out if part == 1 else vn_out
            for h_at in range(heads):
                out[h_at] = r[h_at].T


def qkv_call(pair, a, b, w, vec, bias, carry):
    d, rows = a.shape
    per = rows // BLK
    total = rows * SLOTS
    heads = w.shape[1] // HEAD_DIM
    wide = 2 * BLK
    outs = [
        jax.ShapeDtypeStruct((d, total), BF16),
        jax.ShapeDtypeStruct((d, total), BF16),
        jax.ShapeDtypeStruct((3 * heads, HEAD_DIM, total), BF16),
        jax.ShapeDtypeStruct((heads, total, HEAD_DIM), BF16),
        jax.ShapeDtypeStruct((heads, total, HEAD_DIM), BF16),
    ]
    at = lambda p: p * (SLOTS // 2) + pair
    in_specs = [
        pl.BlockSpec((d, BLK), lambda p: (0, p)),
        pl.BlockSpec((d, BLK), lambda p: (0, p)),
        pl.BlockSpec(w.shape, lambda p: (0, 0, 0)),
        pl.BlockSpec(vec.shape, lambda p: (0, 0)),
        pl.BlockSpec(bias.shape, lambda p: (0, 0, 0)),
    ]
    args = [a, b, w, vec, bias]
    alias = {}
    if carry is not None:
        alias = {len(args) + n: n for n in range(len(outs))}
        in_specs += [pl.BlockSpec(memory_space=pl.ANY)] * len(outs)
        args += list(carry)
    return pl.pallas_call(
        functools.partial(qkv_kernel, heads),
        grid=(per,),
        in_specs=in_specs,
        out_specs=[
            pl.BlockSpec((d, wide), lambda p: (0, at(p))),
            pl.BlockSpec((d, wide), lambda p: (0, at(p))),
            pl.BlockSpec((3 * heads, HEAD_DIM, wide), lambda p: (0, 0, at(p))),
            pl.BlockSpec((heads, wide, HEAD_DIM), lambda p: (0, at(p), 0)),
            pl.BlockSpec((heads, wide, HEAD_DIM), lambda p: (0, at(p), 0)),
        ],
        out_shape=outs,
        input_output_aliases=alias,
        compiler_params=params(),
        cost_estimate=cost(2 * w.size * rows * 2, 2 * (w.size + 8 * d * rows)),
        name="qkv_call",
    )(*args)


def attend_kernel(heads, nb, per, chunk, info, start_ref, q_ref, kn_ref, v_ref, o_ref, lse_ref, acc, m_s, l_s):
    b = pl.program_id(0) * per + chunk

    def visit(kb, diag):
        at = pl.multiple_of(info[nb + kb] * BLK, BLK)
        kpos = lax.broadcasted_iota(jnp.int32, (BLK, BLK), 0)
        ok = kpos >= (start_ref[...] - kb * BLK)
        if diag:
            ok = ok & (kpos <= lax.broadcasted_iota(jnp.int32, (BLK, BLK), 1))
        scores = [dot(kn_ref[h, pl.ds(at, BLK), :], q_ref[h]) for h in range(heads)]
        scores = [jnp.where(ok, s, NEG) for s in scores]
        top = jnp.concatenate([jnp.max(s, axis=0, keepdims=True) for s in scores], 0)
        if not diag:
            old = m_s[0:heads, :]
            top = jnp.maximum(old, top)
            fade = jnp.exp2((old - top) * SCALE2)
        m_s[0:heads, :] = top
        expo = [jnp.exp2((scores[h] - top[h : h + 1]) * SCALE2) for h in range(heads)]
        sums = jnp.concatenate([jnp.sum(e, axis=0, keepdims=True) for e in expo], 0)
        l_s[0:heads, :] = sums if diag else l_s[0:heads, :] * fade + sums
        for h in range(heads):
            new = dot(v_ref[h, :, pl.ds(at, BLK)], expo[h].astype(BF16))
            acc[h] = new if diag else acc[h] * fade[h : h + 1] + new

    visit(b, True)

    def step(kb, _):
        visit(kb, False)
        return 0

    lax.fori_loop(info[b], b, step, 0)
    for h in range(heads):
        total = l_s[h : h + 1, :]
        o_ref[h] = (acc[h] * (1.0 / total)).astype(BF16)
        lse_ref[h : h + 1, :] = m_s[h : h + 1, :] * SCALE2 + jnp.log2(total)


def attend(chunk, info, start, qkv, kn):
    heads, total = qkv.shape[0] // 3, qkv.shape[2]
    nb = total // BLK
    per = nb // SLOTS
    spec = pltpu.PrefetchScalarGridSpec(
        num_scalar_prefetch=1,
        grid=(SLOTS,),
        in_specs=[
            pl.BlockSpec((1, BLK), lambda i, s: (0, i * per + chunk)),
            pl.BlockSpec((heads, HEAD_DIM, BLK), lambda i, s: (0, 0, s[nb + i * per + chunk])),
            pl.BlockSpec((heads, total, HEAD_DIM), lambda i, s: (0, 0, 0)),
            pl.BlockSpec((heads, HEAD_DIM, total), lambda i, s: (2, 0, 0)),
        ],
        out_specs=[
            pl.BlockSpec((heads, HEAD_DIM, BLK), lambda i, s: (0, 0, i)),
            pl.BlockSpec((8, BLK), lambda i, s: (0, i)),
        ],
        scratch_shapes=[
            pltpu.VMEM((heads, HEAD_DIM, BLK), F32),
            pltpu.VMEM((8, BLK), F32),
            pltpu.VMEM((8, BLK), F32),
        ],
    )
    return pl.pallas_call(
        functools.partial(attend_kernel, heads, nb, per, chunk),
        grid_spec=spec,
        out_shape=[
            jax.ShapeDtypeStruct((heads, HEAD_DIM, SLOTS * BLK), BF16),
            jax.ShapeDtypeStruct((8, SLOTS * BLK), F32),
        ],
        compiler_params=params(),
        cost_estimate=cost(6e9, 6e6, 4e6),
        name="attend",
    )(info, start, qkv, kn, qkv)


def attend_back_kernel(heads, nb, per, info, start_ref, q_ref, k_ref, kn_ref, vn_ref, o_ref, do_ref, lse_ref, out_ref, dq_s, dk_s, dv_s, dl):
    j = pl.program_id(0)

    def place(b):
        return pl.multiple_of(info[nb + b] * BLK, BLK)

    def ordered(b):
        return pl.multiple_of(((b % per) * SLOTS + b // per) * BLK, BLK)

    @pl.when(j == 0)
    def _():
        dq_s[...] = jnp.zeros_like(dq_s)
        for b in range(nb):
            cut = slice(b * BLK, (b + 1) * BLK)
            for h in range(heads):
                dl[h : h + 1, cut] = jnp.sum(
                    o_ref[h, :, cut].astype(F32) * do_ref[h, :, cut].astype(F32), axis=0, keepdims=True
                )

    def visit(b, diag):
        at = place(b)
        mine = ordered(b)
        kpos = lax.broadcasted_iota(jnp.int32, (BLK, BLK), 0)
        ok = kpos >= (start_ref[:, pl.ds(pl.multiple_of(b * BLK, BLK), BLK)] - j * BLK)
        if diag:
            ok = ok & (kpos <= lax.broadcasted_iota(jnp.int32, (BLK, BLK), 1))
        every = range(heads)
        query = [q_ref[h, :, pl.ds(at, BLK)] for h in every]
        grad = [do_ref[h, :, pl.ds(mine, BLK)] for h in every]
        scores = [dot(kn_ref[h], query[h]) for h in every]
        prob_grad = [dot(vn_ref[h], grad[h]) for h in every]
        probs = [
            jnp.where(ok, jnp.exp2(scores[h] * SCALE2 - lse_ref[h : h + 1, pl.ds(mine, BLK)]), 0.0) for h in every
        ]
        score_grad = [
            (probs[h] * (prob_grad[h] - dl[h : h + 1, pl.ds(mine, BLK)])).astype(BF16) for h in every
        ]
        dv = [dot(grad[h], probs[h].astype(BF16), NT) for h in every]
        dk = [dot(query[h], score_grad[h], NT) for h in every]
        dq = [dot(k_ref[h], score_grad[h]) for h in every]
        for h in every:
            if diag:
                dv_s[h] = dv[h]
                dk_s[h] = dk[h]
            else:
                dv_s[h] += dv[h]
                dk_s[h] += dk[h]
            dq_s[h, :, pl.ds(at, BLK)] += dq[h]

    visit(j, True)

    def step(b, _):
        visit(b, False)
        return 0

    lax.fori_loop(j + 1, info[2 * nb + j] + 1, step, 0)
    at = place(j)
    for h in range(heads):
        out_ref[h] = (dq_s[h, :, pl.ds(at, BLK)] * SCALE).astype(BF16)
        out_ref[heads + h] = (dk_s[h] * SCALE).astype(BF16)
        out_ref[2 * heads + h] = dv_s[h].astype(BF16)


def attend_back(info, start, qkv, kn, vn, o, do, lse):
    heads, total = qkv.shape[0] // 3, qkv.shape[2]
    nb = total // BLK
    per = nb // SLOTS
    whole = pl.BlockSpec((heads, HEAD_DIM, total), lambda j, s: (0, 0, 0))
    block = lambda a: pl.BlockSpec((heads, HEAD_DIM, BLK), lambda j, s: (a, 0, s[nb + j]))
    tall = pl.BlockSpec((heads, BLK, HEAD_DIM), lambda j, s: (0, s[nb + j], 0))
    spec = pltpu.PrefetchScalarGridSpec(
        num_scalar_prefetch=1,
        grid=(nb,),
        in_specs=[
            pl.BlockSpec((1, total), lambda j, s: (0, 0)),
            whole,
            block(1),
            tall,
            tall,
            whole,
            whole,
            pl.BlockSpec((8, total), lambda j, s: (0, 0)),
        ],
        out_specs=pl.BlockSpec((3 * heads, HEAD_DIM, BLK), lambda j, s: (0, 0, s[nb + j])),
        scratch_shapes=[
            pltpu.VMEM((heads, HEAD_DIM, total), F32),
            pltpu.VMEM((heads, HEAD_DIM, BLK), F32),
            pltpu.VMEM((heads, HEAD_DIM, BLK), F32),
            pltpu.VMEM((8, total), F32),
        ],
    )
    return pl.pallas_call(
        functools.partial(attend_back_kernel, heads, nb, per),
        grid_spec=spec,
        out_shape=jax.ShapeDtypeStruct((3 * heads, HEAD_DIM, total), BF16),
        compiler_params=params(),
        cost_estimate=cost(16e9, 12e6, 8e6),
        name="attend_back",
    )(info, start, qkv, qkv, kn, vn, o, do, lse)


def middle_kernel(info, att_ref, x_ref, g_ref, wot, wo, upt, up, wd, wdt, vec_ref, *outs):
    h_out, act_out, pg_out, layer_out, y1g_out, own_out, sum_out = outs[:7]
    attg_outs = outs[7:]
    s = pl.program_id(0)
    out_bias, gain, shift, up_bias = (vec_ref[:, n : n + 1] for n in range(4))
    g = g_ref[...]
    y1 = x_ref[...].astype(F32) + (dot(wot[...], att_ref[...]) + out_bias)

    @pl.when(s == 0)
    def _():
        own_out[...] = y1

    n, root = normal(y1)
    h = (n * gain + shift).astype(BF16)
    h_out[...] = h
    pre = dot(upt[...], h) + up_bias
    square = pre * pre
    t = jnp.tanh(pre * (GELU_C + (GELU_C * GELU_A) * square))
    half = 0.5 * (1.0 + t)
    act = (pre * half).astype(BF16)
    act_out[...] = act
    slope = half + (0.5 * pre) * (1.0 - t * t) * (GELU_C + (3.0 * GELU_C * GELU_A) * square)
    pg = dot(wd[...], g) * slope
    pgb = pg.astype(BF16)
    pg_out[...] = pgb
    layer_out[0] = dot(wdt[...], act).astype(BF16)
    hg = dot(up[...], pgb)
    e = hg * gain
    y1g = root * (e - jnp.mean(e, axis=0, keepdims=True) - n * jnp.mean(e * n, axis=0, keepdims=True))
    y1g = y1g + jnp.where(s == 0, g.astype(F32), 0.0)
    y1b = y1g.astype(BF16)
    y1g_out[0] = y1b
    attg = dot(wo[...], y1b)
    rows = attg_outs[0].shape[0]
    for k in range(SLOTS):
        attg_outs[k][...] = attg[k * rows : (k + 1) * rows].astype(BF16)
    parts = (fold(hg * n), fold(hg), fold(y1g), fold(pgb.astype(F32)))
    for at, part in enumerate(parts):
        sum_out[at] = jnp.where(s == 0, part, sum_out[at] + part)


def middle(chunk, info, att, x, g, wot, wo, upt, up, wd, wdt, vec):
    d = x.shape[0]
    f = upt.shape[0]
    rows = att.shape[0] // SLOTS
    wide = SLOTS * BLK
    nb = x.shape[1] // BLK
    dev = 3 * nb
    keep = lambda a: pl.BlockSpec(a.shape, lambda s, i: (0,) * a.ndim, pipeline_mode=pl.Buffered(1))
    place = lambda r: pl.BlockSpec((r, BLK), lambda s, i: (0, s ^ i[dev]))
    block = lambda r: pl.BlockSpec((r, BLK), lambda s, i: (0, s))
    full = lambda r: pl.BlockSpec((r, BLK), lambda s, i: (0, chunk * SLOTS + s))
    slot = lambda r: pl.BlockSpec((1, r, BLK), lambda s, i: (s, 0, 0))
    spec = pltpu.PrefetchScalarGridSpec(
        num_scalar_prefetch=1,
        grid=(SLOTS,),
        in_specs=[place(att.shape[0]), full(d), full(d)] + [keep(a) for a in (wot, wo, upt, up, wd, wdt, vec)],
        out_specs=[
            block(d),
            block(f),
            block(f),
            slot(d),
            slot(d),
            pl.BlockSpec((d, BLK), lambda s, i: (0, 0)),
            pl.BlockSpec((4, d, 128), lambda s, i: (0, 0, 0)),
        ]
        + [place(rows)] * SLOTS,
    )
    shape = jax.ShapeDtypeStruct
    return pl.pallas_call(
        middle_kernel,
        grid_spec=spec,
        out_shape=[
            shape((d, wide), BF16),
            shape((f, wide), BF16),
            shape((f, wide), BF16),
            shape((SLOTS, d, BLK), BF16),
            shape((SLOTS, d, BLK), BF16),
            shape((d, BLK), F32),
            shape((4, d, 128), F32),
        ]
        + [shape((rows, wide), BF16)] * SLOTS,
        compiler_params=params(),
        cost_estimate=cost(12 * d * f * wide, 12 * d * f + 20 * d * wide, 2 * f * wide),
        name="middle",
    )(info, att, x, g, wot, wo, upt, up, wd, wdt, vec)


def outer_kernel(count, *refs):
    out = refs[-1]
    total = None
    for n in range(count):
        part = dot(refs[2 * n][...], refs[2 * n + 1][...], NT)
        total = part if total is None else total + part
    out[...] = total.astype(out.dtype)


def outer(pairs, rows):
    m, n = pairs[0][0].shape[0], pairs[0][1].shape[0]
    in_specs, args = [], []
    depth = 0
    for a, b, width, a_at, b_at in pairs:
        in_specs.append(pl.BlockSpec((rows, width), functools.partial(lambda at, i: (i, at), a_at)))
        in_specs.append(
            pl.BlockSpec((n, width), functools.partial(lambda at, i: (0, at), b_at), pipeline_mode=pl.Buffered(1))
        )
        args += [a, b]
        depth += width
    return pl.pallas_call(
        functools.partial(outer_kernel, len(pairs)),
        grid=(m // rows,),
        in_specs=in_specs,
        out_specs=pl.BlockSpec((rows, n), lambda i: (i, 0)),
        out_shape=jax.ShapeDtypeStruct((m, n), BF16),
        compiler_params=params(),
        cost_estimate=cost(2 * m * n * depth, 2 * (m + n) * depth + 2 * m * n),
        name="outer",
    )(*args)


def out_grad_kernel(count, info, *refs):
    outs = refs[2 * count :]
    total = None
    for n in range(count):
        part = dot(refs[2 * n][...], refs[2 * n + 1][...], NT)
        total = part if total is None else total + part
    for k in range(SLOTS):

        @pl.when(pl.program_id(0) == k)
        def _():
            outs[k][...] = total.astype(BF16)


def out_grad_call(info, atts, y1g):
    rows = atts[0].shape[0] // SLOTS
    d = y1g.shape[0]
    count = len(atts)
    dev = info.shape[0] - 1
    in_specs, args = [], []
    for n in range(count):
        in_specs.append(pl.BlockSpec((rows, BLK), lambda k, i: (k, i[dev])))
        in_specs.append(pl.BlockSpec((d, BLK), functools.partial(lambda at, k, i: (0, at), n)))
        args += [atts[n], y1g]
    spec = pltpu.PrefetchScalarGridSpec(
        num_scalar_prefetch=1,
        grid=(SLOTS,),
        in_specs=in_specs,
        out_specs=[pl.BlockSpec((rows, d), lambda k, i: (0, 0))] * SLOTS,
    )
    return pl.pallas_call(
        functools.partial(out_grad_kernel, count),
        grid_spec=spec,
        out_shape=[jax.ShapeDtypeStruct((rows, d), BF16)] * SLOTS,
        compiler_params=params(),
        cost_estimate=cost(2 * SLOTS * rows * d * BLK * count, 4 * SLOTS * rows * d),
        name="out_grad_call",
    )(info, *args)


def attn_grad_kernel(a_ref, b_ref, out_ref, sum_ref):
    a = a_ref[...]
    out_ref[...] = dot(a, b_ref[...], NT).astype(BF16)
    sum_ref[...] = fold(a.astype(F32))


def attn_grad_call(dqkv, h1):
    m, total = dqkv.shape
    d = h1.shape[0]
    rows = m // 3
    return pl.pallas_call(
        attn_grad_kernel,
        grid=(3,),
        in_specs=[
            pl.BlockSpec((rows, total), lambda i: (i, 0)),
            pl.BlockSpec((d, total), lambda i: (0, 0), pipeline_mode=pl.Buffered(1)),
        ],
        out_specs=[pl.BlockSpec((rows, d), lambda i: (i, 0)), pl.BlockSpec((rows, 128), lambda i: (i, 0))],
        out_shape=[jax.ShapeDtypeStruct((m, d), BF16), jax.ShapeDtypeStruct((m, 128), F32)],
        compiler_params=params(),
        cost_estimate=cost(2 * m * d * total, 2 * (m + d) * total + 2 * m * d),
        name="attn_grad_call",
    )(dqkv, h1)


def h1_grad_kernel(w_ref, dqkv_ref, x_ref, out_ref, sum_ref):
    first = (pl.program_id(0) == 0) & (pl.program_id(1) == 0)
    hg = dot(w_ref[...], dqkv_ref[...])
    n, _ = normal(x_ref[...].astype(F32))
    out_ref[0] = hg.astype(BF16)
    for at, part in enumerate((fold(hg * n), fold(hg))):
        sum_ref[at] = jnp.where(first, part, sum_ref[at] + part)


def h1_grad_call(w, dqkv, x):
    d, total = x.shape
    per = total // (BLK * SLOTS)
    m = w.shape[1]
    at = lambda s, p: (0, p * SLOTS + s)
    return pl.pallas_call(
        h1_grad_kernel,
        grid=(SLOTS, per),
        in_specs=[
            pl.BlockSpec((d, m), lambda s, p: (0, 0), pipeline_mode=pl.Buffered(1)),
            pl.BlockSpec((m, BLK), at),
            pl.BlockSpec((d, BLK), at),
        ],
        out_specs=[
            pl.BlockSpec((1, d, BLK), lambda s, p: (s, 0, p)),
            pl.BlockSpec((2, d, 128), lambda s, p: (0, 0, 0)),
        ],
        out_shape=[jax.ShapeDtypeStruct((SLOTS, d, per * BLK), BF16), jax.ShapeDtypeStruct((2, d, 128), F32)],
        compiler_params=params(),
        cost_estimate=cost(2 * d * m * total, 2 * d * m + 6 * d * total),
        name="h1_grad_call",
    )(w, dqkv, x)


def input_grad_kernel(x_ref, a_ref, b_ref, y1g_ref, gain_ref, out_ref):
    n, root = normal(x_ref[...].astype(F32))
    e = (a_ref[...] + b_ref[...].astype(F32)) * gain_ref[...]
    e = root * (e - jnp.mean(e, axis=0, keepdims=True) - n * jnp.mean(e * n, axis=0, keepdims=True))
    out_ref[...] = (y1g_ref[...] + e).astype(BF16)


def input_grad_call(x, a, b, y1g, gain):
    d, rows = x.shape
    block = pl.BlockSpec((d, 128), lambda i: (0, i))
    return pl.pallas_call(
        input_grad_kernel,
        grid=(rows // 128,),
        in_specs=[block] * 4 + [pl.BlockSpec((d, 1), lambda i: (0, 0))],
        out_specs=block,
        out_shape=jax.ShapeDtypeStruct((d, rows), BF16),
        compiler_params=params(),
        cost_estimate=cost(20 * d * rows, 14 * d * rows),
        name="input_grad_call",
    )(x, a, b, y1g, gain)


def swap(v, k):
    return lax.ppermute(v, "tensor", [(i, i ^ k) for i in range(SLOTS)])


def gather(v):
    far = swap(v, 2)
    return v, swap(v, 1), far, swap(far, 1)


def scatter_sum(parts):
    wide = [p.astype(F32) for p in parts]
    far = (wide[2] + swap(parts[3], 1).astype(F32)).astype(BF16)
    near = wide[0] + swap(parts[1], 1).astype(F32)
    return near, swap(far, 2)


def token_starts(lengths, offsets, total, dev):
    pos = jnp.arange(total, dtype=jnp.int32)[:, None]
    inside = (pos >= offsets[None]) & (pos < (offsets + lengths)[None])
    first = jnp.max(jnp.where(inside, offsets[None], -1), axis=1)
    start = jnp.where(first >= 0, first, pos[:, 0])
    nb = total // BLK
    per = nb // SLOTS
    b = jnp.arange(nb, dtype=jnp.int32)
    first_key = start.reshape(nb, BLK)[:, 0] // BLK
    place = (b % per) * SLOTS + ((b // per) ^ dev)
    last_query = jnp.max(jnp.where(first_key[None, :] <= b[:, None], b[None, :], 0), axis=1)
    info = jnp.concatenate([first_key, place, last_query, jnp.full((1,), dev)])
    return start[None], info.astype(jnp.int32)


def body(
    tokens,
    cotangent,
    ln1_gain,
    ln1_bias,
    attn_weight,
    qv_bias,
    out_weight,
    out_bias,
    ln2_gain,
    ln2_bias,
    up_weight,
    up_bias,
    down_weight,
    down_bias,
    cell_lengths,
    cell_offsets,
):
    rows, d = tokens.shape
    width = attn_weight.shape[2]
    heads = width // HEAD_DIM
    total = rows * SLOTS
    per = rows // BLK
    dev = lax.axis_index("tensor")
    start, info = token_starts(cell_lengths[0], cell_offsets[0], total, dev)

    x_own = tokens.T
    g_own = cotangent.T
    x_parts = gather(x_own)
    wo = jnp.concatenate(gather(out_weight), 0)
    g_parts = gather(g_own)

    w_in = attn_weight.transpose(1, 2, 0)
    w_back = w_in.reshape(3 * width, d).T
    vec1 = jnp.stack([ln1_gain, ln1_bias], 1)
    qkv_bias = jnp.stack([qv_bias[0], jnp.zeros_like(qv_bias[0]), qv_bias[1]])[:, :, None]
    carry = qkv_call(0, x_parts[0], x_parts[1], w_in, vec1, qkv_bias, None)
    x_all, h1, qkv, kn, vn = qkv_call(1, x_parts[2], x_parts[3], w_in, vec1, qkv_bias, carry)

    def chunked(parts):
        cut = lambda p, c: p[:, c * BLK : (c + 1) * BLK]
        return jnp.concatenate([cut(p, c) for c in range(per) for p in parts], 1)

    g_all = chunked(g_parts)
    wot, upt, wdt = wo.T, up_weight.T, down_weight.T
    vec2 = jnp.stack([out_bias, ln2_gain, ln2_bias, up_bias], 1)

    fronts = [attend(c, info, start, qkv, kn) for c in range(per)]
    atts = [jnp.concatenate(gather(o.reshape(width, SLOTS * BLK)), 0) for o, _ in fronts]
    mids = [
        middle(c, info, atts[c], x_all, g_all, wot, wo, upt, up_weight, down_weight, wdt, vec2) for c in range(per)
    ]
    h2s, acts, pgs, layers, y1gs, owns, sums = zip(*[m[:7] for m in mids])
    attg = [scatter_sum(m[7:]) for m in mids]
    do = jnp.concatenate([(a + b.astype(F32)).astype(BF16) for a, b in attg], 1).reshape(heads, HEAD_DIM, total)
    o = jnp.concatenate([f[0] for f in fronts], 2)
    lse = jnp.concatenate([f[1] for f in fronts], 1)

    wide = SLOTS * BLK
    down_grad = outer([(acts[c], g_all, wide, 0, c) for c in range(per)], width)
    up_grad = outer([(h2s[c], pgs[c], wide, 0, 0) for c in range(per)], width)
    early = lax.psum((down_grad, up_grad), "dp")

    y1_parts = [scatter_sum([y[k] for k in range(SLOTS)]) for y in y1gs]
    y1_grad = jnp.concatenate([a + b.astype(F32) for a, b in y1_parts], 1)
    layer_parts = [scatter_sum([y[k] for k in range(SLOTS)]) for y in layers]
    layer = jnp.concatenate([a + b.astype(F32) for a, b in layer_parts], 1)
    layer = (jnp.concatenate(owns, 1) + layer + down_bias[:, None]).astype(BF16)

    out_parts = out_grad_call(info, atts, y1_grad.astype(BF16))
    out_near, out_far = scatter_sum(out_parts)
    out_grad = (out_near + out_far.astype(F32)).astype(BF16)

    dqkv = attend_back(info, start, qkv, kn, vn, o, do, lse).reshape(3 * width, total)
    h1_parts, sum1 = h1_grad_call(w_back, dqkv, x_all)
    attn_grad, qkv_sum = attn_grad_call(dqkv, h1)
    near, far = scatter_sum([h1_parts[k] for k in range(SLOTS)])
    input_grad = input_grad_call(x_own, near, far, y1_grad, ln1_gain[:, None])

    sum2 = jnp.sum(sum(sums), axis=2)
    sum1 = jnp.sum(sum1, axis=2)
    qkv_sum = jnp.sum(qkv_sum, axis=1).reshape(3, width)
    down_sum = jnp.sum(g_own.astype(F32), axis=1)
    small = jnp.concatenate([sum1, sum2[:3], down_sum[None]], 0)
    small = lax.psum(small, ("dp", "tensor"))
    late = lax.optimization_barrier((attn_grad, out_grad, early))
    early = late[2]
    late = lax.psum(late[:2], "dp")
    dp_small = lax.psum((sum2[3], qkv_sum), "dp")

    down_grad, up_grad = (v.astype(F32) for v in early)
    attn_grad, out_grad = (v.astype(F32) for v in late)
    up_bias_grad, qkv_sum = dp_small
    return (
        layer.T,
        input_grad.T,
        small[0],
        small[1],
        attn_grad.reshape(3, width, d).transpose(2, 0, 1),
        jnp.stack([qkv_sum[0], qkv_sum[2]]),
        out_grad,
        small[4],
        small[2],
        small[3],
        up_grad,
        up_bias_grad,
        down_grad,
        small[5],
    )


def solution(mesh):
    rows = P(("dp", "tensor"), None)
    in_specs = (
        rows,
        rows,
        P(),
        P(),
        P(None, None, "tensor"),
        P(None, "tensor"),
        P("tensor", None),
        P(),
        P(),
        P(),
        P(None, "tensor"),
        P("tensor"),
        P("tensor", None),
        P(),
        P("dp", None),
        P("dp", None),
    )
    out_specs = (
        rows,
        rows,
        P(),
        P(),
        P(None, None, "tensor"),
        P(None, "tensor"),
        P("tensor", None),
        P(),
        P(),
        P(),
        P(None, "tensor"),
        P("tensor"),
        P("tensor", None),
        P(),
    )
    return jax.shard_map(body, mesh=mesh, in_specs=in_specs, out_specs=out_specs, check_vma=False)
```

time: 1440 us -> 603 us (0.42)
  waiting for transfers between devices: 761 us -> 180 us
  matrix products: 375 us -> 0 us
  Pallas kernels: 0 us -> 179 us
  other arithmetic: 149 us -> 51.8 us
  blocking collectives: 51.9 us -> 80.3 us
  starting transfers between devices: 0.37 us -> 22.8 us
    dot_general x40 -> x0, matrix products: 375 us -> none  [the longest x4 63.7 us: attend_back(): jnp.einsum('qhe,khe->hqk', grad_block, value_rows, preferred_element_type...]
    psum x1 -> x2, waiting for transfers between devices: 424 us -> 63.9 us  [the longest x1 63.9 us: body(): late = lax.psum(late[:2], 'dp')]
    reduce_scatter x4 -> x0, waiting for transfers between devices: 199 us -> none  [the longest x1 76.1 us: body(): lax.psum_scatter(jnp.dot(piece, out_weight, preferred_element_type=jnp.fl...]
    pallas_call x0 -> x13, Pallas kernels: none -> 179 us  [the longest x2 75.5 us: middle(): pl.pallas_call(middle_kernel, grid_spec=spec, out_shape=[shape((d, wide),...]
    all_gather x4 -> x0, waiting for transfers between devices: 137 us -> none  [the longest x1 39.2 us: body(): lax.all_gather(h1_rows.astype(jnp.bfloat16), 'tensor', axis=0, tiled=True)]
    ppermute x0 -> x39, waiting for transfers between devices: none -> 116 us  [swap(): return lax.ppermute(v, 'tensor', [(i, i ^ k) for i in range(SLOTS)])]
    convert_element_type x8 -> x15, other arithmetic: 84 us -> 28.1 us  [the longest x8 15 us: scatter_sum(): far = (wide[2] + swap(parts[3], 1).astype(F32)).astype(BF16)]
    reduce_sum x17 -> x4, other arithmetic: 47.6 us -> 4.59 us  [the longest x1 2.49 us: body(): sum2 = jnp.sum(sum(sums), axis=2)]
  transfers between devices with their start and end apart: 9 -> 41, of which waited for: 9 -> 9; matrix products, arithmetic and copies ran while one was open for 5% -> 17% of each run, Pallas kernels for 0% -> 30%
where the time goes in v1:
time: 603 us; the launch traced here: 592 us
  waiting for transfers between devices  180 us (30%)
  Pallas kernels  179 us (30%)
  blocking collectives  80.3 us (13%)
  local copies, waits for them, and re-layouts  63 us (10%)
  other arithmetic  51.8 us (9%)
  starting transfers between devices  22.8 us (4%)
  between operations  15 us (2%)
    ppermute x39, waiting for transfers between devices, swap(): return lax.ppermute(v, 'tensor', [(i, i ^ k) for i in range(SLOTS)])  116 us
    pallas_call x2, Pallas kernels, middle(): pl.pallas_call(middle_kernel, grid_spec=spec, out_shape=[shape((d, wide),...  75.5 us
    psum x1, waiting for transfers between devices, body(): late = lax.psum(late[:2], 'dp')  63.9 us
    psum x1, blocking collectives, body(): small = lax.psum(small, ('dp', 'tensor'))  41.3 us
    psum x1, blocking collectives, body(): dp_small = lax.psum((sum2[3], qkv_sum), 'dp')  39.1 us
    unnamed x102, local copies, waits for them, and re-layouts  37.1 us
    ppermute x39, starting transfers between devices, swap(): return lax.ppermute(v, 'tensor', [(i, i ^ k) for i in range(SLOTS)])  22.6 us
    pallas_call x1, Pallas kernels, attend_back(): pl.pallas_call(functools.partial(attend_back_kernel, heads, nb, per), gri...  20.9 us
  transfers between devices with their start and end apart: 41, of which 9 were waited for; matrix products, arithmetic and copies ran while one was open for 17% of the time, Pallas kernels for 30%

profile of v1, /device:TPU:0, one launch (start us, length us, event | category | flops | bytes accessed | tf_op | source)
XLA Modules:
  0.0 592.1 jit_solution(17980566383579273072)
XLA Ops:
  7.8 2.6 collective-permute-start.10
  14.4 2.1 slice_dynamic-update-slice_fusion.7
  21.0 2.4 copy.90
  23.4 5.2 copy.84
  28.6 5.2 copy.85
  38.1 36.9 %collective-permute-done.a_ref = bf16[1120,512]{1,0:T(8,128)(2,1)} collective-permute-done((bf16[1120,512]{1,0:T(8,128)(2,1)}, bf16[1120,512]{1,0:T(8,128)(2,1)}, u32[]{:S(2)}, u32[]{:S(2)}) %collective-permute-start) | collective-permute-done | bytes 1146912 | tf_op jit(solution)/shard_map/ppermute | solution.py:533
  77.4 7.3 %qkv_call.2 = (bf16[1120,2048]{1,0:T(8,128)(2,1)}, bf16[1120,2048]{1,0:T(8,128)(2,1)}, bf16[15,56,2048]{2,1,0:T(8,128)(2,1)}, bf16[5,2048,56]{2,1,0:T(8,128)(2,1)}, bf16[5,2048,56]{2,1,0:T(8,128)(2,1)}) custom-call(bf16[1120,512]{1,0:T(8,128)(2,1)S(1)} %bitcast.92, bf16[1120,512]{1,0:T(8,128)(2,1)} %collective-permute-done.2.b_ref, ...), custom_call_target="tpu_custom_call" | custom-call | flops 1926758400 | bytes 11056640 | tf_op jit(solution)/shard_map/qkv_call/pallas_call | solution.py:100
  87.7 5.2 copy.86.wot
  92.9 7.3 %qkv_call.3 = (bf16[1120,2048]{1,0:T(8,128)(2,1)}, bf16[1120,2048]{1,0:T(8,128)(2,1)}, bf16[15,56,2048]{2,1,0:T(8,128)(2,1)}, bf16[5,2048,56]{2,1,0:T(8,128)(2,1)}, bf16[5,2048,56]{2,1,0:T(8,128)(2,1)}) custom-call(bf16[1120,512]{1,0:T(8,128)(2,1)} %collective-permute-done.a_ref, ...), custom_call_target="tpu_custom_call", output_to_operand_aliasing={{0}: (5, {}), {1}: (6, {}), {2}: (7, {}), {3}: (8, {}), {4}... | custom-call | flops 1926758400 | bytes 11056640 | tf_op jit(solution)/shard_map/qkv_call/pallas_call | solution.py:100
  101.9 8.2 %attend.3 = (bf16[5,56,1024]{2,1,0:T(8,128)(2,1)S(1)}, f32[8,1024]{1,0:T(8,128)S(1)}) custom-call(s32[25]{0:T(128)S(1)} %pad_add_fusion.info, s32[1,2048]{1,0:T(1,128)S(1)} %compare_select_fusion.start_ref, bf16[15,56,2048]{2,1,0:T(8,128)(2,1)} %get-tuple-element.67.q_ref.v_ref.k_ref, bf16[5,2048,56]{2,1,0:T(8,128)(2,1)S(1)} %copy-done.2, ...), custom_call_target="tpu_custom_call" | custom-call | flops 6000000000 | bytes 6000000 | tf_op jit(solution)/shard_map/attend/pallas_call | solution.py:179
  112.0 9.0 %attend.2 = (bf16[5,56,1024]{2,1,0:T(8,128)(2,1)S(1)}, f32[8,1024]{1,0:T(8,128)S(1)}) custom-call(s32[25]{0:T(128)S(1)} %pad_add_fusion.info, s32[1,2048]{1,0:T(1,128)S(1)} %compare_select_fusion.start_ref, bf16[15,56,2048]{2,1,0:T(8,128)(2,1)} %get-tuple-element.67.q_ref.v_ref.k_ref, bf16[5,2048,56]{2,1,0:T(8,128)(2,1)S(1)} %copy-done.2, ...), custom_call_target="tpu_custom_call" | custom-call | flops 6000000000 | bytes 6000000 | tf_op jit(solution)/shard_map/attend/pallas_call | solution.py:179
  122.7 2.0 slice_dynamic-update-slice_fusion.4
  129.5 7.9 %collective-permute-done.4 = bf16[280,1024]{1,0:T(8,128)(2,1)S(1)} collective-permute-done((bf16[280,1024]{1,0:T(8,128)(2,1)S(1)}, bf16[280,1024]{1,0:T(8,128)(2,1)S(1)}, u32[]{:S(2)}, u32[]{:S(2)}) %collective-permute-start.4) | collective-permute-done | bytes 573472 | tf_op jit(solution)/shard_map/ppermute | solution.py:533
  141.5 37.7 %middle.2 = (bf16[1120,1024]{1,0:T(8,128)(2,1)}, bf16[1120,1024]{1,0:T(8,128)(2,1)}, bf16[1120,1024]{1,0:T(8,128)(2,1)}, bf16[4,1120,256]{2,1,0:T(8,128)(2,1)}, ...) custom-call(s32[25]{0:T(128)S(1)} %pad_add_fusion.info, ...), custom_call_target="tpu_custom_call" | custom-call | flops 15414067200 | bytes 37990400 | tf_op jit(solution)/shard_map/middle/pallas_call | solution.py:362
  179.7 2.4 slice_bitcast_fusion.9
  185.5 37.8 %middle.3 = (bf16[1120,1024]{1,0:T(8,128)(2,1)}, bf16[1120,1024]{1,0:T(8,128)(2,1)}, bf16[1120,1024]{1,0:T(8,128)(2,1)}, bf16[4,1120,256]{2,1,0:T(8,128)(2,1)}, ...) custom-call(s32[25]{0:T(128)S(1)} %pad_add_fusion.info, ...), custom_call_target="tpu_custom_call" | custom-call | flops 15414067200 | bytes 37990400 | tf_op jit(solution)/shard_map/middle/pallas_call | solution.py:362
  223.4 3.3 slice_bitcast_fusion.7
  226.7 2.3 slice_bitcast_fusion.3
  229.1 10.3 %outer.2 = bf16[1120,1120]{1,0:T(8,128)(2,1)} custom-call(bf16[1120,1024]{1,0:T(8,128)(2,1)S(1)} %copy-done.17, bf16[1120,2048]{1,0:T(8,128)(2,1)} %slice_dynamic-update-slice_fusion.g_ref.refs_1_.refs_3_, bf16[1120,1024]{1,0:T(8,128)(2,1)S(1)} %copy-done.18, bf16[1120,2048]{1,0:T(8,128)(2,1)} %slice_dynamic-update-slice_fusion.g_ref.refs_1_.refs_3_), custom_call_target="tpu_custom_call" | custom-call | flops 5138022400 | bytes 11683840 | tf_op jit(solution)/shard_map/outer/pallas_call | solution.py:401
  239.4 2.5 add_reduce_fusion
  242.4 9.6 %outer.3 = bf16[1120,1120]{1,0:T(8,128)(2,1)} custom-call(bf16[1120,1024]{1,0:T(8,128)(2,1)S(1)} %copy-done.19, bf16[1120,1024]{1,0:T(8,128)(2,1)S(1)} %copy-done.20, bf16[1120,1024]{1,0:T(8,128)(2,1)} %get-tuple-element.103.refs_2_, bf16[1120,1024]{1,0:T(8,128)(2,1)} %get-tuple-element.104.refs_3_), custom_call_target="tpu_custom_call" | custom-call | flops 5138022400 | bytes 11683840 | tf_op jit(solution)/shard_map/outer/pallas_call | solution.py:401
  252.8 2.2 fusion.10
  255.1 2.3 fusion.6
  257.8 2.0 fusion.8
  265.8 11.4 %collective-permute-done.23 = bf16[280,1024]{1,0:T(8,128)(2,1)S(1)} collective-permute-done((bf16[280,1024]{1,0:T(8,128)(2,1)S(1)}, bf16[280,1024]{1,0:T(8,128)(2,1)S(1)}, u32[]{:S(2)}, u32[]{:S(2)}) %collective-permute-start.23) | collective-permute-done | bytes 573472 | tf_op jit(solution)/shard_map/ppermute | solution.py:533
  280.5 9.1 %collective-permute-done.26 = bf16[280,1024]{1,0:T(8,128)(2,1)S(1)} collective-permute-done((bf16[280,1024]{1,0:T(8,128)(2,1)S(1)}, bf16[280,1024]{1,0:T(8,128)(2,1)S(1)}, u32[]{:S(2)}, u32[]{:S(2)}) %collective-permute-start.26) | collective-permute-done | bytes 573472 | tf_op jit(solution)/shard_map/ppermute | solution.py:533
  293.4 20.9 %attend_back.1 = bf16[15,56,2048]{2,1,0:T(8,128)(2,1)} custom-call(s32[25]{0:T(128)S(1)} %pad_add_fusion.info, s32[1,2048]{1,0:T(1,128)S(1)} %compare_select_fusion.start_ref, bf16[15,56,2048]{2,1,0:T(8,128)(2,1)} %get-tuple-element.67.q_ref.v_ref.k_ref, bf16[15,56,2048]{2,1,0:T(8,128)(2,1)} %get-tuple-element.67.q_ref.v_ref.k_ref, ...), custom_call_target="tpu_custom_call" | custom-call | flops 16000000000 | bytes 12000000 | tf_op jit(solution)/shard_map/attend_back/pallas_call | solution.py:283
  314.3 10.8 %h1_grad_call.1 = (bf16[4,1120,512]{2,1,0:T(8,128)(2,1)}, f32[2,1120,128]{2,1,0:T(8,128)S(1)}) custom-call(bf16[1120,840]{1,0:T(8,128)(2,1)S(1)} %bitcast.88, bf16[840,2048]{1,0:T(8,128)(2,1)} %bitcast.94, bf16[1120,2048]{1,0:T(8,128)(2,1)} %get-tuple-element.70.x_ref), custom_call_target="tpu_custom_call" | custom-call | flops 3853516800 | bytes 15644160 | tf_op jit(solution)/shard_map/h1_grad_call/pallas_call | solution.py:491
  327.6 8.5 %attn_grad_call.1 = (bf16[840,1120]{1,0:T(8,128)(2,1)}, f32[840,128]{1,0:T(8,128)S(1)}) custom-call(bf16[840,2048]{1,0:T(8,128)(2,1)S(1)} %bitcast.95, bf16[1120,2048]{1,0:T(8,128)(2,1)} %get-tuple-element.93.b_ref), custom_call_target="tpu_custom_call" | custom-call | flops 3853516800 | bytes 9909760 | tf_op jit(solution)/shard_map/attn_grad_call/pallas_call | solution.py:462
  338.7 11.8 %collective-permute-done.35 = bf16[1120,256]{1,0:T(8,128)(2,1)S(1)} collective-permute-done((bf16[1120,256]{1,0:T(8,128)(2,1)S(1)}, bf16[1120,256]{1,0:T(8,128)(2,1)S(1)}, u32[]{:S(2)}, u32[]{:S(2)}) %collective-permute-start.35) | collective-permute-done | bytes 573472 | tf_op jit(solution)/shard_map/ppermute | solution.py:533
  350.5 2.5 fusion.5
  355.2 5.5 out_grad_call.1
  361.2 3.1 slice_bitcast_fusion
  364.3 39.1 %all-reduce = (f32[3,280]{1,0:T(4,128)S(1)}, f32[1120]{0:T(1024)}) all-reduce(f32[3,280]{1,0:T(4,128)S(1)} %reshape.122, f32[1120]{0:T(1024)S(1)} %slice_reduce_fusion.1), channel_id=1, replica_groups=mesh['dp'=8,'tensor'=4] {'dp'}, use_global_device_ids=true, to_apply=%region_10.11 | all-reduce | flops 1960 | bytes 15680 | tf_op jit(solution)/shard_map/psum | solution.py:651
  403.4 41.3 %psum.49 = f32[6,1120]{1,0:T(8,128)S(1)} all-reduce(f32[6,1120]{1,0:T(8,128)S(1)} %pad_maximum_fusion.6), channel_id=1, replica_groups=mesh['dp'=8,'tensor'=4] {'dp','tensor'}, use_global_device_ids=true, to_apply=%region_5.6 | all-reduce | flops 6720 | bytes 53760 | tf_op jit(solution)/shard_map/psum | solution.py:647
  446.1 2.2 collective-permute-start.38
  448.9 3.0 pad_maximum_fusion.2.y1g_ref
  452.6 9.6 %collective-permute-done.38 = bf16[280,1120]{1,0:T(8,128)(2,1)S(1)} collective-permute-done((bf16[280,1120]{1,0:T(8,128)(2,1)S(1)}, bf16[280,1120]{1,0:T(8,128)(2,1)S(1)}, u32[]{:S(2)}, u32[]{:S(2)}) %collective-permute-start.38) | collective-permute-done | bytes 627232 | tf_op jit(solution)/shard_map/ppermute | solution.py:533
  462.2 2.2 add_convert_fusion
  468.8 3.5 fusion.2
  473.0 8.2 %collective-permute-done.20 = bf16[1120,256]{1,0:T(8,128)(2,1)S(1)} collective-permute-done((bf16[1120,256]{1,0:T(8,128)(2,1)S(1)}, bf16[1120,256]{1,0:T(8,128)(2,1)S(1)}, u32[]{:S(2)}, u32[]{:S(2)}) %collective-permute-start.20) | collective-permute-done | bytes 573472 | tf_op jit(solution)/shard_map/ppermute | solution.py:533
  483.9 21.5 %collective-permute-done.29.b_ref = bf16[1120,512]{1,0:T(8,128)(2,1)S(1)} collective-permute-done((bf16[1120,512]{1,0:T(8,128)(2,1)S(1)}, bf16[1120,512]{1,0:T(8,128)(2,1)S(1)}, u32[]{:S(2)}, u32[]{:S(2)}) %collective-permute-start.29) | collective-permute-done | bytes 1146912 | tf_op jit(solution)/shard_map/ppermute | solution.py:533
  505.4 5.7 input_grad_call.1
  511.1 2.7 convert_element_type.263
  513.9 2.7 convert_element_type.264
  516.6 63.9 %all-reduce.6.cloned.1.call-done = (bf16[1120,3,280]{0,2,1:T(8,128)(2,1)}, bf16[280,1120]{1,0:T(8,128)(2,1)}) async-done(((bf16[1120,3,280]{0,2,1:T(8,128)(2,1)}, bf16[280,1120]{1,0:T(8,128)(2,1)}), (bf16[1120,3,280]{0,2,1:T(8,128)(2,1)}, bf16[280,1120]{1,0:T(8,128)(2,1)})) %all-reduce.6.cloned.1.call-update) | async-done | bytes 2508816 | tf_op jit(solution)/shard_map/psum | solution.py:650
  580.5 2.4 convert_element_type.262
  582.8 2.2 transpose.50
  (223 shorter events, 69.7 us)
Async XLA Ops:
  7.3 457.1 %all-reduce.8.cloned.1.call-start = ((), (), s32[]{:S(2)}) async-start(), calls=%async_computation.1 | async-start | bytes 10321920 | tf_op jit(solution)/shard_map/psum | solution.py:624
  7.3 11.3 %collective-permute-start.9 = (bf16[280,1120]{1,0:T(8,128)(2,1)}, bf16[280,1120]{1,0:T(8,128)(2,1)S(1)}, u32[]{:S(2)}, u32[]{:S(2)}) collective-permute-start(bf16[280,1120]{1,0:T(8,128)(2,1)} %param.22), channel_id=1, source_target_pairs={{0,1},{1,0},{2,3},{3,2},{4,5},{5,4},{6,7},{7,6},{8,9},{9,8},{10,11... | collective-permute-start | bytes 1881608 | tf_op jit(solution)/shard_map/ppermute | solution.py:533
  7.8 26.0 %collective-permute-start.10 = (bf16[280,1120]{1,0:T(8,128)(2,1)}, bf16[280,1120]{1,0:T(8,128)(2,1)}, u32[]{:S(2)}, u32[]{:S(2)}) collective-permute-start(bf16[280,1120]{1,0:T(8,128)(2,1)} %param.22), channel_id=1, source_target_pairs={{0,2},{1,3},{2,0},{3,1},{4,6},{5,7},{6,4},{7,5},{8,10},{9,11},{10,... | collective-permute-start | bytes 1881608 | tf_op jit(solution)/shard_map/ppermute | solution.py:533
  10.4 64.6 %collective-permute-start.7 = (bf16[1120,512]{1,0:T(8,128)(2,1)}, bf16[1120,512]{1,0:T(8,128)(2,1)}, u32[]{:S(2)}, u32[]{:S(2)}) collective-permute-start(bf16[1120,512]{1,0:T(8,128)(2,1)} %bitcast.96), channel_id=1, source_target_pairs={{0,2},{1,3},{2,0},{3,1},{4,6},{5,7},{6,4},{7,5},{8,10},{9,11},{10,... | collective-permute-start | bytes 3440648 | tf_op jit(solution)/shard_map/ppermute | solution.py:533
  10.5 65.0 %collective-permute-start.6 = (bf16[1120,512]{1,0:T(8,128)(2,1)}, bf16[1120,512]{1,0:T(8,128)(2,1)}, u32[]{:S(2)}, u32[]{:S(2)}) collective-permute-start(bf16[1120,512]{1,0:T(8,128)(2,1)} %bitcast.97), channel_id=1, source_target_pairs={{0,1},{1,0},{2,3},{3,2},{4,5},{5,4},{6,7},{7,6},{8,9},{9,8},{10,11... | collective-permute-start | bytes 3440648 | tf_op jit(solution)/shard_map/ppermute | solution.py:533
  10.6 64.4 %collective-permute-start = (bf16[1120,512]{1,0:T(8,128)(2,1)}, bf16[1120,512]{1,0:T(8,128)(2,1)}, u32[]{:S(2)}, u32[]{:S(2)}) collective-permute-start(bf16[1120,512]{1,0:T(8,128)(2,1)} %bitcast.90), channel_id=1, source_target_pairs={{0,2},{1,3},{2,0},{3,1},{4,6},{5,7},{6,4},{7,5},{8,10},{9,11},{10,... | collective-permute-start | bytes 3440648 | tf_op jit(solution)/shard_map/ppermute | solution.py:533
  18.7 58.8 %collective-permute-start.2 = (bf16[1120,512]{1,0:T(8,128)(2,1)}, bf16[1120,512]{1,0:T(8,128)(2,1)}, u32[]{:S(2)}, u32[]{:S(2)}) collective-permute-start(bf16[1120,512]{1,0:T(8,128)(2,1)} %bitcast.91), channel_id=1, source_target_pairs={{0,1},{1,0},{2,3},{3,2},{4,5},{5,4},{6,7},{7,6},{8,9},{9,8},{10,11... | collective-permute-start | bytes 3440648 | tf_op jit(solution)/shard_map/ppermute | solution.py:533
  33.8 43.7 %copy-start.8 = (bf16[512,1120]{0,1:T(8,128)(2,1)S(1)}, bf16[512,1120]{0,1:T(8,128)(2,1)}, u32[]{:S(2)}) copy-start(bf16[512,1120]{0,1:T(8,128)(2,1)} %param.16) | copy-start | bytes 3440644
  33.9 52.9 %collective-permute-start.11 = (bf16[280,1120]{1,0:T(8,128)(2,1)}, bf16[280,1120]{1,0:T(8,128)(2,1)S(1)}, u32[]{:S(2)}, u32[]{:S(2)}) collective-permute-start(bf16[280,1120]{1,0:T(8,128)(2,1)} %collective-permute-done.10), channel_id=1, source_target_pairs={{0,1},{1,0},{2,3},{3,2},{4,5},{5,4},{6,7},{7,6},{8,9},{9,8},{10,11... | collective-permute-start | bytes 1881608 | tf_op jit(solution)/shard_map/ppermute | solution.py:533
  75.0 17.9 %collective-permute-start.1 = (bf16[1120,512]{1,0:T(8,128)(2,1)}, bf16[1120,512]{1,0:T(8,128)(2,1)}, u32[]{:S(2)}, u32[]{:S(2)}) collective-permute-start(bf16[1120,512]{1,0:T(8,128)(2,1)} %collective-permute-done.a_ref), channel_id=1, source_target_pairs={{0,1},{1,0},{2,3},{3,2},{4,5},{5,4},{6,7},{7,6},{8,9},{9,8},{10,11... | collective-permute-start | bytes 3440648 | tf_op jit(solution)/shard_map/ppermute | solution.py:533
  75.0 47.7 %collective-permute-start.8 = (bf16[1120,512]{1,0:T(8,128)(2,1)}, bf16[1120,512]{1,0:T(8,128)(2,1)}, u32[]{:S(2)}, u32[]{:S(2)}) collective-permute-start(bf16[1120,512]{1,0:T(8,128)(2,1)} %collective-permute-done.7), channel_id=1, source_target_pairs={{0,1},{1,0},{2,3},{3,2},{4,5},{5,4},{6,7},{7,6},{8,9},{9,8},{10,11... | collective-permute-start | bytes 3440648 | tf_op jit(solution)/shard_map/ppermute | solution.py:533
  110.1 29.3 %collective-permute-start.13 = (bf16[280,1024]{1,0:T(8,128)(2,1)S(1)}, bf16[280,1024]{1,0:T(8,128)(2,1)S(1)}, u32[]{:S(2)}, u32[]{:S(2)}) collective-permute-start(bf16[280,1024]{1,0:T(8,128)(2,1)S(1)} %bitcast.82), channel_id=1, source_target_pairs={{0,2},{1,3},{2,0},{3,1},{4,6},{5,7},{6,4},{7,5},{8,10},{9,11},{10,... | collective-permute-start | bytes 1720328 | tf_op jit(solution)/shard_map/ppermute | solution.py:533
  112.0 71.4 %collective-permute-start.12 = (bf16[280,1024]{1,0:T(8,128)(2,1)S(1)}, bf16[280,1024]{1,0:T(8,128)(2,1)S(1)}, u32[]{:S(2)}, u32[]{:S(2)}) collective-permute-start(bf16[280,1024]{1,0:T(8,128)(2,1)S(1)} %bitcast.83), channel_id=1, source_target_pairs={{0,1},{1,0},{2,3},{3,2},{4,5},{5,4},{6,7},{7,6},{8,9},{9,8},{10,11... | collective-permute-start | bytes 1720328 | tf_op jit(solution)/shard_map/ppermute | solution.py:533
  121.0 16.4 %collective-permute-start.4 = (bf16[280,1024]{1,0:T(8,128)(2,1)S(1)}, bf16[280,1024]{1,0:T(8,128)(2,1)S(1)}, u32[]{:S(2)}, u32[]{:S(2)}) collective-permute-start(bf16[280,1024]{1,0:T(8,128)(2,1)S(1)} %bitcast.85), channel_id=1, source_target_pairs={{0,2},{1,3},{2,0},{3,1},{4,6},{5,7},{6,4},{7,5},{8,10},{9,11},{10,... | collective-permute-start | bytes 1720328 | tf_op jit(solution)/shard_map/ppermute | solution.py:533
  121.3 18.6 %collective-permute-start.3 = (bf16[280,1024]{1,0:T(8,128)(2,1)S(1)}, bf16[280,1024]{1,0:T(8,128)(2,1)S(1)}, u32[]{:S(2)}, u32[]{:S(2)}) collective-permute-start(bf16[280,1024]{1,0:T(8,128)(2,1)S(1)} %bitcast.86), channel_id=1, source_target_pairs={{0,1},{1,0},{2,3},{3,2},{4,5},{5,4},{6,7},{7,6},{8,9},{9,8},{10,11... | collective-permute-start | bytes 1720328 | tf_op jit(solution)/shard_map/ppermute | solution.py:533
  137.4 2.5 collective-permute-start.5
  139.4 44.4 %collective-permute-start.14 = (bf16[280,1024]{1,0:T(8,128)(2,1)S(1)}, bf16[280,1024]{1,0:T(8,128)(2,1)S(1)}, u32[]{:S(2)}, u32[]{:S(2)}) collective-permute-start(bf16[280,1024]{1,0:T(8,128)(2,1)S(1)} %collective-permute-done.13), channel_id=1, source_target_pairs={{0,1},{1,0},{2,3},{3,2},{4,5},{5,4},{6,7},{7,6},{8,9},{9,8},{10,11... | collective-permute-start | bytes 1720328 | tf_op jit(solution)/shard_map/ppermute | solution.py:533
  179.2 86.7 %collective-permute-start.21 = (bf16[280,1024]{1,0:T(8,128)(2,1)}, bf16[280,1024]{1,0:T(8,128)(2,1)}, u32[]{:S(2)}, u32[]{:S(2)}) collective-permute-start(bf16[280,1024]{1,0:T(8,128)(2,1)} %get-tuple-element.78), channel_id=1, source_target_pairs={{0,1},{1,0},{2,3},{3,2},{4,5},{5,4},{6,7},{7,6},{8,9},{9,8},{10,11... | collective-permute-start | bytes 1720328 | tf_op jit(solution)/shard_map/ppermute | solution.py:533
  179.3 80.5 %collective-permute-start.22 = (bf16[280,1024]{1,0:T(8,128)(2,1)}, bf16[280,1024]{1,0:T(8,128)(2,1)}, u32[]{:S(2)}, u32[]{:S(2)}) collective-permute-start(bf16[280,1024]{1,0:T(8,128)(2,1)} %get-tuple-element.80), channel_id=1, source_target_pairs={{0,1},{1,0},{2,3},{3,2},{4,5},{5,4},{6,7},{7,6},{8,9},{9,8},{10,11... | collective-permute-start | bytes 1720328 | tf_op jit(solution)/shard_map/ppermute | solution.py:533
  182.2 282.2 %collective-permute-start.15 = (bf16[1120,256]{1,0:T(8,128)(2,1)}, bf16[1120,256]{1,0:T(8,128)(2,1)}, u32[]{:S(2)}, u32[]{:S(2)}) collective-permute-start(bf16[1120,256]{1,0:T(8,128)(2,1)} %get-tuple-element.130), channel_id=1, source_target_pairs={{0,1},{1,0},{2,3},{3,2},{4,5},{5,4},{6,7},{7,6},{8,9},{9,8},{10,11... | collective-permute-start | bytes 1720328 | tf_op jit(solution)/shard_map/ppermute | solution.py:533
  183.3 69.0 %collective-permute-start.16 = (bf16[1120,256]{1,0:T(8,128)(2,1)}, bf16[1120,256]{1,0:T(8,128)(2,1)}, u32[]{:S(2)}, u32[]{:S(2)}) collective-permute-start(bf16[1120,256]{1,0:T(8,128)(2,1)} %get-tuple-element.131), channel_id=1, source_target_pairs={{0,1},{1,0},{2,3},{3,2},{4,5},{5,4},{6,7},{7,6},{8,9},{9,8},{10,11... | collective-permute-start | bytes 1720328 | tf_op jit(solution)/shard_map/ppermute | solution.py:533
  183.8 71.2 %collective-permute-start.31 = (bf16[1120,256]{1,0:T(8,128)(2,1)}, bf16[1120,256]{1,0:T(8,128)(2,1)}, u32[]{:S(2)}, u32[]{:S(2)}) collective-permute-start(bf16[1120,256]{1,0:T(8,128)(2,1)} %get-tuple-element.127), channel_id=1, source_target_pairs={{0,1},{1,0},{2,3},{3,2},{4,5},{5,4},{6,7},{7,6},{8,9},{9,8},{10,11... | collective-permute-start | bytes 1720328 | tf_op jit(solution)/shard_map/ppermute | solution.py:533
  229.0 10.3 %copy-start.26 = (f32[4,1120,128]{2,1,0:T(8,128)S(1)}, f32[4,1120,128]{2,1,0:T(8,128)}, u32[]{:S(2)}) copy-start(f32[4,1120,128]{2,1,0:T(8,128)} %get-tuple-element.91) | copy-start | bytes 6881284
  252.1 328.4 %all-reduce.6.cloned.1.call-start = ((), (), s32[]{:S(2)}) async-start(), calls=%async_computation | async-start | bytes 5160960 | tf_op jit(solution)/shard_map/psum | solution.py:650
  252.3 5.1 collective-permute-start.19
  255.0 6.4 %collective-permute-start.25 = (bf16[280,1024]{1,0:T(8,128)(2,1)}, bf16[280,1024]{1,0:T(8,128)(2,1)S(1)}, u32[]{:S(2)}, u32[]{:S(2)}) collective-permute-start(bf16[280,1024]{1,0:T(8,128)(2,1)} %copy-done.15), channel_id=1, source_target_pairs={{0,1},{1,0},{2,3},{3,2},{4,5},{5,4},{6,7},{7,6},{8,9},{9,8},{10,11... | collective-permute-start | bytes 1720328 | tf_op jit(solution)/shard_map/ppermute | solution.py:533
  257.4 6.1 %collective-permute-start.34 = (bf16[1120,256]{1,0:T(8,128)(2,1)S(1)}, bf16[1120,256]{1,0:T(8,128)(2,1)S(1)}, u32[]{:S(2)}, u32[]{:S(2)}) collective-permute-start(bf16[1120,256]{1,0:T(8,128)(2,1)S(1)} %copy-done.31), channel_id=1, source_target_pairs={{0,1},{1,0},{2,3},{3,2},{4,5},{5,4},{6,7},{7,6},{8,9},{9,8},{10,11... | collective-permute-start | bytes 1720328 | tf_op jit(solution)/shard_map/ppermute | solution.py:533
  259.8 18.9 %collective-permute-start.24 = (bf16[280,1024]{1,0:T(8,128)(2,1)S(1)}, bf16[280,1024]{1,0:T(8,128)(2,1)S(1)}, u32[]{:S(2)}, u32[]{:S(2)}) collective-permute-start(bf16[280,1024]{1,0:T(8,128)(2,1)S(1)} %copy-done.14), channel_id=1, source_target_pairs={{0,1},{1,0},{2,3},{3,2},{4,5},{5,4},{6,7},{7,6},{8,9},{9,8},{10,11... | collective-permute-start | bytes 1720328 | tf_op jit(solution)/shard_map/ppermute | solution.py:533
  261.4 15.9 %collective-permute-start.23 = (bf16[280,1024]{1,0:T(8,128)(2,1)S(1)}, bf16[280,1024]{1,0:T(8,128)(2,1)S(1)}, u32[]{:S(2)}, u32[]{:S(2)}) collective-permute-start(bf16[280,1024]{1,0:T(8,128)(2,1)S(1)} %add_convert_fusion.5), channel_id=1, source_target_pairs={{0,2},{1,3},{2,0},{3,1},{4,6},{5,7},{6,4},{7,5},{8,10},{9,11},{10,... | collective-permute-start | bytes 1720328 | tf_op jit(solution)/shard_map/ppermute | solution.py:533
  263.5 26.1 %collective-permute-start.26 = (bf16[280,1024]{1,0:T(8,128)(2,1)S(1)}, bf16[280,1024]{1,0:T(8,128)(2,1)S(1)}, u32[]{:S(2)}, u32[]{:S(2)}) collective-permute-start(bf16[280,1024]{1,0:T(8,128)(2,1)S(1)} %add_convert_fusion.3), channel_id=1, source_target_pairs={{0,2},{1,3},{2,0},{3,1},{4,6},{5,7},{6,4},{7,5},{8,10},{9,11},{10,... | collective-permute-start | bytes 1720328 | tf_op jit(solution)/shard_map/ppermute | solution.py:533
  265.8 70.6 %collective-permute-start.30 = (bf16[1120,256]{1,0:T(8,128)(2,1)}, bf16[1120,256]{1,0:T(8,128)(2,1)}, u32[]{:S(2)}, u32[]{:S(2)}) collective-permute-start(bf16[1120,256]{1,0:T(8,128)(2,1)} %get-tuple-element.126), channel_id=1, source_target_pairs={{0,1},{1,0},{2,3},{3,2},{4,5},{5,4},{6,7},{7,6},{8,9},{9,8},{10,11... | collective-permute-start | bytes 1720328 | tf_op jit(solution)/shard_map/ppermute | solution.py:533
  277.3 61.4 %collective-permute-start.33 = (bf16[1120,256]{1,0:T(8,128)(2,1)}, bf16[1120,256]{1,0:T(8,128)(2,1)}, u32[]{:S(2)}, u32[]{:S(2)}) collective-permute-start(bf16[1120,256]{1,0:T(8,128)(2,1)} %get-tuple-element.128), channel_id=1, source_target_pairs={{0,1},{1,0},{2,3},{3,2},{4,5},{5,4},{6,7},{7,6},{8,9},{9,8},{10,11... | collective-permute-start | bytes 1720328 | tf_op jit(solution)/shard_map/ppermute | solution.py:533
  278.7 188.5 %collective-permute-start.17 = (bf16[1120,256]{1,0:T(8,128)(2,1)}, bf16[1120,256]{1,0:T(8,128)(2,1)}, u32[]{:S(2)}, u32[]{:S(2)}) collective-permute-start(bf16[1120,256]{1,0:T(8,128)(2,1)} %fusion.10), channel_id=1, source_target_pairs={{0,2},{1,3},{2,0},{3,1},{4,6},{5,7},{6,4},{7,5},{8,10},{9,11},{10,... | collective-permute-start | bytes 1720328 | tf_op jit(solution)/shard_map/ppermute | solution.py:533
  289.6 47.5 %collective-permute-start.32 = (bf16[1120,256]{1,0:T(8,128)(2,1)}, bf16[1120,256]{1,0:T(8,128)(2,1)}, u32[]{:S(2)}, u32[]{:S(2)}) collective-permute-start(bf16[1120,256]{1,0:T(8,128)(2,1)} %fusion.6), channel_id=1, source_target_pairs={{0,2},{1,3},{2,0},{3,1},{4,6},{5,7},{6,4},{7,5},{8,10},{9,11},{10,... | collective-permute-start | bytes 1720328 | tf_op jit(solution)/shard_map/ppermute | solution.py:533
  293.4 20.9 %copy-start.4 = (bf16[840,1120]{0,1:T(8,128)(2,1)S(1)}, bf16[840,1120]{0,1:T(8,128)(2,1)}, u32[]{:S(2)}) copy-start(bf16[840,1120]{0,1:T(8,128)(2,1)} %copy.90) | copy-start | bytes 5644804
  336.4 14.1 %collective-permute-start.35 = (bf16[1120,256]{1,0:T(8,128)(2,1)S(1)}, bf16[1120,256]{1,0:T(8,128)(2,1)S(1)}, u32[]{:S(2)}, u32[]{:S(2)}) collective-permute-start(bf16[1120,256]{1,0:T(8,128)(2,1)S(1)} %copy-done.33), channel_id=1, source_target_pairs={{0,2},{1,3},{2,0},{3,1},{4,6},{5,7},{6,4},{7,5},{8,10},{9,11},{10,... | collective-permute-start | bytes 1720328 | tf_op jit(solution)/shard_map/ppermute | solution.py:533
  338.7 14.3 %copy-start.21 = (f32[1120,256]{1,0:T(8,128)}, f32[1120,256]{1,0:T(8,128)S(1)}, u32[]{:S(2)}) copy-start(f32[1120,256]{1,0:T(8,128)S(1)} %fusion.7) | copy-start | bytes 3440644
  360.7 91.3 %collective-permute-start.36 = (bf16[280,1120]{1,0:T(8,128)(2,1)}, bf16[280,1120]{1,0:T(8,128)(2,1)}, u32[]{:S(2)}, u32[]{:S(2)}) collective-permute-start(bf16[280,1120]{1,0:T(8,128)(2,1)} %get-tuple-element.96), channel_id=1, source_target_pairs={{0,1},{1,0},{2,3},{3,2},{4,5},{5,4},{6,7},{7,6},{8,9},{9,8},{10,11... | collective-permute-start | bytes 1881608 | tf_op jit(solution)/shard_map/ppermute | solution.py:533
  360.7 84.0 %collective-permute-start.37 = (bf16[280,1120]{1,0:T(8,128)(2,1)}, bf16[280,1120]{1,0:T(8,128)(2,1)}, u32[]{:S(2)}, u32[]{:S(2)}) collective-permute-start(bf16[280,1120]{1,0:T(8,128)(2,1)} %get-tuple-element.98), channel_id=1, source_target_pairs={{0,1},{1,0},{2,3},{3,2},{4,5},{5,4},{6,7},{7,6},{8,9},{9,8},{10,11... | collective-permute-start | bytes 1881608 | tf_op jit(solution)/shard_map/ppermute | solution.py:533
  364.3 104.4 %collective-permute-start.28 = (bf16[1120,512]{1,0:T(8,128)(2,1)}, bf16[1120,512]{1,0:T(8,128)(2,1)}, u32[]{:S(2)}, u32[]{:S(2)}) collective-permute-start(bf16[1120,512]{1,0:T(8,128)(2,1)} %get-tuple-element.124), channel_id=1, source_target_pairs={{0,1},{1,0},{2,3},{3,2},{4,5},{5,4},{6,7},{7,6},{8,9},{9,8},{10,11... | collective-permute-start | bytes 3440648 | tf_op jit(solution)/shard_map/ppermute | solution.py:533
  446.1 16.1 %collective-permute-start.38 = (bf16[280,1120]{1,0:T(8,128)(2,1)S(1)}, bf16[280,1120]{1,0:T(8,128)(2,1)S(1)}, u32[]{:S(2)}, u32[]{:S(2)}) collective-permute-start(bf16[280,1120]{1,0:T(8,128)(2,1)S(1)} %add_convert_fusion.1), channel_id=1, source_target_pairs={{0,2},{1,3},{2,0},{3,1},{4,6},{5,7},{6,4},{7,5},{8,10},{9,11},{10,... | collective-permute-start | bytes 1881608 | tf_op jit(solution)/shard_map/ppermute | solution.py:533
  451.9 16.8 %collective-permute-start.27 = (bf16[1120,512]{1,0:T(8,128)(2,1)S(1)}, bf16[1120,512]{1,0:T(8,128)(2,1)}, u32[]{:S(2)}, u32[]{:S(2)}) collective-permute-start(bf16[1120,512]{1,0:T(8,128)(2,1)S(1)} %copy-done.29), channel_id=1, source_target_pairs={{0,1},{1,0},{2,3},{3,2},{4,5},{5,4},{6,7},{7,6},{8,9},{9,8},{10,11... | collective-permute-start | bytes 3440648 | tf_op jit(solution)/shard_map/ppermute | solution.py:533
  462.2 10.8 %collective-permute-start.18 = (bf16[1120,256]{1,0:T(8,128)(2,1)}, bf16[1120,256]{1,0:T(8,128)(2,1)}, u32[]{:S(2)}, u32[]{:S(2)}) collective-permute-start(bf16[1120,256]{1,0:T(8,128)(2,1)} %get-tuple-element.132), channel_id=1, source_target_pairs={{0,1},{1,0},{2,3},{3,2},{4,5},{5,4},{6,7},{7,6},{8,9},{9,8},{10,11... | collective-permute-start | bytes 1720328 | tf_op jit(solution)/shard_map/ppermute | solution.py:533
  465.4 15.8 %collective-permute-start.20 = (bf16[1120,256]{1,0:T(8,128)(2,1)S(1)}, bf16[1120,256]{1,0:T(8,128)(2,1)S(1)}, u32[]{:S(2)}, u32[]{:S(2)}) collective-permute-start(bf16[1120,256]{1,0:T(8,128)(2,1)S(1)} %copy-done.32), channel_id=1, source_target_pairs={{0,2},{1,3},{2,0},{3,1},{4,6},{5,7},{6,4},{7,5},{8,10},{9,11},{10,... | collective-permute-start | bytes 1720328 | tf_op jit(solution)/shard_map/ppermute | solution.py:533
  472.3 10.3 %copy-start.6 = (f32[1120,256]{1,0:T(8,128)S(1)}, f32[1120,256]{1,0:T(8,128)}, u32[]{:S(2)}) copy-start(f32[1120,256]{1,0:T(8,128)} %copy-done.5) | copy-start | bytes 3440644
  472.3 10.3 %copy-start.34 = (f32[1120]{0:T(1024)S(1)}, f32[1120]{0:T(1024)}, u32[]{:S(2)}) copy-start(f32[1120]{0:T(1024)} %param.29) | copy-start | bytes 13444
  472.3 33.0 %collective-permute-start.29 = (bf16[1120,512]{1,0:T(8,128)(2,1)S(1)}, bf16[1120,512]{1,0:T(8,128)(2,1)S(1)}, u32[]{:S(2)}, u32[]{:S(2)}) collective-permute-start(bf16[1120,512]{1,0:T(8,128)(2,1)S(1)} %get-tuple-element.122), channel_id=1, source_target_pairs={{0,2},{1,3},{2,0},{3,1},{4,6},{5,7},{6,4},{7,5},{8,10},{9,11},{10,... | collective-permute-start | bytes 3440648 | tf_op jit(solution)/shard_map/ppermute | solution.py:533
  482.6 22.8 %copy-start.9 = (bf16[512,1120]{0,1:T(8,128)(2,1)S(1)}, bf16[512,1120]{0,1:T(8,128)(2,1)}, u32[]{:S(2)}) copy-start(bf16[512,1120]{0,1:T(8,128)(2,1)} %param.16) | copy-start | bytes 3440644
  (38 other events, 202.0 us)
Sparse Core Ops, SparseCore 0:
  252.2 186.3 all-reduce.7
  464.5 115.9 all-reduce.5

commit v2 on v1

v2 whole, which is shorter than its diff:
```python
import functools
import math

import jax
import jax.numpy as jnp
from jax import lax
from jax.experimental import pallas as pl
from jax.experimental.pallas import tpu as pltpu
from jax.sharding import PartitionSpec as P


HEAD_DIM = 56
BLK = 256
SLOTS = 4
NEG = -1e30
EPS = 1e-05
SCALE = 1.0 / math.sqrt(HEAD_DIM)
SCALE2 = SCALE * math.log2(math.e)
GELU_C = math.sqrt(2.0 / math.pi)
GELU_A = 0.044715
F32 = jnp.float32
BF16 = jnp.bfloat16
NT = ((1,), (1,))
ROWS = 224
GAIN1, SHIFT1, OUT_BIAS, GAIN2, SHIFT2, UP_BIAS, DOWN_BIAS = range(7)
VEC8 = True
ATT_PIECES = True
VMEM = 60 << 20
PACE = 2.3e9


def dot(a, b, dims=((1,), (0,))):
    return lax.dot_general(a, b, (dims, ((), ())), preferred_element_type=F32)


def params():
    return pltpu.CompilerParams(vmem_limit_bytes=VMEM)


def cost(microseconds):
    return pl.CostEstimate(flops=int(microseconds * PACE), bytes_accessed=1, transcendentals=0)


def fold(v):
    total = v[:, :128]
    for at in range(128, v.shape[1], 128):
        total = total + v[:, at : at + 128]
    return total


def normal(x):
    center = x - jnp.mean(x, axis=0, keepdims=True)
    root = lax.rsqrt(jnp.mean(center * center, axis=0, keepdims=True) + EPS)
    return center * root, root


def turn_kernel(count, parts, *refs):
    for n in range(count):
        refs[count + 1 + n][...] = refs[n][...].T
    for n in range(parts):
        refs[2 * count + 1 + n][...] = refs[count][:, n * BLK : (n + 1) * BLK]


def turn(cut, *arrays):
    wide = max(a.shape[1] for a in arrays)
    steps = -(-wide // 256)
    in_specs, out_specs, outs = [], [], []
    for a in arrays:
        rows, columns = a.shape
        if columns == wide:
            in_specs.append(pl.BlockSpec((rows, 256), lambda i: (0, i)))
            out_specs.append(pl.BlockSpec((256, rows), lambda i: (i, 0)))
        else:
            in_specs.append(pl.BlockSpec((rows, columns), lambda i: (0, 0)))
            out_specs.append(pl.BlockSpec((columns, rows), lambda i: (0, 0)))
        outs.append(jax.ShapeDtypeStruct((columns, rows), a.dtype))
    rows, columns = cut.shape
    parts = columns // BLK
    size = -(-rows // (16 * steps)) * 16
    in_specs.append(pl.BlockSpec((size, columns), lambda i: (i, 0)))
    out_specs += [pl.BlockSpec((size, BLK), lambda i: (i, 0))] * parts
    outs += [jax.ShapeDtypeStruct((rows, BLK), cut.dtype)] * parts
    return pl.pallas_call(
        functools.partial(turn_kernel, len(arrays), parts),
        grid=(steps,),
        in_specs=in_specs,
        out_specs=out_specs,
        out_shape=outs,
        compiler_params=params(),
        cost_estimate=cost(8),
        name="turn",
    )(*arrays, cut)


def turn_pieces_kernel(*refs):
    refs[-1][...] = jnp.concatenate([ref[...] for ref in refs[:-1]], 0).T


def turn_pieces(*pieces):
    rows, columns = pieces[0].shape
    return pl.pallas_call(
        turn_pieces_kernel,
        grid=(-(-columns // 256),),
        in_specs=[pl.BlockSpec((rows, 256), lambda i: (0, i))] * len(pieces),
        out_specs=pl.BlockSpec((256, rows * len(pieces)), lambda i: (i, 0)),
        out_shape=jax.ShapeDtypeStruct((columns, rows * len(pieces)), pieces[0].dtype),
        compiler_params=params(),
        cost_estimate=cost(5),
        name="turn_pieces",
    )(*pieces)


def col(ref, at, m):
    return ref[m, at : at + 1]


def cuts(total, size):
    return [slice(at, min(at + size, total)) for at in range(0, total, size)]


def qkv_kernel(heads, a_ref, b_ref, w_ref, vec_ref, bias_ref, *rest):
    x_out, h_out, q_out, kn_out, vn_out = rest[-5:]
    x_out[:, :BLK] = a_ref[...]
    x_out[:, BLK:] = b_ref[...]
    d = x_out.shape[0]
    pieces = cuts(d, ROWS)
    total = 0.0
    for m in pieces:
        total = total + jnp.sum(x_out[m].astype(F32), axis=0, keepdims=True)
    mean = total * (1.0 / d)
    total = 0.0
    for m in pieces:
        center = x_out[m].astype(F32) - mean
        total = total + jnp.sum(center * center, axis=0, keepdims=True)
    root = lax.rsqrt(total * (1.0 / d) + EPS)
    for m in pieces:
        n = (x_out[m].astype(F32) - mean) * root
        h_out[m] = (n * col(vec_ref, GAIN1, m) + col(vec_ref, SHIFT1, m)).astype(BF16)
    h = h_out[...]
    for part in range(3):
        r = (dot(w_ref[part], h) + bias_ref[:, part : part + 1]).astype(BF16)
        r = r.reshape(heads, HEAD_DIM, r.shape[1])
        q_out[part * heads : (part + 1) * heads] = r
        if part > 0:
            out = kn_out if part == 1 else vn_out
            for h_at in range(heads):
                out[h_at] = r[h_at].T


def qkv_call(pair, a, b, w, vec, bias, carry):
    d, rows = a.shape
    per = rows // BLK
    total = rows * SLOTS
    heads = w.shape[1] // HEAD_DIM
    wide = 2 * BLK
    outs = [
        jax.ShapeDtypeStruct((d, total), BF16),
        jax.ShapeDtypeStruct((d, total), BF16),
        jax.ShapeDtypeStruct((3 * heads, HEAD_DIM, total), BF16),
        jax.ShapeDtypeStruct((heads, total, HEAD_DIM), BF16),
        jax.ShapeDtypeStruct((heads, total, HEAD_DIM), BF16),
    ]
    at = lambda p: p * (SLOTS // 2) + pair
    in_specs = [
        pl.BlockSpec((d, BLK), lambda p: (0, p)),
        pl.BlockSpec((d, BLK), lambda p: (0, p)),
        pl.BlockSpec(w.shape, lambda p: (0, 0, 0)),
        pl.BlockSpec(vec.shape, lambda p: (0, 0)),
        pl.BlockSpec(bias.shape, lambda p: (0, 0)),
    ]
    args = [a, b, w, vec, bias]
    alias = {}
    if carry is not None:
        alias = {len(args) + n: n for n in range(len(outs))}
        in_specs += [pl.BlockSpec(memory_space=pl.ANY)] * len(outs)
        args += list(carry)
    return pl.pallas_call(
        functools.partial(qkv_kernel, heads),
        grid=(per,),
        in_specs=in_specs,
        out_specs=[
            pl.BlockSpec((d, wide), lambda p: (0, at(p))),
            pl.BlockSpec((d, wide), lambda p: (0, at(p))),
            pl.BlockSpec((3 * heads, HEAD_DIM, wide), lambda p: (0, 0, at(p))),
            pl.BlockSpec((heads, wide, HEAD_DIM), lambda p: (0, at(p), 0)),
            pl.BlockSpec((heads, wide, HEAD_DIM), lambda p: (0, at(p), 0)),
        ],
        out_shape=outs,
        input_output_aliases=alias,
        compiler_params=params(),
        cost_estimate=cost(8),
        name="qkv_call",
    )(*args)


def attend_kernel(heads, nb, per, chunk, info, start_ref, q_ref, kn_ref, v_ref, o_ref, lse_ref, acc, m_s, l_s):
    b = pl.program_id(0) * per + chunk

    def visit(kb, diag):
        at = pl.multiple_of(info[nb + kb] * BLK, BLK)
        kpos = lax.broadcasted_iota(jnp.int32, (BLK, BLK), 0)
        ok = kpos >= (start_ref[...] - kb * BLK)
        if diag:
            ok = ok & (kpos <= lax.broadcasted_iota(jnp.int32, (BLK, BLK), 1))
        scores = [dot(kn_ref[h, pl.ds(at, BLK), :], q_ref[h]) for h in range(heads)]
        scores = [jnp.where(ok, s, NEG) for s in scores]
        top = jnp.concatenate([jnp.max(s, axis=0, keepdims=True) for s in scores], 0)
        if not diag:
            old = m_s[0:heads, :]
            top = jnp.maximum(old, top)
            fade = jnp.exp2((old - top) * SCALE2)
        m_s[0:heads, :] = top
        expo = [jnp.exp2((scores[h] - top[h : h + 1]) * SCALE2) for h in range(heads)]
        sums = jnp.concatenate([jnp.sum(e, axis=0, keepdims=True) for e in expo], 0)
        l_s[0:heads, :] = sums if diag else l_s[0:heads, :] * fade + sums
        for h in range(heads):
            new = dot(v_ref[h, :, pl.ds(at, BLK)], expo[h].astype(BF16))
            acc[h] = new if diag else acc[h] * fade[h : h + 1] + new

    visit(b, True)

    def step(kb, _):
        visit(kb, False)
        return 0

    lax.fori_loop(info[b], b, step, 0)
    for h in range(heads):
        total = l_s[h : h + 1, :]
        o_ref[h] = (acc[h] * (1.0 / total)).astype(BF16)
        lse_ref[h : h + 1, :] = m_s[h : h + 1, :] * SCALE2 + jnp.log2(total)


def attend(chunk, info, start, qkv, kn):
    heads, total = qkv.shape[0] // 3, qkv.shape[2]
    nb = total // BLK
    per = nb // SLOTS
    spec = pltpu.PrefetchScalarGridSpec(
        num_scalar_prefetch=1,
        grid=(SLOTS,),
        in_specs=[
            pl.BlockSpec((1, BLK), lambda i, s: (0, i * per + chunk)),
            pl.BlockSpec((heads, HEAD_DIM, BLK), lambda i, s: (0, 0, s[nb + i * per + chunk])),
            pl.BlockSpec((heads, total, HEAD_DIM), lambda i, s: (0, 0, 0)),
            pl.BlockSpec((heads, HEAD_DIM, total), lambda i, s: (2, 0, 0)),
        ],
        out_specs=[
            pl.BlockSpec((heads, HEAD_DIM, BLK), lambda i, s: (0, 0, i)),
            pl.BlockSpec((8, BLK), lambda i, s: (0, i)),
        ],
        scratch_shapes=[
            pltpu.VMEM((heads, HEAD_DIM, BLK), F32),
            pltpu.VMEM((8, BLK), F32),
            pltpu.VMEM((8, BLK), F32),
        ],
    )
    return pl.pallas_call(
        functools.partial(attend_kernel, heads, nb, per, chunk),
        grid_spec=spec,
        out_shape=[
            jax.ShapeDtypeStruct((heads, HEAD_DIM, SLOTS * BLK), BF16),
            jax.ShapeDtypeStruct((8, SLOTS * BLK), F32),
        ],
        compiler_params=params(),
        cost_estimate=cost(9.5),
        name="attend",
    )(info, start, qkv, kn, qkv)


def attend_back_kernel(heads, nb, per, info, start_ref, q_ref, k_ref, kn_ref, vn_ref, do_ref, stat_ref, out_ref, dq_s, dk_s, dv_s):
    j = pl.program_id(0)

    def place(b):
        return pl.multiple_of(info[nb + b] * BLK, BLK)

    def ordered(b):
        return pl.multiple_of(((b % per) * SLOTS + b // per) * BLK, BLK)

    @pl.when(j == 0)
    def _():
        dq_s[...] = jnp.zeros_like(dq_s)

    def visit(b, diag):
        at = place(b)
        mine = ordered(b)
        kpos = lax.broadcasted_iota(jnp.int32, (BLK, BLK), 0)
        ok = kpos >= (start_ref[:, pl.ds(pl.multiple_of(b * BLK, BLK), BLK)] - j * BLK)
        if diag:
            ok = ok & (kpos <= lax.broadcasted_iota(jnp.int32, (BLK, BLK), 1))
        every = range(heads)
        query = [q_ref[h, :, pl.ds(at, BLK)] for h in every]
        grad = [do_ref[h, :, pl.ds(mine, BLK)] for h in every]
        scores = [dot(kn_ref[h], query[h]) for h in every]
        prob_grad = [dot(vn_ref[h], grad[h]) for h in every]
        probs = [
            jnp.where(ok, jnp.exp2(scores[h] * SCALE2 - stat_ref[h : h + 1, pl.ds(mine, BLK)]), 0.0) for h in every
        ]
        score_grad = [
            (probs[h] * (prob_grad[h] - stat_ref[8 + h : 9 + h, pl.ds(mine, BLK)])).astype(BF16) for h in every
        ]
        dv = [dot(grad[h], probs[h].astype(BF16), NT) for h in every]
        dk = [dot(query[h], score_grad[h], NT) for h in every]
        dq = [dot(k_ref[h], score_grad[h]) for h in every]
        for h in every:
            if diag:
                dv_s[h] = dv[h]
                dk_s[h] = dk[h]
            else:
                dv_s[h] += dv[h]
                dk_s[h] += dk[h]
            dq_s[h, :, pl.ds(at, BLK)] += dq[h]

    visit(j, True)

    def step(b, _):
        visit(b, False)
        return 0

    lax.fori_loop(j + 1, info[2 * nb + j] + 1, step, 0)
    at = place(j)
    for h in range(heads):
        out_ref[h] = (dq_s[h, :, pl.ds(at, BLK)] * SCALE).astype(BF16)
        out_ref[heads + h] = (dk_s[h] * SCALE).astype(BF16)
        out_ref[2 * heads + h] = dv_s[h].astype(BF16)


def attend_back(info, start, qkv, kn, vn, do, stat):
    heads, total = qkv.shape[0] // 3, qkv.shape[2]
    nb = total // BLK
    per = nb // SLOTS
    whole = pl.BlockSpec((heads, HEAD_DIM, total), lambda j, s: (0, 0, 0))
    block = lambda a: pl.BlockSpec((heads, HEAD_DIM, BLK), lambda j, s: (a, 0, s[nb + j]))
    tall = pl.BlockSpec((heads, BLK, HEAD_DIM), lambda j, s: (0, s[nb + j], 0))
    spec = pltpu.PrefetchScalarGridSpec(
        num_scalar_prefetch=1,
        grid=(nb,),
        in_specs=[
            pl.BlockSpec((1, total), lambda j, s: (0, 0)),
            whole,
            block(1),
            tall,
            tall,
            whole,
            pl.BlockSpec((16, total), lambda j, s: (0, 0)),
        ],
        out_specs=pl.BlockSpec((3 * heads, HEAD_DIM, BLK), lambda j, s: (0, 0, s[nb + j])),
        scratch_shapes=[
            pltpu.VMEM((heads, HEAD_DIM, total), F32),
            pltpu.VMEM((heads, HEAD_DIM, BLK), F32),
            pltpu.VMEM((heads, HEAD_DIM, BLK), F32),
        ],
    )
    return pl.pallas_call(
        functools.partial(attend_back_kernel, heads, nb, per),
        grid_spec=spec,
        out_shape=jax.ShapeDtypeStruct((3 * heads, HEAD_DIM, total), BF16),
        compiler_params=params(),
        cost_estimate=cost(20),
        name="attend_back",
    )(info, start, qkv, qkv, kn, vn, do, stat)


def join_kernel(chunks, *refs):
    do_out, stat_out = refs[-2:]
    h = pl.program_id(0)
    wide = SLOTS * BLK
    for c in range(chunks):
        a, near, far, o, lse = refs[5 * c : 5 * c + 5]
        cut = slice(c * wide, (c + 1) * wide)
        do = (a[0].astype(F32) + near[0, 0].astype(F32) + far[0].astype(F32)).astype(BF16)
        do_out[0, :, cut] = do
        stat_out[pl.ds(h + 8, 1), cut] = jnp.sum(o[0].astype(F32) * do.astype(F32), axis=0, keepdims=True)

        @pl.when(h == 0)
        def _():
            stat_out[0:8, cut] = lse[...]


def join(parts):
    heads, _, wide = parts[0][3].shape
    total = wide * len(parts)
    in_specs, args = [], []
    block = pl.BlockSpec((1, HEAD_DIM, wide), lambda h: (h, 0, 0))
    for a, near, far, o, lse in parts:
        args += [
            a.reshape(heads, HEAD_DIM, wide),
            near.reshape(2, heads, HEAD_DIM, wide),
            far.reshape(heads, HEAD_DIM, wide),
            o,
            lse,
        ]
        in_specs += [
            block,
            pl.BlockSpec((1, 1, HEAD_DIM, wide), lambda h: (0, h, 0, 0)),
            block,
            block,
            pl.BlockSpec((8, wide), lambda h: (0, 0)),
        ]
    return pl.pallas_call(
        functools.partial(join_kernel, len(parts)),
        grid=(heads,),
        in_specs=in_specs,
        out_specs=[pl.BlockSpec((1, HEAD_DIM, total), lambda h: (h, 0, 0)), pl.BlockSpec((16, total), lambda h: (0, 0))],
        out_shape=[jax.ShapeDtypeStruct((heads, HEAD_DIM, total), BF16), jax.ShapeDtypeStruct((16, total), F32)],
        compiler_params=params(),
        cost_estimate=cost(5),
        name="join",
    )(*args)


def to_slot(s, value_ref, outs):
    places = (outs[0], outs[2].at[0], outs[1], outs[2].at[1])
    for k in range(SLOTS):

        @pl.when(s == k)
        def _():
            places[k][...] = value_ref[...]


def add_to(first, ref, at, m, part):
    ref[at, m] = jnp.where(first, part, ref[at, m] + part)


def forward_kernel(info, x_ref, *refs):
    att_refs, refs = refs[:SLOTS], refs[SLOTS:]
    g_refs = refs[:SLOTS]
    wot, upt, wd, wdt, vec_ref = refs[SLOTS : SLOTS + 5]
    h_out, act_out, pg_out, g_out, n_out, root_out, sum_out, own_out = refs[-13:-5]
    layer_outs = refs[-5:-2]
    y1_s, layer_s = refs[-2:]
    s = pl.program_id(0)
    for k in range(SLOTS):

        @pl.when(s == k)
        def _():
            g_out[...] = g_refs[k][...]

    d = x_ref.shape[0]
    pieces = cuts(d, ROWS)
    att = jnp.concatenate([ref[...] for ref in att_refs], 0)
    total = 0.0
    for m in pieces:
        y1 = x_ref[m].astype(F32) + (dot(wot[m], att) + col(vec_ref, OUT_BIAS, m))
        y1_s[m] = y1
        total = total + jnp.sum(y1, axis=0, keepdims=True)
    mean = total * (1.0 / d)
    total = 0.0
    for m in pieces:
        center = y1_s[m] - mean
        total = total + jnp.sum(center * center, axis=0, keepdims=True)
    root = lax.rsqrt(total * (1.0 / d) + EPS)
    root_out[...] = jnp.broadcast_to(root, root_out.shape)
    for m in pieces:
        n = (y1_s[m] - mean) * root
        n_out[m] = n.astype(BF16)
        h_out[m] = (n * col(vec_ref, GAIN2, m) + col(vec_ref, SHIFT2, m)).astype(BF16)
    h = h_out[...]
    g = g_out[...]
    for m in cuts(upt.shape[0], ROWS):
        pre = dot(upt[m], h) + col(vec_ref, UP_BIAS, m)
        act_grad = dot(wd[m], g)
        square = pre * pre
        t = jnp.tanh(pre * (GELU_C + (GELU_C * GELU_A) * square))
        half = 0.5 * (1.0 + t)
        act_out[m] = (pre * half).astype(BF16)
        slope = half + (0.5 * pre) * (1.0 - t * t) * (GELU_C + (3.0 * GELU_C * GELU_A) * square)
        pg = (act_grad * slope).astype(BF16)
        pg_out[m] = pg
        add_to(s == 0, sum_out, 0, m, fold(pg.astype(F32)))
    act = act_out[...]
    for m in pieces:
        layer_s[m] = dot(wdt[m], act).astype(BF16)
    to_slot(s, layer_s, layer_outs)

    @pl.when(s == 0)
    def _():
        own_out[...] = y1_s[...]


def forward(chunk, info, atts, x, gs, wot, upt, wd, wdt, vec, carry):
    d, total = x.shape
    f = upt.shape[0]
    wide = SLOTS * BLK
    dev = 3 * (total // BLK)
    keep = lambda a: pl.BlockSpec(a.shape, lambda s, i: (0,) * a.ndim, pipeline_mode=pl.Buffered(1))
    block = lambda r: pl.BlockSpec((r, BLK), lambda s, i: (0, s))
    mine = pl.BlockSpec((d, BLK), lambda s, i: (0, chunk))
    args = [info, x, *atts, *gs, wot, upt, wd, wdt, vec]
    in_specs = [pl.BlockSpec((d, BLK), lambda s, i: (0, chunk * SLOTS + s))]
    in_specs += [pl.BlockSpec((atts[0].shape[0], BLK), lambda s, i: (0, s ^ i[dev]))] * SLOTS
    in_specs += [pl.BlockSpec((d, BLK), lambda s, i: (0, 0))] * SLOTS + [keep(a) for a in (wot, upt, wd, wdt, vec)]
    alias = {}
    if carry is not None:
        alias = {len(args) + n: 7 + n for n in range(len(carry))}
        in_specs += [pl.BlockSpec(memory_space=pl.ANY)] * len(carry)
        args += list(carry)
    spec = pltpu.PrefetchScalarGridSpec(
        num_scalar_prefetch=1,
        grid=(SLOTS,),
        in_specs=in_specs,
        out_specs=[
            block(d),
            block(f),
            block(f),
            block(d),
            block(d),
            block(8),
            pl.BlockSpec((1, f, 128), lambda s, i: (0, 0, 0)),
            mine,
            mine,
            mine,
            pl.BlockSpec((2, d, BLK), lambda s, i: (0, 0, chunk)),
        ],
        scratch_shapes=[pltpu.VMEM((d, BLK), F32), pltpu.VMEM((d, BLK), BF16)],
    )
    shape = jax.ShapeDtypeStruct
    rows = total // SLOTS
    return pl.pallas_call(
        forward_kernel,
        grid_spec=spec,
        out_shape=[
            shape((d, wide), BF16),
            shape((f, wide), BF16),
            shape((f, wide), BF16),
            shape((d, wide), BF16),
            shape((d, wide), BF16),
            shape((8, wide), F32),
            shape((1, f, 128), F32),
            shape((d, rows), F32),
            shape((d, rows), BF16),
            shape((d, rows), BF16),
            shape((2, d, rows), BF16),
        ],
        input_output_aliases=alias,
        compiler_params=params(),
        cost_estimate=cost(26),
        name="forward",
    )(*args)


def backward_kernel(info, pg_ref, n_ref, root_ref, g_ref, up, *refs):
    wo = refs[:SLOTS]
    vec_ref = refs[SLOTS]
    sum_out, attg0_out, attg2_out, attg_side = refs[-9:-5]
    attg_outs = (attg0_out, attg_side.at[0], attg2_out, attg_side.at[1])
    y1g_outs = refs[-5:-2]
    e_s, y1g_s = refs[-2:]
    s = pl.program_id(0)
    d = n_ref.shape[0]
    pieces = cuts(d, ROWS)
    pg = pg_ref[...]
    mean = 0.0
    tilt = 0.0
    for m in pieces:
        hg = dot(up[m], pg)
        n = n_ref[m].astype(F32)
        hn = hg * n
        gain = col(vec_ref, GAIN2, m)
        e = hg * gain
        e_s[m] = e
        mean = mean + jnp.sum(e, axis=0, keepdims=True)
        tilt = tilt + jnp.sum(hn * gain, axis=0, keepdims=True)
        add_to(s == 0, sum_out, 0, m, fold(hn))
        add_to(s == 0, sum_out, 1, m, fold(hg))
    mean = mean * (1.0 / d)
    tilt = tilt * (1.0 / d)
    root = root_ref[0:1]
    mine = jnp.where(s == 0, 1.0, 0.0)
    for m in pieces:
        y1g = root * (e_s[m] - mean - n_ref[m].astype(F32) * tilt) + g_ref[m].astype(F32) * mine
        y1g_s[m] = y1g.astype(BF16)
        add_to(s == 0, sum_out, 2, m, fold(y1g))
    y1b = y1g_s[...]
    for k in range(SLOTS):
        attg_outs[k][...] = dot(wo[k][...], y1b).astype(BF16)
    to_slot(s, y1g_s, y1g_outs)


def backward(chunk, info, pg, n, root, g, up, wos, vec, carry):
    d, wide = n.shape
    f = up.shape[1]
    rows = wos[0].shape[0]
    dev = info.shape[0] - 1
    keep = lambda a: pl.BlockSpec(a.shape, lambda s, i: (0,) * a.ndim, pipeline_mode=pl.Buffered(1))
    block = lambda r: pl.BlockSpec((r, BLK), lambda s, i: (0, s))
    mine = pl.BlockSpec((d, BLK), lambda s, i: (0, chunk))
    ordered = pl.BlockSpec((rows, BLK), lambda s, i: (0, s ^ i[dev]))
    args = [info, pg, n, root, g, up, *wos, vec]
    in_specs = [block(f), block(d), block(8), mine] + [keep(a) for a in (up, *wos, vec)]
    alias = {}
    if carry is not None:
        alias = {len(args) + n: 4 + n for n in range(len(carry))}
        in_specs += [pl.BlockSpec(memory_space=pl.ANY)] * len(carry)
        args += list(carry)
    spec = pltpu.PrefetchScalarGridSpec(
        num_scalar_prefetch=1,
        grid=(SLOTS,),
        in_specs=in_specs,
        out_specs=[
            pl.BlockSpec((3, d, 128), lambda s, i: (0, 0, 0)),
            ordered,
            ordered,
            pl.BlockSpec((2, rows, BLK), lambda s, i: (0, 0, s ^ i[dev])),
            mine,
            mine,
            pl.BlockSpec((2, d, BLK), lambda s, i: (0, 0, chunk)),
        ],
        scratch_shapes=[pltpu.VMEM((d, BLK), F32), pltpu.VMEM((d, BLK), BF16)],
    )
    shape = jax.ShapeDtypeStruct
    return pl.pallas_call(
        backward_kernel,
        grid_spec=spec,
        out_shape=[
            shape((3, d, 128), F32),
            shape((rows, wide), BF16),
            shape((rows, wide), BF16),
            shape((2, rows, wide), BF16),
            shape((d, g.shape[1]), BF16),
            shape((d, g.shape[1]), BF16),
            shape((2, d, g.shape[1]), BF16),
        ],
        input_output_aliases=alias,
        compiler_params=params(),
        cost_estimate=cost(17),
        name="backward",
    )(*args)


def shard_rows(m):
    return -(-m // (8 * 16)) * 16


def outer_kernel(count, order, with_sum, info, *refs):
    dp = info[0]
    i = pl.program_id(0)
    outs = refs[2 * count :]
    total = None
    for n in range(count):
        part = dot(refs[2 * n][...], refs[2 * n + 1][...], NT)
        total = part if total is None else total + part
    size = total.shape[0] // 2
    for half in range(2):
        slot = (2 * i) ^ (dp & 1) ^ half
        at = jnp.where((slot & order[2]) != 0, 1, 0) + jnp.where((slot & order[1]) != 0, 2, 0)
        rows = pl.ds(pl.multiple_of(at * size, size), size)
        value = total[half * size : (half + 1) * size].astype(BF16)
        goes = (slot & order[0]) != 0

        @pl.when(goes)
        def _():
            outs[1][rows] = value

        @pl.when(jnp.logical_not(goes))
        def _():
            outs[0][rows] = value

    if with_sum:
        outs[2][...] = fold(refs[0][...].astype(F32))


def outer(pairs, info, order, first=0, rows=None, with_sum=False):
    m, depth = pairs[0][0].shape
    n = pairs[0][1].shape[0]
    rows = m if rows is None else rows
    size = shard_rows(rows)
    skip = first // (2 * size)
    in_specs, args = [], []
    for a, b in pairs:
        in_specs.append(pl.BlockSpec((2 * size, depth), lambda i, s: (skip + (i ^ (s[0] >> 1)), 0)))
        in_specs.append(pl.BlockSpec((n, depth), lambda i, s: (0, 0), pipeline_mode=pl.Buffered(1)))
        args += [a, b]
    out_specs = [pl.BlockSpec((4 * size, n), lambda i, s: (0, 0))] * 2
    out_shape = [jax.ShapeDtypeStruct((4 * size, n), BF16)] * 2
    if with_sum:
        out_specs.append(pl.BlockSpec((2 * size, 128), lambda i, s: (i ^ (s[0] >> 1), 0)))
        out_shape.append(jax.ShapeDtypeStruct((8 * size, 128), F32))
    return pl.pallas_call(
        functools.partial(outer_kernel, len(pairs), order, with_sum),
        grid_spec=pltpu.PrefetchScalarGridSpec(num_scalar_prefetch=1, grid=(4,), in_specs=in_specs, out_specs=out_specs),
        out_shape=out_shape,
        compiler_params=params(),
        cost_estimate=cost(11),
        name="outer",
    )(info, *args)


def halve_kernel(keep_ref, recv_ref, keep_out, send_out):
    i = pl.program_id(0)
    total = (keep_ref[...].astype(F32) + recv_ref[...].astype(F32)).astype(BF16)

    @pl.when(i == 0)
    def _():
        keep_out[...] = total

    @pl.when(i == 1)
    def _():
        send_out[...] = total


def halve(keep, recv):
    size, n = keep.shape[0] // 2, keep.shape[1]
    block = pl.BlockSpec((size, n), lambda i: (i, 0))
    return pl.pallas_call(
        halve_kernel,
        grid=(2,),
        in_specs=[block, block],
        out_specs=[pl.BlockSpec((size, n), lambda i: (0, 0))] * 2,
        out_shape=[jax.ShapeDtypeStruct((size, n), BF16)] * 2,
        compiler_params=params(),
        cost_estimate=cost(2.5),
        name="halve",
    )(keep, recv)


def slot_of(i, order):
    return jnp.where(i & 1, order[2], 0) | jnp.where(i & 2, order[1], 0) | jnp.where(i & 4, order[0], 0)


def place_kernel(info, one, two, four, eight, *rest):
    i = pl.program_id(0)
    out = rest[-1]
    for ref, low, high in ((one, 0, 1), (two, 1, 2), (four, 2, 4), (eight, 4, 8)):

        @pl.when((i >= low) & (i < high))
        def _():
            out[...] = ref[...].astype(F32)


def place(parts, info, order, first, rows, carry):
    size, n = parts[0].shape
    start = first // size
    near = lambda at, many: pl.BlockSpec((size, n), lambda i, s: (jnp.clip(i - at, 0, many - 1), 0))
    in_specs = [near(0, 1), near(1, 1), near(2, 2), near(4, 4)]
    args = list(parts)
    alias = {}
    if carry is not None:
        in_specs.append(pl.BlockSpec(memory_space=pl.ANY))
        args.append(carry)
        alias = {5: 0}
    spec = pltpu.PrefetchScalarGridSpec(
        num_scalar_prefetch=1,
        grid=(8,),
        in_specs=in_specs,
        out_specs=pl.BlockSpec((size, n), lambda i, s: (start + (slot_of(i, order) ^ s[0]), 0)),
    )
    return pl.pallas_call(
        place_kernel,
        grid_spec=spec,
        out_shape=jax.ShapeDtypeStruct((rows, n), F32),
        input_output_aliases=alias,
        compiler_params=params(),
        cost_estimate=cost(6.5),
        name="place",
    )(info, *args)


def swap_dp(v, k):
    return lax.ppermute(v, "dp", [(i, i ^ k) for i in range(8)])


class CellSum:
    def __init__(self, line, keep, send, info, order, rows, first=0):
        self.line, self.keep, self.info, self.order = line, keep, info, order
        self.rows, self.first = rows, first
        self.stage = 0
        self.known = lax.axis_size("dp") == 8
        if not self.known:
            both = lax.psum(jnp.stack([keep, send]), "dp")
            size = keep.shape[0] // 4
            self.parts = [both[0, :size], both[0, size : 2 * size], both[0, 2 * size :], both[1]]
            self.got = both[1]
            return
        self.got = swap_dp(send, order[0])

    def step(self):
        if not self.known:
            return
        self.stage += 1
        k1, k2, k3 = self.order
        if self.stage < 3:
            self.keep, send = self.line(halve, self.keep, self.got)
            self.got = swap_dp(send, k2 if self.stage == 1 else k3)
        elif self.stage == 3:
            self.parts = [self.line(lambda a, b: add(BF16, a, b), self.keep, self.got)]
            self.got = swap_dp(self.parts[0], k3)
        else:
            self.parts.append(self.got)
            self.got = swap_dp(self.line(stack, *self.parts), k2 if self.stage == 4 else k1)
            if self.stage == 5:
                self.parts.append(self.got)

    def finish(self, carry=None):
        return self.line(
            lambda p, *c: place(p, self.info, self.order, self.first, self.rows, *(c or (None,))),
            self.parts,
            *([] if carry is None else [carry]),
        )


class Rounds:
    def __init__(self, line, v, over_tensor=False):
        self.line, self.v = line, v
        self.todo = [(swap_dp, 1), (swap_dp, 2), (swap_dp, 4)]
        if lax.axis_size("dp") != 8:
            self.v = lax.psum(v.astype(F32), "dp").astype(v.dtype)
            self.todo = []
        self.cells = self.v
        if over_tensor:
            self.todo += [(swap, 1), (swap, 2)]
        self.send()

    def send(self):
        self.got = None
        if self.todo:
            self.move, k = self.todo.pop(0)
            self.got = self.move(self.v, k)

    def step(self):
        if self.got is None:
            return
        self.v = self.line(lambda a, b: add(a.dtype, a, b), self.v, self.got)
        if self.move is swap_dp:
            self.cells = self.v
        self.send()


def out_grad_kernel(count, info, *refs):
    atts, y1gs, outs = refs[: count * SLOTS], refs[count * SLOTS : count * (SLOTS + 1)], refs[count * (SLOTS + 1) :]
    for k in range(SLOTS):
        total = None
        for n in range(count):
            part = dot(atts[n * SLOTS + k][...], y1gs[n][...], NT)
            total = part if total is None else total + part
        (outs[0], outs[2].at[0], outs[1], outs[2].at[1])[k][...] = total.astype(BF16)


def out_grad_call(info, atts, y1g):
    rows = atts[0][0].shape[0]
    d = y1g.shape[0]
    count = len(atts)
    dev = info.shape[0] - 1
    in_specs = [pl.BlockSpec((rows, BLK), lambda i, s: (0, s[dev]))] * (count * SLOTS)
    in_specs += [pl.BlockSpec((d, BLK), functools.partial(lambda at, i, s: (0, at), n)) for n in range(count)]
    spec = pltpu.PrefetchScalarGridSpec(
        num_scalar_prefetch=1,
        grid=(1,),
        in_specs=in_specs,
        out_specs=[pl.BlockSpec((rows, d), lambda i, s: (0, 0))] * 2 + [pl.BlockSpec((2, rows, d), lambda i, s: (0, 0, 0))],
    )
    return pl.pallas_call(
        functools.partial(out_grad_kernel, count),
        grid_spec=spec,
        out_shape=[jax.ShapeDtypeStruct((rows, d), BF16)] * 2 + [jax.ShapeDtypeStruct((2, rows, d), BF16)],
        compiler_params=params(),
        cost_estimate=cost(5),
        name="out_grad_call",
    )(info, *[a for chunk in atts for a in chunk], *[y1g] * count)


def h1_grad_kernel(w_ref, dqkv_ref, x_ref, sum_ref, *outs):
    s = pl.program_id(1)
    first = (s == 0) & (pl.program_id(0) == 0)
    hg_s = outs[-1]
    d = x_ref.shape[0]
    pieces = cuts(d, ROWS)
    total = 0.0
    for m in pieces:
        total = total + jnp.sum(x_ref[m].astype(F32), axis=0, keepdims=True)
    mean = total * (1.0 / d)
    total = 0.0
    for m in pieces:
        center = x_ref[m].astype(F32) - mean
        total = total + jnp.sum(center * center, axis=0, keepdims=True)
    root = lax.rsqrt(total * (1.0 / d) + EPS)
    dqkv = dqkv_ref[...]
    for m in pieces:
        hg = dot(w_ref[m], dqkv)
        n = (x_ref[m].astype(F32) - mean) * root
        hg_s[m] = hg.astype(BF16)
        add_to(first, sum_ref, 0, m, fold(hg * n))
        add_to(first, sum_ref, 1, m, fold(hg))
    to_slot(s, hg_s, outs[:3])


def h1_grad_call(w, dqkv, x):
    d, total = x.shape
    per = total // (BLK * SLOTS)
    m = w.shape[1]
    at = lambda p, s: (0, p * SLOTS + s)
    mine = pl.BlockSpec((d, BLK), lambda p, s: (0, p))
    side = pl.BlockSpec((2, d, BLK), lambda p, s: (0, 0, p))
    return pl.pallas_call(
        h1_grad_kernel,
        grid=(per, SLOTS),
        in_specs=[
            pl.BlockSpec((d, m), lambda p, s: (0, 0), pipeline_mode=pl.Buffered(1)),
            pl.BlockSpec((m, BLK), at),
            pl.BlockSpec((d, BLK), at),
        ],
        out_specs=[pl.BlockSpec((2, d, 128), lambda p, s: (0, 0, 0)), mine, mine, side],
        out_shape=[jax.ShapeDtypeStruct((2, d, 128), F32)]
        + [jax.ShapeDtypeStruct((d, per * BLK), BF16)] * 2
        + [jax.ShapeDtypeStruct((2, d, per * BLK), BF16)],
        scratch_shapes=[pltpu.VMEM((d, BLK), BF16)],
        compiler_params=params(),
        cost_estimate=cost(13),
        name="h1_grad_call",
    )(w, dqkv, x)


def input_grad_kernel(x_ref, a_ref, b_ref, y1g_ref, gain_ref, out_ref):
    n, root = normal(x_ref[...].astype(F32))
    e = (a_ref[...] + b_ref[...].astype(F32)) * gain_ref[:, GAIN1 : GAIN1 + 1]
    e = root * (e - jnp.mean(e, axis=0, keepdims=True) - n * jnp.mean(e * n, axis=0, keepdims=True))
    out_ref[...] = (y1g_ref[...] + e).astype(BF16)


def input_grad_call(x, a, b, y1g, gain):
    d, rows = x.shape
    block = pl.BlockSpec((d, 128), lambda i: (0, i))
    return pl.pallas_call(
        input_grad_kernel,
        grid=(rows // 128,),
        in_specs=[block] * 4 + [pl.BlockSpec(gain.shape, lambda i: (0, 0))],
        out_specs=block,
        out_shape=jax.ShapeDtypeStruct((d, rows), BF16),
        compiler_params=params(),
        cost_estimate=cost(6),
        name="input_grad_call",
    )(x, a, b, y1g, gain)


def swap(v, k):
    return lax.ppermute(v, "tensor", [(i, i ^ k) for i in range(SLOTS)])


def after(v, *done):
    return lax.optimization_barrier((v, done))[0]


class Line:
    def __init__(self):
        self.last = []

    def __call__(self, step, *args):
        args, _ = lax.optimization_barrier((args, self.last))
        out = step(*args)
        self.last = jax.tree.leaves(out)
        return out

    def wait(self, *values):
        self.last = self.last + jax.tree.leaves(values)

    def pin(self, v, *also):
        return after(v, self.last, also)


class Gather:
    def __init__(self, v):
        self.own, self.side, self.across = v, swap(v, 1), swap(v, 2)

    def finish(self, line):
        self.corner = swap(line.pin(self.across), 1)
        return self

    def all(self):
        return self.own, self.side, self.across, self.corner


def plus(a, b):
    return a.astype(F32) + b.astype(F32)


def plus_low(a, b):
    return plus(a, b).astype(BF16)


def add_kernel(*refs):
    total = None
    for ref in refs[:-1]:
        v = (ref[0] if len(ref.shape) == 3 else ref[...]).astype(F32)
        total = v if total is None else total + v
    refs[-1][...] = total.astype(refs[-1].dtype)


def add(dtype, *terms):
    rows, columns = terms[0].shape
    size = rows // 2 if rows % 32 == 0 and rows * columns > 1 << 18 else rows
    in_specs, args = [], []
    for term in terms:
        if isinstance(term, tuple):
            in_specs.append(pl.BlockSpec((1, size, columns), functools.partial(lambda at, i: (at, i, 0), term[1])))
            args.append(term[0])
        else:
            in_specs.append(pl.BlockSpec((size, columns), lambda i: (i, 0)))
            args.append(term)
    return pl.pallas_call(
        add_kernel,
        grid=(rows // size,),
        in_specs=in_specs,
        out_specs=pl.BlockSpec((size, columns), lambda i: (i, 0)),
        out_shape=jax.ShapeDtypeStruct((rows, columns), dtype),
        compiler_params=params(),
        cost_estimate=cost(2.3),
        name="add",
    )(*args)


def plus_second(a, pair):
    return add(BF16, a, (pair, 1))


def plus_first(a, pair, far, dtype=F32):
    return add(dtype, a, (pair, 0), far)


def stack_kernel(*refs):
    at = 0
    for ref in refs[:-1]:
        refs[-1][at : at + ref.shape[0]] = ref[...]
        at += ref.shape[0]


def stack(*parts):
    return pl.pallas_call(
        stack_kernel,
        out_shape=jax.ShapeDtypeStruct((sum(p.shape[0] for p in parts), parts[0].shape[1]), parts[0].dtype),
        compiler_params=params(),
        cost_estimate=cost(2),
        name="stack",
    )(*parts)


def token_starts(lengths, offsets, total, dev):
    pos = jnp.arange(total, dtype=jnp.int32)[:, None]
    inside = (pos >= offsets[None]) & (pos < (offsets + lengths)[None])
    first = jnp.max(jnp.where(inside, offsets[None], -1), axis=1)
    start = jnp.where(first >= 0, first, pos[:, 0])
    nb = total // BLK
    per = nb // SLOTS
    b = jnp.arange(nb, dtype=jnp.int32)
    first_key = start.reshape(nb, BLK)[:, 0] // BLK
    place = (b % per) * SLOTS + ((b // per) ^ dev)
    last_query = jnp.max(jnp.where(first_key[None, :] <= b[:, None], b[None, :], 0), axis=1)
    info = jnp.concatenate([first_key, place, last_query, jnp.full((1,), dev)])
    return start[None], info.astype(jnp.int32)


def body(
    tokens,
    cotangent,
    ln1_gain,
    ln1_bias,
    attn_weight,
    qv_bias,
    out_weight,
    out_bias,
    ln2_gain,
    ln2_bias,
    up_weight,
    up_bias,
    down_weight,
    down_bias,
    cell_lengths,
    cell_offsets,
):
    rows, d = tokens.shape
    width = attn_weight.shape[2]
    heads = width // HEAD_DIM
    total = rows * SLOTS
    per = rows // BLK
    dev = lax.axis_index("tensor")
    start, info = token_starts(cell_lengths[0], cell_offsets[0], total, dev)

    whole_dp = lax.axis_size("dp") == 8
    dp_info = jnp.full((1,), lax.axis_index("dp") if whole_dp else 0, jnp.int32)

    line = Line()
    x_own = tokens.T
    g_own = cotangent.T
    x_go = Gather(x_own)

    w_in = attn_weight.transpose(1, 2, 0)
    zero = jnp.zeros_like(ln1_gain)
    rows8 = jnp.stack([ln1_gain, ln1_bias, out_bias, ln2_gain, ln2_bias, up_bias, down_bias, zero])
    bias8 = jnp.zeros((8, width), F32).at[0].set(qv_bias[0]).at[2].set(qv_bias[1])
    upt, wdt, w_back, vec, bias, *g_cuts = line(
        turn, g_own, up_weight, down_weight, w_in.reshape(3 * width, d), rows8, bias8
    )
    carry = line(lambda a, b: qkv_call(0, a, b, w_in, vec, bias, None), x_own, x_go.side)
    wo_go = Gather(line.pin(out_weight, x_go.across))
    x_parts = x_go.finish(line).all()
    x_all, h1, qkv, kn, vn = line(lambda a, b, c: qkv_call(1, a, b, w_in, vec, bias, c), x_parts[2], x_parts[3], carry)
    chunks = range(per)
    g_go = [Gather(line.pin(g_cuts[0]))]
    fronts, att_go = [], []
    for c in chunks:
        fronts.append(line(functools.partial(attend, c), info, start, qkv, kn))
        att_go.append(Gather(fronts[c][0].reshape(width, SLOTS * BLK)))
        if c == 0:
            wo_parts = wo_go.finish(line).all()
    wot = line(turn_pieces, *wo_parts)
    g_parts = [g_go[0].finish(line).all()]
    atts, ahead = [], []
    for c in chunks:
        atts.append(att_go[c].finish(line).all())
        if c > 0:
            g_parts.append(g_go[c].finish(line).all())
        if c + 1 < per:
            g_go.append(Gather(line.pin(g_cuts[c + 1], atts[c][2])))
        ahead.append(
            line(
                functools.partial(forward, c),
                info,
                atts[c],
                x_all,
                g_parts[c],
                wot,
                upt,
                down_weight,
                wdt,
                vec,
                ahead[-1][7:] if c else None,
            )
        )
    h2s, acts, pgs, gs, ns, roots, up_sums = zip(*[m[:7] for m in ahead])
    own, layer0, layer2, layer13 = ahead[-1][7:]
    layer_near = swap(layer13, 1)
    flat = lambda a, b: list(zip(a, b))
    y_first, z_first = (1, 2, 4), (2, 1, 4)
    f = down_weight.shape[0]
    down = CellSum(line, *line(lambda a, b: outer(flat(a, b), dp_info, y_first), acts, gs), dp_info, y_first, f)
    layer_far = swap(line(plus_second, layer2, layer_near), 2)
    up = CellSum(line, *line(lambda a, b: outer(flat(a, b), dp_info, z_first), h2s, pgs), dp_info, z_first, d)

    back, attgs = [], []
    for c in chunks:
        carry = back[-1][4:] if c else None
        back.append(
            line(functools.partial(backward, c), info, pgs[c], ns[c], roots[c], g_own, up_weight, wo_parts, vec, carry)
        )
        attg0, attg2, attg13 = back[c][1:4]
        line.wait(attgs[-1][2] if c else layer_far)
        near = swap(line.pin(attg13), 1)
        (up if c else down).step()
        attgs.append((attg0, near, swap(line(plus_second, attg2, near), 2)))
    y1g0, y1g2, y1g13 = back[-1][4:]
    y1_near = swap(line.pin(y1g13), 1)
    down.step()
    y1_far = swap(line(plus_second, y1g2, y1_near), 2)
    do, stat = line(join, [a + tuple(f) for a, f in zip(attgs, fronts)])
    dqkv = line(attend_back, info, start, qkv, kn, vn, do, stat).reshape(3 * width, total)
    down.step()
    up.step()
    line.wait(y1_far)
    attn_parts = line(lambda a, b: outer([(a, b)], dp_info, y_first, with_sum=True), dqkv, h1)
    attn = CellSum(line, *attn_parts[:2], dp_info, y_first, 3 * width)
    down.step()
    up.step()
    sum1, h10, h12, h113 = line(h1_grad_call, w_back, dqkv, x_all)
    h1_near = swap(line.pin(h113), 1)
    down.step()
    up.step()
    h1_far = swap(line(plus_second, h12, h1_near), 2)
    attn.step()
    y1_grad = line(plus_first, y1g0, y1_near, y1_far)
    out0, out2, out13 = line(lambda a, y: out_grad_call(info, a, y.astype(BF16)), atts, y1_grad)

    def smalls(sum1, sums, up_sums, qkv_sum, g):
        sum1 = jnp.sum(sum1, axis=2)
        sum2 = jnp.sum(sum(sums), axis=2)
        up_row = jnp.sum(sum(up_sums), axis=2)
        qkv_sum = jnp.sum(qkv_sum[: 3 * width], axis=1).reshape(3, width)
        down_row = jnp.sum(g.astype(F32), axis=1)
        qv_row = jnp.pad(jnp.concatenate([qkv_sum[0], qkv_sum[2]]), (0, d - 2 * width))
        return jnp.concatenate([sum1, sum2, down_row[None], up_row, qv_row[None]], 0)

    small = line(smalls, sum1, [m[0] for m in back], up_sums, attn_parts[2], g_own)
    up.step()
    attn.step()
    layer = line(
        lambda own, a, near, far: (own + plus_first(a, near, far) + down_bias[:, None]).astype(BF16),
        own,
        layer0,
        layer_near,
        layer_far,
    )
    near = line(lambda a, b: add(F32, a, (b, 0)), h10, h1_near)
    line.wait(h1_far, down.got)
    out_near = swap(line.pin(out13), 1)
    attn.step()
    out_far = swap(line(plus_second, out2, out_near), 2)
    down_grad = down.finish()
    line.wait(out_far)
    small = Rounds(line, line.pin(small), True)
    input_grad = line(input_grad_call, x_own, near, h1_far, y1_grad, vec)
    attn.step()
    small.step()
    line.wait(up.got)
    out_sum = Rounds(line, line(lambda a, b, c: plus_first(a, b, c, BF16), out0, out_near, out_far))
    small.step()
    up_grad = up.finish()
    out_sum.step()
    attn.step()
    small.step()
    out_sum.step()
    small.step()
    out_sum.step()
    small.step()
    out_grad = line(lambda v: v.astype(F32), out_sum.v)
    attn_grad = attn.finish()
    small, own_small = small.v, small.cells[6:]
    return (
        layer.T,
        input_grad.T,
        small[0],
        small[1],
        attn_grad.reshape(3, width, d).transpose(2, 0, 1),
        own_small[1, : 2 * width].reshape(2, width),
        out_grad,
        small[4],
        small[2],
        small[3],
        up_grad,
        own_small[0],
        down_grad,
        small[5],
    )


def solution(mesh):
    rows = P(("dp", "tensor"), None)
    in_specs = (
        rows,
        rows,
        P(),
        P(),
        P(None, None, "tensor"),
        P(None, "tensor"),
        P("tensor", None),
        P(),
        P(),
        P(),
        P(None, "tensor"),
        P("tensor"),
        P("tensor", None),
        P(),
        P("dp", None),
        P("dp", None),
    )
    out_specs = (
        rows,
        rows,
        P(),
        P(),
        P(None, None, "tensor"),
        P(None, "tensor"),
        P("tensor", None),
        P(),
        P(),
        P(),
        P(None, "tensor"),
        P("tensor"),
        P("tensor", None),
        P(),
    )
    return jax.shard_map(body, mesh=mesh, in_specs=in_specs, out_specs=out_specs, check_vma=False)
```

time: 603 us -> 561 us (0.930)
  Pallas kernels: 179 us -> 324 us
  blocking collectives: 80.3 us -> 0 us
  waiting for transfers between devices: 180 us -> 126 us
  other arithmetic: 51.8 us -> 15 us
  local copies, waits for them, and re-layouts: 63 us -> 34.1 us
  starting transfers between devices: 22.8 us -> 50.3 us
  between operations: 15 us -> 1.52 us
    pallas_call x6 -> x47, Pallas kernels: 115 us -> 252 us  [the longest x2 53.9 us: forward(): pl.pallas_call(forward_kernel, grid_spec=spec, out_shape=[shape((d, wide)...]
    ppermute x0 -> x24, waiting for transfers between devices: none -> 114 us  [swap_dp(): return lax.ppermute(v, 'dp', [(i, i ^ k) for i in range(8)])]
    ppermute x39 -> x32, waiting for transfers between devices: 116 us -> 12.4 us  [swap(): return lax.ppermute(v, 'tensor', [(i, i ^ k) for i in range(SLOTS)])]
    psum x2 -> x0, blocking collectives: 80.3 us -> none  [the longest x1 41.3 us: body(): small = lax.psum(small, ('dp', 'tensor'))]
    psum x2 -> x0, waiting for transfers between devices: 63.9 us -> none  [the longest x1 63.9 us: body(): late = lax.psum(late[:2], 'dp')]
    ppermute x0 -> x24, starting transfers between devices: none -> 30.8 us  [swap_dp(): return lax.ppermute(v, 'dp', [(i, i ^ k) for i in range(8)])]
    convert_element_type x15 -> x3, other arithmetic: 28.1 us -> 6.84 us  [the longest x1 2.91 us: body(): (own + plus_first(a, near, far) + down_bias[:, None]).astype(BF16)]
    squeeze x5 -> x0, local copies, waits for them, and re-layouts: 12.3 us -> none  [the longest x2 5.72 us: body(): layer_parts = [scatter_sum([y[k] for k in range(SLOTS)]) for y in layers]]
  transfers between devices with their start and end apart: 41 -> 56, of which waited for: 9 -> 16; matrix products, arithmetic and copies ran while one was open for 17% -> 4% of each run, Pallas kernels for 30% -> 49%
where the time goes in v2:
time: 561 us; the launch traced here: 551 us
  Pallas kernels  324 us (58%)
  waiting for transfers between devices  126 us (22%)
  starting transfers between devices  50.3 us (9%)
  local copies, waits for them, and re-layouts  34.1 us (6%)
  other arithmetic  15 us (3%)
    ppermute x24, waiting for transfers between devices, swap_dp(): return lax.ppermute(v, 'dp', [(i, i ^ k) for i in range(8)])  114 us
    pallas_call x2, Pallas kernels, forward(): pl.pallas_call(forward_kernel, grid_spec=spec, out_shape=[shape((d, wide)...  53.9 us
    pallas_call x21, Pallas kernels, add(): pl.pallas_call(add_kernel, grid=(rows // size,), in_specs=in_specs, out_s...  45.9 us
    pallas_call x3, Pallas kernels, outer(): pl.pallas_call(functools.partial(outer_kernel, len(pairs), order, with_su...  34.8 us
    pallas_call x2, Pallas kernels, backward(): pl.pallas_call(backward_kernel, grid_spec=spec, out_shape=[shape((3, d, 1...  34.6 us
    ppermute x24, starting transfers between devices, swap_dp(): return lax.ppermute(v, 'dp', [(i, i ^ k) for i in range(8)])  30.8 us
    unnamed x116, local copies, waits for them, and re-layouts  25.6 us
    pallas_call x1, Pallas kernels, attend_back(): pl.pallas_call(functools.partial(attend_back_kernel, heads, nb, per), gri...  22.5 us
  transfers between devices with their start and end apart: 56, of which 16 were waited for; matrix products, arithmetic and copies ran while one was open for 4% of the time, Pallas kernels for 49%

profile of v2, /device:TPU:0, one launch (start us, length us, event | category | flops | bytes accessed | tf_op | source)
XLA Modules:
  0.0 550.5 jit_solution(18385699009111438222)
XLA Ops:
  1.2 2.6 collective-permute-start
  10.2 9.2 %turn.1 = (bf16[1120,1120]{1,0:T(8,128)(2,1)}, bf16[1120,1120]{1,0:T(8,128)(2,1)}, bf16[1120,840]{1,0:T(8,128)(2,1)}, f32[1120,8]{1,0:T(8,128)}, f32[280,8]{1,0:...) custom-call(bf16[1120,1120]{1,0:T(8,128)(2,1)} %up.1, bf16[1120,1120]{1,0:T(8,128)(2,1)} %refs_10_.1, ...), custom_call_target="tpu_custom_call" | custom-call | flops 18400000000 | bytes 1 | tf_op jit(solution)/shard_map/turn/pallas_call | solution.py:83
  20.4 8.3 %qkv_call.2 = (bf16[1120,2048]{1,0:T(8,128)(2,1)}, bf16[1120,2048]{1,0:T(8,128)(2,1)}, bf16[15,56,2048]{2,1,0:T(8,128)(2,1)}, bf16[5,2048,56]{2,1,0:T(8,128)(2,1)}, bf16[5,2048,56]{2,1,0:T(8,128)(2,1)}) custom-call(bf16[1120,512]{1,0:T(8,128)(2,1)} %bitcast.37, bf16[1120,512]{1,0:T(8,128)(2,1)} %copy-done.22, bf16[3,280,1120]{2,1,0:T(8,128)(2,1)} %bitcast.33, ...), custom_call_target="tpu_custom_call" | custom-call | flops 18400000000 | bytes 1 | tf_op jit(solution)/shard_map/qkv_call/pallas_call | solution.py:177
  34.4 8.2 %qkv_call.3 = (bf16[1120,2048]{1,0:T(8,128)(2,1)}, bf16[1120,2048]{1,0:T(8,128)(2,1)}, bf16[15,56,2048]{2,1,0:T(8,128)(2,1)}, bf16[5,2048,56]{2,1,0:T(8,128)(2,1)}, bf16[5,2048,56]{2,1,0:T(8,128)(2,1)}) custom-call(bf16[1120,512]{1,0:T(8,128)(2,1)} %copy-done.20, ...), custom_call_target="tpu_custom_call", output_to_operand_aliasing={{0}: (5, {}), {1}: (6, {}), {2}: (7, {}), {3}: (8, {}), {4}... | custom-call | flops 18400000000 | bytes 1 | tf_op jit(solution)/shard_map/qkv_call/pallas_call | solution.py:177
  43.6 11.4 %attend.2 = (bf16[5,56,1024]{2,1,0:T(8,128)(2,1)}, f32[8,1024]{1,0:T(8,128)}) custom-call(s32[25]{0:T(128)} %pad_add_fusion.info, s32[1,2048]{1,0:T(1,128)} %compare_select_fusion.start_ref, bf16[15,56,2048]{2,1,0:T(8,128)(2,1)} %get-tuple-element.562.q_ref.v_ref.k_ref, bf16[5,2048,56]{2,1,0:T(8,128)(2,1)} %get-tuple-element.563.kn_ref, ...), custom_call_target="tpu_custom_call" | custom-call | flops 21849999360 | bytes 1 | tf_op jit(solution)/shard_map/attend/pallas_call | solution.py:256
  56.4 9.8 %attend.3 = (bf16[5,56,1024]{2,1,0:T(8,128)(2,1)}, f32[8,1024]{1,0:T(8,128)}) custom-call(s32[25]{0:T(128)} %pad_add_fusion.info, s32[1,2048]{1,0:T(1,128)} %compare_select_fusion.start_ref, bf16[15,56,2048]{2,1,0:T(8,128)(2,1)} %get-tuple-element.562.q_ref.v_ref.k_ref, bf16[5,2048,56]{2,1,0:T(8,128)(2,1)} %get-tuple-element.563.kn_ref, ...), custom_call_target="tpu_custom_call" | custom-call | flops 21849999360 | bytes 1 | tf_op jit(solution)/shard_map/attend/pallas_call | solution.py:256
  67.4 5.3 turn_pieces.1.refs_8_
  76.4 27.0 %forward.2 = (bf16[1120,1024]{1,0:T(8,128)(2,1)}, bf16[1120,1024]{1,0:T(8,128)(2,1)}, bf16[1120,1024]{1,0:T(8,128)(2,1)}, bf16[1120,1024]{1,0:T(8,128)(2,1)}, bf...) custom-call(s32[25]{0:T(128)} %pad_add_fusion.info, ...), custom_call_target="tpu_custom_call" | custom-call | flops 59799998464 | bytes 1 | tf_op jit(solution)/shard_map/forward/pallas_call | solution.py:517
  108.1 26.9 %forward.3 = (bf16[1120,1024]{1,0:T(8,128)(2,1)}, bf16[1120,1024]{1,0:T(8,128)(2,1)}, bf16[1120,1024]{1,0:T(8,128)(2,1)}, bf16[1120,1024]{1,0:T(8,128)(2,1)}, bf...) custom-call(s32[25]{0:T(128)} %pad_add_fusion.info, ...), custom_call_target="tpu_custom_call", output_to_operand_aliasing={{7}: (15, {}), {8}: (16, {}), {9}: (17, {}), {10}: (18, {})} | custom-call | flops 59799998464 | bytes 1 | tf_op jit(solution)/shard_map/forward/pallas_call | solution.py:517
  135.4 11.5 %outer.3 = (bf16[576,1120]{1,0:T(8,128)(2,1)}, bf16[576,1120]{1,0:T(8,128)(2,1)}) custom-call(s32[1]{0:T(128)} %bitcast.10.info, bf16[1120,1024]{1,0:T(8,128)(2,1)} %get-tuple-element.474.refs_0_, bf16[1120,1024]{1,0:T(8,128)(2,1)} %get-tuple-element.475.refs_1_, bf16[1120,1024]{1,0:T(8,128)(2,1)} %get-tuple-element.476.refs_2_, ...), custom_call_target="tpu_custom_call" | custom-call | flops 25300000768 | bytes 1 | tf_op jit(solution)/shard_map/outer/pallas_call | solution.py:677
  154.0 11.7 %outer.4 = (bf16[576,1120]{1,0:T(8,128)(2,1)}, bf16[576,1120]{1,0:T(8,128)(2,1)}) custom-call(s32[1]{0:T(128)} %bitcast.10.info, bf16[1120,1024]{1,0:T(8,128)(2,1)} %get-tuple-element.482.refs_0_, bf16[1120,1024]{1,0:T(8,128)(2,1)} %get-tuple-element.489.refs_1_.pg_ref, bf16[1120,1024]{1,0:T(8,128)(2,1)} %get-tuple-element.484.refs_2_, ...), custom_call_target="tpu_custom_call" | custom-call | flops 25300000768 | bytes 1 | tf_op jit(solution)/shard_map/outer/pallas_call | solution.py:677
  165.8 17.4 %backward.2 = (f32[3,1120,128]{2,1,0:T(8,128)}, bf16[280,1024]{1,0:T(8,128)(2,1)}, bf16[280,1024]{1,0:T(8,128)(2,1)}, bf16[2,280,1024]{2,1,0:T(8,128)(2,1)}, bf1...) custom-call(s32[25]{0:T(128)} %pad_add_fusion.info, ...), custom_call_target="tpu_custom_call" | custom-call | flops 39099998208 | bytes 1 | tf_op jit(solution)/shard_map/backward/pallas_call | solution.py:610
  184.2 3.6 collective-permute-start.24
  188.9 3.1 halve.6
  195.3 17.2 %backward.3 = (f32[3,1120,128]{2,1,0:T(8,128)}, bf16[280,1024]{1,0:T(8,128)(2,1)}, bf16[280,1024]{1,0:T(8,128)(2,1)}, bf16[2,280,1024]{2,1,0:T(8,128)(2,1)}, bf1...) custom-call(s32[25]{0:T(128)} %pad_add_fusion.info, ...), custom_call_target="tpu_custom_call", output_to_operand_aliasing={{4}: (11, {}), {5}: (12, {}), {6}: (13, {})} | custom-call | flops 39099998208 | bytes 1 | tf_op jit(solution)/shard_map/backward/pallas_call | solution.py:610
  213.4 4.2 collective-permute-done.24.recv_ref
  218.7 3.0 halve.7
  227.9 14.6 %collective-permute-done.27.recv_ref = bf16[288,1120]{1,0:T(8,128)(2,1)S(1)} collective-permute-done((bf16[288,1120]{1,0:T(8,128)(2,1)}, bf16[288,1120]{1,0:T(8,128)(2,1)S(1)}, u32[]{:S(2)}, u32[]{:S(2)}) %collective-permute-start.27) | collective-permute-done | bytes 645152 | tf_op jit(solution)/shard_map/ppermute | solution.py:758
  247.8 2.5 add.108
  250.9 5.2 join.1
  256.1 22.5 %attend_back.1 = bf16[15,56,2048]{2,1,0:T(8,128)(2,1)} custom-call(s32[25]{0:T(128)} %pad_add_fusion.info, s32[1,2048]{1,0:T(1,128)} %compare_select_fusion.start_ref, bf16[15,56,2048]{2,1,0:T(8,128)(2,1)} %get-tuple-element.562.q_ref.v_ref.k_ref, bf16[15,56,2048]{2,1,0:T(8,128)(2,1)} %get-tuple-element.562.q_ref.v_ref.k_ref, ...), custom_call_target="tpu_custom_call" | custom-call | flops 46000001024 | bytes 1 | tf_op jit(solution)/shard_map/attend_back/pallas_call | solution.py:352
  280.5 2.6 collective-permute-start.33
  286.5 11.5 %outer.5 = (bf16[448,1120]{1,0:T(8,128)(2,1)}, bf16[448,1120]{1,0:T(8,128)(2,1)}, f32[896,128]{1,0:T(8,128)}) custom-call(s32[1]{0:T(128)} %bitcast.10.info, bf16[840,2048]{1,0:T(8,128)(2,1)} %bitcast.50, bf16[1120,2048]{1,0:T(8,128)(2,1)} %get-tuple-element.574.refs_1_), custom_call_target="tpu_custom_call" | custom-call | flops 25300000768 | bytes 1 | tf_op jit(solution)/shard_map/outer/pallas_call | solution.py:677
  298.1 8.5 %collective-permute-done.33.refs_1_.two = bf16[144,1120]{1,0:T(8,128)(2,1)S(1)} collective-permute-done((bf16[144,1120]{1,0:T(8,128)(2,1)}, bf16[144,1120]{1,0:T(8,128)(2,1)S(1)}, u32[]{:S(2)}, u32[]{:S(2)}) %collective-permute-start.33) | collective-permute-done | bytes 322592 | tf_op jit(solution)/shard_map/ppermute | solution.py:758
  309.2 2.7 collective-permute-done.32.refs_1_
  314.6 13.7 %h1_grad_call.1 = (f32[2,1120,128]{2,1,0:T(8,128)}, bf16[1120,512]{1,0:T(8,128)(2,1)}, bf16[1120,512]{1,0:T(8,128)(2,1)}, bf16[2,1120,512]{2,1,0:T(8,128)(2,1)}) custom-call(bf16[1120,840]{1,0:T(8,128)(2,1)} %get-tuple-element.582.w_ref, bf16[840,2048]{1,0:T(8,128)(2,1)} %bitcast.51, bf16[1120,2048]{1,0:T(8,128)(2,1)} %get-tuple-element.584.x_ref), custom_call_target="tpu_custom_call" | custom-call | flops 29899999232 | bytes 1 | tf_op jit(solution)/shard_map/h1_grad_call/pallas_call | solution.py:892
  329.1 3.3 collective-permute-start.35
  332.5 20.4 %collective-permute-done.36.refs_2_.four = bf16[288,1120]{1,0:T(8,128)(2,1)S(1)} collective-permute-done((bf16[288,1120]{1,0:T(8,128)(2,1)}, bf16[288,1120]{1,0:T(8,128)(2,1)S(1)}, u32[]{:S(2)}, u32[]{:S(2)}) %collective-permute-start.36) | collective-permute-done | bytes 645152 | tf_op jit(solution)/shard_map/ppermute | solution.py:758
  365.5 2.7 halve.10
  368.2 3.1 add.112.y1g_ref
  371.4 2.8 convert_element_type.14.refs_8_.refs_9_
  374.2 5.2 out_grad_call.1
  386.1 15.4 %collective-permute-done.38.refs_2_.four = bf16[288,1120]{1,0:T(8,128)(2,1)} collective-permute-done((bf16[288,1120]{1,0:T(8,128)(2,1)}, bf16[288,1120]{1,0:T(8,128)(2,1)}, u32[]{:S(2)}, u32[]{:S(2)}) %collective-permute-start.38) | collective-permute-done | bytes 645152 | tf_op jit(solution)/shard_map/ppermute | solution.py:758
  401.5 2.6 stack.41
  406.4 3.3 add.113
  409.7 2.9 add_convert_fusion
  412.6 2.8 add.114.a_ref
  419.6 11.1 %collective-permute-done.42.refs_1_ = bf16[112,1120]{1,0:T(8,128)(2,1)S(1)} collective-permute-done((bf16[112,1120]{1,0:T(8,128)(2,1)S(1)}, bf16[112,1120]{1,0:T(8,128)(2,1)S(1)}, u32[]{:S(2)}, u32[]{:S(2)}) %collective-permute-start.42) | collective-permute-done | bytes 250912 | tf_op jit(solution)/shard_map/ppermute | solution.py:758
  436.8 6.7 %place.3 = f32[1120,1120]{1,0:T(8,128)} custom-call(s32[1]{0:T(128)} %bitcast.10.info, bf16[144,1120]{1,0:T(8,128)(2,1)} %add.109.refs_0_.one, bf16[144,1120]{1,0:T(8,128)(2,1)} %copy-done.47, bf16[288,1120]{1,0:T(8,128)(2,1)} %copy-done.27, bf16[576,1120]{1,0:T(8,128)(2,1)} %collective-permute-done.40.eight), custom_call_target="tpu_custom_call" | custom-call | flops 14949999616 | bytes 1 | tf_op jit(solution)/shard_map/place/pallas_call | solution.py:746
  443.5 8.2 %collective-permute-done.43.refs_2_ = bf16[280,1120]{1,0:T(8,128)(2,1)S(1)} collective-permute-done((bf16[280,1120]{1,0:T(8,128)(2,1)}, bf16[280,1120]{1,0:T(8,128)(2,1)S(1)}, u32[]{:S(2)}, u32[]{:S(2)}) %collective-permute-start.43) | collective-permute-done | bytes 627232 | tf_op jit(solution)/shard_map/ppermute | solution.py:934
  451.7 6.7 %input_grad_call.1 = bf16[1120,512]{1,0:T(8,128)(2,1)} custom-call(bf16[1120,512]{1,0:T(8,128)(2,1)} %bitcast.38, f32[1120,512]{1,0:T(8,128)} %add.114.a_ref, bf16[1120,512]{1,0:T(8,128)(2,1)} %collective-permute-done.39.b_ref, f32[1120,512]{1,0:T(8,128)} %add.112.y1g_ref, f32[1120,8]{1,0:T(8,128)} %get-tuple-element.649.vec_ref.refs_12_.refs_4_.gain_ref), custom_call_target="tpu_custom_call" | custom-call | flops 13799999488 | bytes 1 | tf_op jit(solution)/shard_map/input_grad_call/pallas_call | solution.py:921
  461.0 3.1 collective-permute-start.49
  467.6 3.0 add.118.refs_0_
  470.9 5.0 collective-permute-done.46.refs_1_
  479.5 6.7 %place.4 = f32[1120,1120]{1,0:T(8,128)} custom-call(s32[1]{0:T(128)} %bitcast.10.info, bf16[144,1120]{1,0:T(8,128)(2,1)} %add.110.refs_0_.one, bf16[144,1120]{1,0:T(8,128)(2,1)} %collective-permute-done.35.refs_1_.two, bf16[288,1120]{1,0:T(8,128)(2,1)} %collective-permute-done.38.refs_2_.four, bf16[576,1120]{1,0:T(8,128)(2,1)} %copy-done.14), custom_call_target="tpu_custom_call" | custom-call | flops 14949999616 | bytes 1 | tf_op jit(solution)/shard_map/place/pallas_call | solution.py:746
  494.4 9.6 %collective-permute-done.52.refs_1_ = bf16[280,1120]{1,0:T(8,128)(2,1)S(1)} collective-permute-done((bf16[280,1120]{1,0:T(8,128)(2,1)}, bf16[280,1120]{1,0:T(8,128)(2,1)S(1)}, u32[]{:S(2)}, u32[]{:S(2)}) %collective-permute-start.52) | collective-permute-done | bytes 627232 | tf_op jit(solution)/shard_map/ppermute | solution.py:758
  513.6 22.1 %collective-permute-done.54.refs_1_ = bf16[280,1120]{1,0:T(8,128)(2,1)S(1)} collective-permute-done((bf16[280,1120]{1,0:T(8,128)(2,1)}, bf16[280,1120]{1,0:T(8,128)(2,1)S(1)}, u32[]{:S(2)}, u32[]{:S(2)}) %collective-permute-start.54) | collective-permute-done | bytes 627232 | tf_op jit(solution)/shard_map/ppermute | solution.py:758
  543.5 6.6 %place.5 = f32[840,1120]{1,0:T(8,128)} custom-call(s32[1]{0:T(128)} %bitcast.10.info, bf16[112,1120]{1,0:T(8,128)(2,1)} %add.115.refs_0_.one, bf16[112,1120]{1,0:T(8,128)(2,1)} %copy-done.49, bf16[224,1120]{1,0:T(8,128)(2,1)} %collective-permute-done.49.refs_2_.four, bf16[448,1120]{1,0:T(8,128)(2,1)} %copy-done.26), custom_call_target="tpu_custom_call" | custom-call | flops 14949999616 | bytes 1 | tf_op jit(solution)/shard_map/place/pallas_call | solution.py:746
  (272 shorter events, 131.3 us)
Async XLA Ops:
  0.6 18.8 %collective-permute-start.1 = (bf16[1120,512]{1,0:T(8,128)(2,1)}, bf16[1120,512]{1,0:T(8,128)(2,1)S(1)}, u32[]{:S(2)}, u32[]{:S(2)}) collective-permute-start(bf16[1120,512]{1,0:T(8,128)(2,1)} %bitcast.35), channel_id=1, source_target_pairs={{0,1},{1,0},{2,3},{3,2},{4,5},{5,4},{6,7},{7,6},{8,9},{9,8},{10,11... | collective-permute-start | bytes 3440648 | tf_op jit(solution)/shard_map/ppermute | solution.py:934
  1.2 28.6 %collective-permute-start = (bf16[1120,512]{1,0:T(8,128)(2,1)}, bf16[1120,512]{1,0:T(8,128)(2,1)S(1)}, u32[]{:S(2)}, u32[]{:S(2)}) collective-permute-start(bf16[1120,512]{1,0:T(8,128)(2,1)} %bitcast.36), channel_id=1, source_target_pairs={{0,2},{1,3},{2,0},{3,1},{4,6},{5,7},{6,4},{7,5},{8,10},{9,11},{10,... | collective-permute-start | bytes 3440648 | tf_op jit(solution)/shard_map/ppermute | solution.py:934
  31.4 23.5 %collective-permute-start.8 = (bf16[280,1120]{1,0:T(8,128)(2,1)S(1)}, bf16[280,1120]{1,0:T(8,128)(2,1)S(1)}, u32[]{:S(2)}, u32[]{:S(2)}) collective-permute-start(bf16[280,1120]{1,0:T(8,128)(2,1)S(1)} %copy-done.30), channel_id=1, source_target_pairs={{0,2},{1,3},{2,0},{3,1},{4,6},{5,7},{6,4},{7,5},{8,10},{9,11},{10,... | collective-permute-start | bytes 1881608 | tf_op jit(solution)/shard_map/ppermute | solution.py:934
  33.2 33.0 %collective-permute-start.7 = (bf16[280,1120]{1,0:T(8,128)(2,1)S(1)}, bf16[280,1120]{1,0:T(8,128)(2,1)}, u32[]{:S(2)}, u32[]{:S(2)}) collective-permute-start(bf16[280,1120]{1,0:T(8,128)(2,1)S(1)} %copy-done.30), channel_id=1, source_target_pairs={{0,1},{1,0},{2,3},{3,2},{4,5},{5,4},{6,7},{7,6},{8,9},{9,8},{10,11... | collective-permute-start | bytes 1881608 | tf_op jit(solution)/shard_map/ppermute | solution.py:934
  42.6 30.1 %collective-permute-start.12 = (bf16[1120,256]{1,0:T(8,128)(2,1)}, bf16[1120,256]{1,0:T(8,128)(2,1)}, u32[]{:S(2)}, u32[]{:S(2)}) collective-permute-start(bf16[1120,256]{1,0:T(8,128)(2,1)} %get-tuple-element.421.refs_4_), channel_id=1, source_target_pairs={{0,2},{1,3},{2,0},{3,1},{4,6},{5,7},{6,4},{7,5},{8,10},{9,11},{10,... | collective-permute-start | bytes 1720328 | tf_op jit(solution)/shard_map/ppermute | solution.py:934
  43.6 31.6 %collective-permute-start.11 = (bf16[1120,256]{1,0:T(8,128)(2,1)}, bf16[1120,256]{1,0:T(8,128)(2,1)}, u32[]{:S(2)}, u32[]{:S(2)}) collective-permute-start(bf16[1120,256]{1,0:T(8,128)(2,1)} %get-tuple-element.421.refs_4_), channel_id=1, source_target_pairs={{0,1},{1,0},{2,3},{3,2},{4,5},{5,4},{6,7},{7,6},{8,9},{9,8},{10,11... | collective-permute-start | bytes 1720328 | tf_op jit(solution)/shard_map/ppermute | solution.py:934
  55.0 18.0 %collective-permute-start.6 = (bf16[280,1024]{1,0:T(8,128)(2,1)}, bf16[280,1024]{1,0:T(8,128)(2,1)S(1)}, u32[]{:S(2)}, u32[]{:S(2)}) collective-permute-start(bf16[280,1024]{1,0:T(8,128)(2,1)} %bitcast.40), channel_id=1, source_target_pairs={{0,2},{1,3},{2,0},{3,1},{4,6},{5,7},{6,4},{7,5},{8,10},{9,11},{10,... | collective-permute-start | bytes 1720328 | tf_op jit(solution)/shard_map/ppermute | solution.py:934
  56.1 10.4 %collective-permute-start.9 = (bf16[280,1120]{1,0:T(8,128)(2,1)S(1)}, bf16[280,1120]{1,0:T(8,128)(2,1)S(1)}, u32[]{:S(2)}, u32[]{:S(2)}) collective-permute-start(bf16[280,1120]{1,0:T(8,128)(2,1)S(1)} %collective-permute-done.8.refs_2_), channel_id=1, source_target_pairs={{0,1},{1,0},{2,3},{3,2},{4,5},{5,4},{6,7},{7,6},{8,9},{9,8},{10,11... | collective-permute-start | bytes 1881608 | tf_op jit(solution)/shard_map/ppermute | solution.py:934
  66.2 9.0 %collective-permute-start.5 = (bf16[280,1024]{1,0:T(8,128)(2,1)S(1)}, bf16[280,1024]{1,0:T(8,128)(2,1)S(1)}, u32[]{:S(2)}, u32[]{:S(2)}) collective-permute-start(bf16[280,1024]{1,0:T(8,128)(2,1)S(1)} %bitcast.43), channel_id=1, source_target_pairs={{0,1},{1,0},{2,3},{3,2},{4,5},{5,4},{6,7},{7,6},{8,9},{9,8},{10,11... | collective-permute-start | bytes 1720328 | tf_op jit(solution)/shard_map/ppermute | solution.py:934
  73.4 30.8 %collective-permute-start.4 = (bf16[280,1024]{1,0:T(8,128)(2,1)S(1)}, bf16[280,1024]{1,0:T(8,128)(2,1)S(1)}, u32[]{:S(2)}, u32[]{:S(2)}) collective-permute-start(bf16[280,1024]{1,0:T(8,128)(2,1)S(1)} %bitcast.46), channel_id=1, source_target_pairs={{0,2},{1,3},{2,0},{3,1},{4,6},{5,7},{6,4},{7,5},{8,10},{9,11},{10,... | collective-permute-start | bytes 1720328 | tf_op jit(solution)/shard_map/ppermute | solution.py:934
  75.2 29.6 %collective-permute-start.3 = (bf16[280,1024]{1,0:T(8,128)(2,1)S(1)}, bf16[280,1024]{1,0:T(8,128)(2,1)}, u32[]{:S(2)}, u32[]{:S(2)}) collective-permute-start(bf16[280,1024]{1,0:T(8,128)(2,1)S(1)} %bitcast.47), channel_id=1, source_target_pairs={{0,1},{1,0},{2,3},{3,2},{4,5},{5,4},{6,7},{7,6},{8,9},{9,8},{10,11... | collective-permute-start | bytes 1720328 | tf_op jit(solution)/shard_map/ppermute | solution.py:934
  75.2 28.2 %collective-permute-start.16 = (bf16[1120,256]{1,0:T(8,128)(2,1)}, bf16[1120,256]{1,0:T(8,128)(2,1)S(1)}, u32[]{:S(2)}, u32[]{:S(2)}) collective-permute-start(bf16[1120,256]{1,0:T(8,128)(2,1)} %get-tuple-element.450.refs_4_), channel_id=1, source_target_pairs={{0,2},{1,3},{2,0},{3,1},{4,6},{5,7},{6,4},{7,5},{8,10},{9,11},{10,... | collective-permute-start | bytes 1720328 | tf_op jit(solution)/shard_map/ppermute | solution.py:934
  75.6 29.2 %collective-permute-start.15 = (bf16[1120,256]{1,0:T(8,128)(2,1)}, bf16[1120,256]{1,0:T(8,128)(2,1)}, u32[]{:S(2)}, u32[]{:S(2)}) collective-permute-start(bf16[1120,256]{1,0:T(8,128)(2,1)} %get-tuple-element.450.refs_4_), channel_id=1, source_target_pairs={{0,1},{1,0},{2,3},{3,2},{4,5},{5,4},{6,7},{7,6},{8,9},{9,8},{10,11... | collective-permute-start | bytes 1720328 | tf_op jit(solution)/shard_map/ppermute | solution.py:934
  135.0 13.6 %collective-permute-start.18 = (bf16[2,1120,512]{2,1,0:T(8,128)(2,1)}, bf16[2,1120,512]{2,1,0:T(8,128)(2,1)S(1)}, u32[]{:S(2)}, u32[]{:S(2)}) collective-permute-start(bf16[2,1120,512]{2,1,0:T(8,128)(2,1)} %get-tuple-element.465), channel_id=1, source_target_pairs={{0,1},{1,0},{2,3},{3,2},{4,5},{5,4},{6,7},{7,6},{8,9},{9,8},{10,11... | collective-permute-start | bytes 6881288 | tf_op jit(solution)/shard_map/ppermute | solution.py:934
  146.9 40.9 %collective-permute-start.21 = (bf16[576,1120]{1,0:T(8,128)(2,1)}, bf16[576,1120]{1,0:T(8,128)(2,1)S(1)}, u32[]{:S(2)}, u32[]{:S(2)}) collective-permute-start(bf16[576,1120]{1,0:T(8,128)(2,1)} %get-tuple-element.479), channel_id=1, source_target_pairs={{0,4},{4,0},{8,12},{12,8},{16,20},{20,16},{24,28},{28,24},{1,5},{5... | collective-permute-start | bytes 3870728 | tf_op jit(solution)/shard_map/ppermute | solution.py:758
  152.5 30.7 %collective-permute-start.19 = (bf16[1120,512]{1,0:T(8,128)(2,1)}, bf16[1120,512]{1,0:T(8,128)(2,1)S(1)}, u32[]{:S(2)}, u32[]{:S(2)}) collective-permute-start(bf16[1120,512]{1,0:T(8,128)(2,1)} %add.105), channel_id=1, source_target_pairs={{0,2},{1,3},{2,0},{3,1},{4,6},{5,7},{6,4},{7,5},{8,10},{9,11},{10,... | collective-permute-start | bytes 3440648 | tf_op jit(solution)/shard_map/ppermute | solution.py:934
  184.2 33.4 %collective-permute-start.24 = (bf16[576,1120]{1,0:T(8,128)(2,1)S(1)}, bf16[576,1120]{1,0:T(8,128)(2,1)S(1)}, u32[]{:S(2)}, u32[]{:S(2)}) collective-permute-start(bf16[576,1120]{1,0:T(8,128)(2,1)S(1)} %copy-done.15), channel_id=1, source_target_pairs={{0,8},{4,12},{8,0},{12,4},{16,24},{20,28},{24,16},{28,20},{1,9},{5... | collective-permute-start | bytes 3870728 | tf_op jit(solution)/shard_map/ppermute | solution.py:758
  194.2 18.4 %collective-permute-start.22 = (bf16[280,1024]{1,0:T(8,128)(2,1)}, bf16[280,1024]{1,0:T(8,128)(2,1)S(1)}, u32[]{:S(2)}, u32[]{:S(2)}) collective-permute-start(bf16[280,1024]{1,0:T(8,128)(2,1)} %add.106), channel_id=1, source_target_pairs={{0,2},{1,3},{2,0},{3,1},{4,6},{5,7},{6,4},{7,5},{8,10},{9,11},{10,... | collective-permute-start | bytes 1720328 | tf_op jit(solution)/shard_map/ppermute | solution.py:934
  213.4 8.3 %collective-permute-start.23 = (bf16[2,280,1024]{2,1,0:T(8,128)(2,1)}, bf16[2,280,1024]{2,1,0:T(8,128)(2,1)S(1)}, u32[]{:S(2)}, u32[]{:S(2)}) collective-permute-start(bf16[2,280,1024]{2,1,0:T(8,128)(2,1)} %get-tuple-element.534), channel_id=1, source_target_pairs={{0,1},{1,0},{2,3},{3,2},{4,5},{5,4},{6,7},{7,6},{8,9},{9,8},{10,11... | collective-permute-start | bytes 3440648 | tf_op jit(solution)/shard_map/ppermute | solution.py:934
  225.0 21.4 %collective-permute-start.26 = (bf16[2,1120,512]{2,1,0:T(8,128)(2,1)}, bf16[2,1120,512]{2,1,0:T(8,128)(2,1)S(1)}, u32[]{:S(2)}, u32[]{:S(2)}) collective-permute-start(bf16[2,1120,512]{2,1,0:T(8,128)(2,1)} %get-tuple-element.541), channel_id=1, source_target_pairs={{0,1},{1,0},{2,3},{3,2},{4,5},{5,4},{6,7},{7,6},{8,9},{9,8},{10,11... | collective-permute-start | bytes 6881288 | tf_op jit(solution)/shard_map/ppermute | solution.py:934
  225.0 17.5 %collective-permute-start.27 = (bf16[288,1120]{1,0:T(8,128)(2,1)}, bf16[288,1120]{1,0:T(8,128)(2,1)S(1)}, u32[]{:S(2)}, u32[]{:S(2)}) collective-permute-start(bf16[288,1120]{1,0:T(8,128)(2,1)} %get-tuple-element.510), channel_id=1, source_target_pairs={{0,8},{4,12},{8,0},{12,4},{16,24},{20,28},{24,16},{28,20},{1,9},{5... | collective-permute-start | bytes 1935368 | tf_op jit(solution)/shard_map/ppermute | solution.py:758
  226.7 56.4 %collective-permute-start.28 = (bf16[288,1120]{1,0:T(8,128)(2,1)}, bf16[288,1120]{1,0:T(8,128)(2,1)S(1)}, u32[]{:S(2)}, u32[]{:S(2)}) collective-permute-start(bf16[288,1120]{1,0:T(8,128)(2,1)} %get-tuple-element.538), channel_id=1, source_target_pairs={{0,4},{4,0},{8,12},{12,8},{16,20},{20,16},{24,28},{28,24},{1,5},{5... | collective-permute-start | bytes 1935368 | tf_op jit(solution)/shard_map/ppermute | solution.py:758
  226.7 24.2 %collective-permute-start.25 = (bf16[280,1024]{1,0:T(8,128)(2,1)}, bf16[280,1024]{1,0:T(8,128)(2,1)}, u32[]{:S(2)}, u32[]{:S(2)}) collective-permute-start(bf16[280,1024]{1,0:T(8,128)(2,1)} %add.107), channel_id=1, source_target_pairs={{0,2},{1,3},{2,0},{3,1},{4,6},{5,7},{6,4},{7,5},{8,10},{9,11},{10,... | collective-permute-start | bytes 1720328 | tf_op jit(solution)/shard_map/ppermute | solution.py:934
  245.6 33.0 %collective-permute-start.29 = (bf16[144,1120]{1,0:T(8,128)(2,1)}, bf16[144,1120]{1,0:T(8,128)(2,1)}, u32[]{:S(2)}, u32[]{:S(2)}) collective-permute-start(bf16[144,1120]{1,0:T(8,128)(2,1)} %get-tuple-element.545), channel_id=1, source_target_pairs={{0,16},{4,20},{8,24},{12,28},{16,0},{20,4},{24,8},{28,12},{1,17},{... | collective-permute-start | bytes 967688 | tf_op jit(solution)/shard_map/ppermute | solution.py:758
  250.3 36.2 %collective-permute-start.30 = (bf16[1120,512]{1,0:T(8,128)(2,1)}, bf16[1120,512]{1,0:T(8,128)(2,1)S(1)}, u32[]{:S(2)}, u32[]{:S(2)}) collective-permute-start(bf16[1120,512]{1,0:T(8,128)(2,1)} %add.108), channel_id=1, source_target_pairs={{0,2},{1,3},{2,0},{3,1},{4,6},{5,7},{6,4},{7,5},{8,10},{9,11},{10,... | collective-permute-start | bytes 3440648 | tf_op jit(solution)/shard_map/ppermute | solution.py:934
  280.5 26.1 %collective-permute-start.33 = (bf16[144,1120]{1,0:T(8,128)(2,1)}, bf16[144,1120]{1,0:T(8,128)(2,1)S(1)}, u32[]{:S(2)}, u32[]{:S(2)}) collective-permute-start(bf16[144,1120]{1,0:T(8,128)(2,1)} %add.109.refs_0_.one), channel_id=1, source_target_pairs={{0,16},{4,20},{8,24},{12,28},{16,0},{20,4},{24,8},{28,12},{1,17},{... | collective-permute-start | bytes 967688 | tf_op jit(solution)/shard_map/ppermute | solution.py:758
  286.2 25.7 %collective-permute-start.32 = (bf16[144,1120]{1,0:T(8,128)(2,1)}, bf16[144,1120]{1,0:T(8,128)(2,1)S(1)}, u32[]{:S(2)}, u32[]{:S(2)}) collective-permute-start(bf16[144,1120]{1,0:T(8,128)(2,1)} %get-tuple-element.572), channel_id=1, source_target_pairs={{0,16},{4,20},{8,24},{12,28},{16,0},{20,4},{24,8},{28,12},{1,17},{... | collective-permute-start | bytes 967688 | tf_op jit(solution)/shard_map/ppermute | solution.py:758
  328.3 32.0 %collective-permute-start.34 = (bf16[2,1120,512]{2,1,0:T(8,128)(2,1)}, bf16[2,1120,512]{2,1,0:T(8,128)(2,1)S(1)}, u32[]{:S(2)}, u32[]{:S(2)}) collective-permute-start(bf16[2,1120,512]{2,1,0:T(8,128)(2,1)} %get-tuple-element.589), channel_id=1, source_target_pairs={{0,1},{1,0},{2,3},{3,2},{4,5},{5,4},{6,7},{7,6},{8,9},{9,8},{10,11... | collective-permute-start | bytes 6881288 | tf_op jit(solution)/shard_map/ppermute | solution.py:934
  328.3 24.6 %collective-permute-start.36 = (bf16[288,1120]{1,0:T(8,128)(2,1)}, bf16[288,1120]{1,0:T(8,128)(2,1)S(1)}, u32[]{:S(2)}, u32[]{:S(2)}) collective-permute-start(bf16[288,1120]{1,0:T(8,128)(2,1)} %stack.38), channel_id=1, source_target_pairs={{0,8},{4,12},{8,0},{12,4},{16,24},{20,28},{24,16},{28,20},{1,9},{5... | collective-permute-start | bytes 1935368 | tf_op jit(solution)/shard_map/ppermute | solution.py:758
  329.1 27.3 %collective-permute-start.35 = (bf16[144,1120]{1,0:T(8,128)(2,1)}, bf16[144,1120]{1,0:T(8,128)(2,1)}, u32[]{:S(2)}, u32[]{:S(2)}) collective-permute-start(bf16[144,1120]{1,0:T(8,128)(2,1)} %add.110.refs_0_.one), channel_id=1, source_target_pairs={{0,16},{4,20},{8,24},{12,28},{16,0},{20,4},{24,8},{28,12},{1,17},{... | collective-permute-start | bytes 967688 | tf_op jit(solution)/shard_map/ppermute | solution.py:758
  332.3 33.2 %collective-permute-start.31 = (bf16[448,1120]{1,0:T(8,128)(2,1)S(1)}, bf16[448,1120]{1,0:T(8,128)(2,1)}, u32[]{:S(2)}, u32[]{:S(2)}) collective-permute-start(bf16[448,1120]{1,0:T(8,128)(2,1)S(1)} %copy-done.24), channel_id=1, source_target_pairs={{0,4},{4,0},{8,12},{12,8},{16,20},{20,16},{24,28},{28,24},{1,5},{5... | collective-permute-start | bytes 3010568 | tf_op jit(solution)/shard_map/ppermute | solution.py:758
  356.2 59.3 %collective-permute-start.40 = (bf16[576,1120]{1,0:T(8,128)(2,1)}, bf16[576,1120]{1,0:T(8,128)(2,1)}, u32[]{:S(2)}, u32[]{:S(2)}) collective-permute-start(bf16[576,1120]{1,0:T(8,128)(2,1)} %stack.39), channel_id=1, source_target_pairs={{0,4},{4,0},{8,12},{12,8},{16,20},{20,16},{24,28},{28,24},{1,5},{5... | collective-permute-start | bytes 3870728 | tf_op jit(solution)/shard_map/ppermute | solution.py:758
  358.3 43.2 %collective-permute-start.38 = (bf16[288,1120]{1,0:T(8,128)(2,1)}, bf16[288,1120]{1,0:T(8,128)(2,1)}, u32[]{:S(2)}, u32[]{:S(2)}) collective-permute-start(bf16[288,1120]{1,0:T(8,128)(2,1)} %stack.40), channel_id=1, source_target_pairs={{0,4},{4,0},{8,12},{12,8},{16,20},{20,16},{24,28},{28,24},{1,5},{5... | collective-permute-start | bytes 1935368 | tf_op jit(solution)/shard_map/ppermute | solution.py:758
  364.2 51.3 %collective-permute-start.39 = (bf16[1120,512]{1,0:T(8,128)(2,1)}, bf16[1120,512]{1,0:T(8,128)(2,1)}, u32[]{:S(2)}, u32[]{:S(2)}) collective-permute-start(bf16[1120,512]{1,0:T(8,128)(2,1)} %add.111), channel_id=1, source_target_pairs={{0,2},{1,3},{2,0},{3,1},{4,6},{5,7},{6,4},{7,5},{8,10},{9,11},{10,... | collective-permute-start | bytes 3440648 | tf_op jit(solution)/shard_map/ppermute | solution.py:934
  368.2 35.9 %collective-permute-start.37 = (bf16[224,1120]{1,0:T(8,128)(2,1)}, bf16[224,1120]{1,0:T(8,128)(2,1)}, u32[]{:S(2)}, u32[]{:S(2)}) collective-permute-start(bf16[224,1120]{1,0:T(8,128)(2,1)} %get-tuple-element.600), channel_id=1, source_target_pairs={{0,8},{4,12},{8,0},{12,4},{16,24},{20,28},{24,16},{28,20},{1,9},{5... | collective-permute-start | bytes 1505288 | tf_op jit(solution)/shard_map/ppermute | solution.py:758
  415.5 17.8 %collective-permute-start.41 = (bf16[2,280,1120]{2,1,0:T(8,128)(2,1)}, bf16[2,280,1120]{2,1,0:T(8,128)(2,1)}, u32[]{:S(2)}, u32[]{:S(2)}) collective-permute-start(bf16[2,280,1120]{2,1,0:T(8,128)(2,1)} %get-tuple-element.636), channel_id=1, source_target_pairs={{0,1},{1,0},{2,3},{3,2},{4,5},{5,4},{6,7},{7,6},{8,9},{9,8},{10,11... | collective-permute-start | bytes 3763208 | tf_op jit(solution)/shard_map/ppermute | solution.py:934
  415.6 15.2 %collective-permute-start.42 = (bf16[112,1120]{1,0:T(8,128)(2,1)S(1)}, bf16[112,1120]{1,0:T(8,128)(2,1)S(1)}, u32[]{:S(2)}, u32[]{:S(2)}) collective-permute-start(bf16[112,1120]{1,0:T(8,128)(2,1)S(1)} %copy-done.50), channel_id=1, source_target_pairs={{0,16},{4,20},{8,24},{12,28},{16,0},{20,4},{24,8},{28,12},{1,17},{... | collective-permute-start | bytes 752648 | tf_op jit(solution)/shard_map/ppermute | solution.py:758
  417.1 50.5 %collective-permute-start.47 = (bf16[576,1120]{1,0:T(8,128)(2,1)S(1)}, bf16[576,1120]{1,0:T(8,128)(2,1)S(1)}, u32[]{:S(2)}, u32[]{:S(2)}) collective-permute-start(bf16[576,1120]{1,0:T(8,128)(2,1)S(1)} %copy-done.13), channel_id=1, source_target_pairs={{0,8},{4,12},{8,0},{12,4},{16,24},{20,28},{24,16},{28,20},{1,9},{5... | collective-permute-start | bytes 3870728 | tf_op jit(solution)/shard_map/ppermute | solution.py:758
  433.3 25.2 %collective-permute-start.45 = (bf16[112,1120]{1,0:T(8,128)(2,1)}, bf16[112,1120]{1,0:T(8,128)(2,1)S(1)}, u32[]{:S(2)}, u32[]{:S(2)}) collective-permute-start(bf16[112,1120]{1,0:T(8,128)(2,1)} %add.115.refs_0_.one), channel_id=1, source_target_pairs={{0,16},{4,20},{8,24},{12,28},{16,0},{20,4},{24,8},{28,12},{1,17},{... | collective-permute-start | bytes 752648 | tf_op jit(solution)/shard_map/ppermute | solution.py:758
  435.5 16.2 %collective-permute-start.43 = (bf16[280,1120]{1,0:T(8,128)(2,1)}, bf16[280,1120]{1,0:T(8,128)(2,1)S(1)}, u32[]{:S(2)}, u32[]{:S(2)}) collective-permute-start(bf16[280,1120]{1,0:T(8,128)(2,1)} %add.116), channel_id=1, source_target_pairs={{0,2},{1,3},{2,0},{3,1},{4,6},{5,7},{6,4},{7,5},{8,10},{9,11},{10,... | collective-permute-start | bytes 1881608 | tf_op jit(solution)/shard_map/ppermute | solution.py:934
  461.0 29.1 %collective-permute-start.49 = (bf16[224,1120]{1,0:T(8,128)(2,1)}, bf16[224,1120]{1,0:T(8,128)(2,1)}, u32[]{:S(2)}, u32[]{:S(2)}) collective-permute-start(bf16[224,1120]{1,0:T(8,128)(2,1)} %stack.42), channel_id=1, source_target_pairs={{0,8},{4,12},{8,0},{12,4},{16,24},{20,28},{24,16},{28,20},{1,9},{5... | collective-permute-start | bytes 1505288 | tf_op jit(solution)/shard_map/ppermute | solution.py:758
  466.2 9.7 %collective-permute-start.46 = (f32[8,1120]{1,0:T(8,128)}, f32[8,1120]{1,0:T(8,128)S(1)}, u32[]{:S(2)}, u32[]{:S(2)}) collective-permute-start(f32[8,1120]{1,0:T(8,128)} %add.117.refs_0_), channel_id=1, source_target_pairs={{0,8},{4,12},{8,0},{12,4},{16,24},{20,28},{24,16},{28,20},{1,9},{5... | collective-permute-start | bytes 107528 | tf_op jit(solution)/shard_map/ppermute | solution.py:758
  470.6 15.6 %collective-permute-start.50 = (bf16[280,1120]{1,0:T(8,128)(2,1)}, bf16[280,1120]{1,0:T(8,128)(2,1)S(1)}, u32[]{:S(2)}, u32[]{:S(2)}) collective-permute-start(bf16[280,1120]{1,0:T(8,128)(2,1)} %add.118.refs_0_), channel_id=1, source_target_pairs={{0,4},{4,0},{8,12},{12,8},{16,20},{20,16},{24,28},{28,24},{1,5},{5... | collective-permute-start | bytes 1881608 | tf_op jit(solution)/shard_map/ppermute | solution.py:758
  477.9 14.5 %collective-permute-start.48 = (f32[8,1120]{1,0:T(8,128)}, f32[8,1120]{1,0:T(8,128)S(1)}, u32[]{:S(2)}, u32[]{:S(2)}) collective-permute-start(f32[8,1120]{1,0:T(8,128)} %add.119.refs_0_), channel_id=1, source_target_pairs={{0,16},{4,20},{8,24},{12,28},{16,0},{20,4},{24,8},{28,12},{1,17},{... | collective-permute-start | bytes 107528 | tf_op jit(solution)/shard_map/ppermute | solution.py:758
  489.3 14.7 %collective-permute-start.52 = (bf16[280,1120]{1,0:T(8,128)(2,1)}, bf16[280,1120]{1,0:T(8,128)(2,1)S(1)}, u32[]{:S(2)}, u32[]{:S(2)}) collective-permute-start(bf16[280,1120]{1,0:T(8,128)(2,1)} %add.120.refs_0_), channel_id=1, source_target_pairs={{0,8},{4,12},{8,0},{12,4},{16,24},{20,28},{24,16},{28,20},{1,9},{5... | collective-permute-start | bytes 1881608 | tf_op jit(solution)/shard_map/ppermute | solution.py:758
  507.1 28.5 %collective-permute-start.54 = (bf16[280,1120]{1,0:T(8,128)(2,1)}, bf16[280,1120]{1,0:T(8,128)(2,1)S(1)}, u32[]{:S(2)}, u32[]{:S(2)}) collective-permute-start(bf16[280,1120]{1,0:T(8,128)(2,1)} %add.122.refs_0_), channel_id=1, source_target_pairs={{0,16},{4,20},{8,24},{12,28},{16,0},{20,4},{24,8},{28,12},{1,17},{... | collective-permute-start | bytes 1881608 | tf_op jit(solution)/shard_map/ppermute | solution.py:758
  509.1 33.5 %collective-permute-start.55 = (bf16[448,1120]{1,0:T(8,128)(2,1)S(1)}, bf16[448,1120]{1,0:T(8,128)(2,1)S(1)}, u32[]{:S(2)}, u32[]{:S(2)}) collective-permute-start(bf16[448,1120]{1,0:T(8,128)(2,1)S(1)} %copy-done.25), channel_id=1, source_target_pairs={{0,4},{4,0},{8,12},{12,8},{16,20},{20,16},{24,28},{28,24},{1,5},{5... | collective-permute-start | bytes 3010568 | tf_op jit(solution)/shard_map/ppermute | solution.py:758
  512.7 26.1 %collective-permute-start.53 = (f32[8,1120]{1,0:T(8,128)}, f32[8,1120]{1,0:T(8,128)S(1)}, u32[]{:S(2)}, u32[]{:S(2)}) collective-permute-start(f32[8,1120]{1,0:T(8,128)} %add.123.refs_0_), channel_id=1, source_target_pairs={{0,2},{1,3},{2,0},{3,1},{4,6},{5,7},{6,4},{7,5},{8,10},{9,11},{10,... | collective-permute-start | bytes 107528 | tf_op jit(solution)/shard_map/ppermute | solution.py:934
  (66 other events, 313.9 us)

commit v3 on v2

--- a/solution.py
+++ b/solution.py
@@ -26,7 +26,7 @@
 VEC8 = True
 ATT_PIECES = True
 VMEM = 60 << 20
-PACE = 2.3e9
+PACE = 0.0
 
 
 def dot(a, b, dims=((1,), (0,))):
@@ -38,7 +38,7 @@
 
 
 def cost(microseconds):
-    return pl.CostEstimate(flops=int(microseconds * PACE), bytes_accessed=1, transcendentals=0)
+    return pl.CostEstimate(flops=max(1, int(microseconds * PACE)), bytes_accessed=1, transcendentals=0)
 
 
 def fold(v):
@@ -366,7 +366,7 @@
     for c in range(chunks):
         a, near, far, o, lse = refs[5 * c : 5 * c + 5]
         cut = slice(c * wide, (c + 1) * wide)
-        do = (a[0].astype(F32) + near[0, 0].astype(F32) + far[0].astype(F32)).astype(BF16)
+        do = (a[0].astype(F32) + near[0].astype(F32) + far[0].astype(F32)).astype(BF16)
         do_out[0, :, cut] = do
         stat_out[pl.ds(h + 8, 1), cut] = jnp.sum(o[0].astype(F32) * do.astype(F32), axis=0, keepdims=True)
 
@@ -383,14 +383,14 @@
     for a, near, far, o, lse in parts:
         args += [
             a.reshape(heads, HEAD_DIM, wide),
-            near.reshape(2, heads, HEAD_DIM, wide),
+            near.reshape(heads, HEAD_DIM, wide),
             far.reshape(heads, HEAD_DIM, wide),
             o,
             lse,
         ]
         in_specs += [
             block,
-            pl.BlockSpec((1, 1, HEAD_DIM, wide), lambda h: (0, h, 0, 0)),
+            block,
             block,
             block,
             pl.BlockSpec((8, wide), lambda h: (0, 0)),
@@ -408,12 +408,11 @@
 
 
 def to_slot(s, value_ref, outs):
-    places = (outs[0], outs[2].at[0], outs[1], outs[2].at[1])
     for k in range(SLOTS):
 
         @pl.when(s == k)
         def _():
-            places[k][...] = value_ref[...]
+            outs[k][...] = value_ref[...]
 
 
 def add_to(first, ref, at, m, part):
@@ -424,8 +423,8 @@
     att_refs, refs = refs[:SLOTS], refs[SLOTS:]
     g_refs = refs[:SLOTS]
     wot, upt, wd, wdt, vec_ref = refs[SLOTS : SLOTS + 5]
-    h_out, act_out, pg_out, g_out, n_out, root_out, sum_out, own_out = refs[-13:-5]
-    layer_outs = refs[-5:-2]
+    h_out, act_out, pg_out, g_out, n_out, root_out, sum_out, own_out = refs[-14:-6]
+    layer_outs = refs[-6:-2]
     y1_s, layer_s = refs[-2:]
     s = pl.program_id(0)
     for k in range(SLOTS):
@@ -505,11 +504,8 @@
             block(d),
             block(8),
             pl.BlockSpec((1, f, 128), lambda s, i: (0, 0, 0)),
-            mine,
-            mine,
-            mine,
-            pl.BlockSpec((2, d, BLK), lambda s, i: (0, 0, chunk)),
-        ],
+        ]
+        + [mine] * 5,
         scratch_shapes=[pltpu.VMEM((d, BLK), F32), pltpu.VMEM((d, BLK), BF16)],
     )
     shape = jax.ShapeDtypeStruct
@@ -526,10 +522,8 @@
             shape((8, wide), F32),
             shape((1, f, 128), F32),
             shape((d, rows), F32),
-            shape((d, rows), BF16),
-            shape((d, rows), BF16),
-            shape((2, d, rows), BF16),
-        ],
+        ]
+        + [shape((d, rows), BF16)] * SLOTS,
         input_output_aliases=alias,
         compiler_params=params(),
         cost_estimate=cost(26),
@@ -540,9 +534,9 @@
 def backward_kernel(info, pg_ref, n_ref, root_ref, g_ref, up, *refs):
     wo = refs[:SLOTS]
     vec_ref = refs[SLOTS]
-    sum_out, attg0_out, attg2_out, attg_side = refs[-9:-5]
-    attg_outs = (attg0_out, attg_side.at[0], attg2_out, attg_side.at[1])
-    y1g_outs = refs[-5:-2]
+    sum_out = refs[-11]
+    attg_outs = refs[-10:-6]
+    y1g_outs = refs[-6:-2]
     e_s, y1g_s = refs[-2:]
     s = pl.program_id(0)
     d = n_ref.shape[0]
@@ -588,37 +582,21 @@
     in_specs = [block(f), block(d), block(8), mine] + [keep(a) for a in (up, *wos, vec)]
     alias = {}
     if carry is not None:
-        alias = {len(args) + n: 4 + n for n in range(len(carry))}
+        alias = {len(args) + n: 5 + n for n in range(len(carry))}
         in_specs += [pl.BlockSpec(memory_space=pl.ANY)] * len(carry)
         args += list(carry)
     spec = pltpu.PrefetchScalarGridSpec(
         num_scalar_prefetch=1,
         grid=(SLOTS,),
         in_specs=in_specs,
-        out_specs=[
-            pl.BlockSpec((3, d, 128), lambda s, i: (0, 0, 0)),
-            ordered,
-            ordered,
-            pl.BlockSpec((2, rows, BLK), lambda s, i: (0, 0, s ^ i[dev])),
-            mine,
-            mine,
-            pl.BlockSpec((2, d, BLK), lambda s, i: (0, 0, chunk)),
-        ],
+        out_specs=[pl.BlockSpec((3, d, 128), lambda s, i: (0, 0, 0))] + [ordered] * SLOTS + [mine] * SLOTS,
         scratch_shapes=[pltpu.VMEM((d, BLK), F32), pltpu.VMEM((d, BLK), BF16)],
     )
     shape = jax.ShapeDtypeStruct
     return pl.pallas_call(
         backward_kernel,
         grid_spec=spec,
-        out_shape=[
-            shape((3, d, 128), F32),
-            shape((rows, wide), BF16),
-            shape((rows, wide), BF16),
-            shape((2, rows, wide), BF16),
-            shape((d, g.shape[1]), BF16),
-            shape((d, g.shape[1]), BF16),
-            shape((2, d, g.shape[1]), BF16),
-        ],
+        out_shape=[shape((3, d, 128), F32)] + [shape((rows, wide), BF16)] * SLOTS + [shape(g.shape, BF16)] * SLOTS,
         input_output_aliases=alias,
         compiler_params=params(),
         cost_estimate=cost(17),
@@ -630,35 +608,34 @@
     return -(-m // (8 * 16)) * 16
 
 
-def outer_kernel(count, order, with_sum, info, *refs):
+def outer_kernel(count, order, with_sum, with_extra, info, *refs):
     dp = info[0]
     i = pl.program_id(0)
-    outs = refs[2 * count :]
+    extra, outs = refs[2 * count : 2 * count + with_extra], refs[2 * count + with_extra :]
     total = None
     for n in range(count):
         part = dot(refs[2 * n][...], refs[2 * n + 1][...], NT)
         total = part if total is None else total + part
     size = total.shape[0] // 2
+    shard = size * (1 + with_extra)
     for half in range(2):
         slot = (2 * i) ^ (dp & 1) ^ half
         at = jnp.where((slot & order[2]) != 0, 1, 0) + jnp.where((slot & order[1]) != 0, 2, 0)
-        rows = pl.ds(pl.multiple_of(at * size, size), size)
-        value = total[half * size : (half + 1) * size].astype(BF16)
+        values = [total[half * size : (half + 1) * size].astype(BF16)]
+        values += [ref[half * size : (half + 1) * size] for ref in extra]
         goes = (slot & order[0]) != 0
-
-        @pl.when(goes)
-        def _():
-            outs[1][rows] = value
-
-        @pl.when(jnp.logical_not(goes))
-        def _():
-            outs[0][rows] = value
+        for k, out in enumerate(outs[:2]):
+
+            @pl.when(goes if k else jnp.logical_not(goes))
+            def _():
+                for n, value in enumerate(values):
+                    out[pl.ds(pl.multiple_of(at * shard + n * size, 16), size)] = value
 
     if with_sum:
         outs[2][...] = fold(refs[0][...].astype(F32))
 
 
-def outer(pairs, info, order, first=0, rows=None, with_sum=False):
+def outer(pairs, info, order, first=0, rows=None, with_sum=False, extra=None):
     m, depth = pairs[0][0].shape
     n = pairs[0][1].shape[0]
     rows = m if rows is None else rows
@@ -669,19 +646,49 @@
         in_specs.append(pl.BlockSpec((2 * size, depth), lambda i, s: (skip + (i ^ (s[0] >> 1)), 0)))
         in_specs.append(pl.BlockSpec((n, depth), lambda i, s: (0, 0), pipeline_mode=pl.Buffered(1)))
         args += [a, b]
-    out_specs = [pl.BlockSpec((4 * size, n), lambda i, s: (0, 0))] * 2
-    out_shape = [jax.ShapeDtypeStruct((4 * size, n), BF16)] * 2
+    both = 0 if extra is None else 1
+    if both:
+        last = -(-extra.shape[0] // (2 * size)) - 1
+        in_specs.append(pl.BlockSpec((2 * size, n), lambda i, s: (jnp.minimum(i ^ (s[0] >> 1), last), 0)))
+        args.append(extra)
+    out_specs = [pl.BlockSpec((4 * size * (1 + both), n), lambda i, s: (0, 0))] * 2
+    out_shape = [jax.ShapeDtypeStruct((4 * size * (1 + both), n), BF16)] * 2
     if with_sum:
         out_specs.append(pl.BlockSpec((2 * size, 128), lambda i, s: (i ^ (s[0] >> 1), 0)))
         out_shape.append(jax.ShapeDtypeStruct((8 * size, 128), F32))
     return pl.pallas_call(
-        functools.partial(outer_kernel, len(pairs), order, with_sum),
+        functools.partial(outer_kernel, len(pairs), order, with_sum, both),
         grid_spec=pltpu.PrefetchScalarGridSpec(num_scalar_prefetch=1, grid=(4,), in_specs=in_specs, out_specs=out_specs),
         out_shape=out_shape,
         compiler_params=params(),
         cost_estimate=cost(11),
         name="outer",
     )(info, *args)
+
+
+def attn_grad_kernel(a_ref, b_ref, out_ref, sum_ref):
+    a = a_ref[...]
+    out_ref[...] = dot(a, b_ref[...], NT).astype(BF16)
+    sum_ref[...] = fold(a.astype(F32))
+
+
+def attn_grad_call(dqkv, h1):
+    m, total = dqkv.shape
+    d = h1.shape[0]
+    rows = m // 3
+    return pl.pallas_call(
+        attn_grad_kernel,
+        grid=(3,),
+        in_specs=[
+            pl.BlockSpec((rows, total), lambda i: (i, 0)),
+            pl.BlockSpec((d, total), lambda i: (0, 0), pipeline_mode=pl.Buffered(1)),
+        ],
+        out_specs=[pl.BlockSpec((rows, d), lambda i: (i, 0)), pl.BlockSpec((rows, 128), lambda i: (i, 0))],
+        out_shape=[jax.ShapeDtypeStruct((m, d), BF16), jax.ShapeDtypeStruct((m, 128), F32)],
+        compiler_params=params(),
+        cost_estimate=cost(9),
+        name="attn_grad_call",
+    )(dqkv, h1)
 
 
 def halve_kernel(keep_ref, recv_ref, keep_out, send_out):
@@ -716,19 +723,23 @@
     return jnp.where(i & 1, order[2], 0) | jnp.where(i & 2, order[1], 0) | jnp.where(i & 4, order[0], 0)
 
 
-def place_kernel(info, one, two, four, eight, *rest):
+def place_kernel(count, info, one, two, four, eight, *rest):
     i = pl.program_id(0)
-    out = rest[-1]
+    outs = rest[-count:]
     for ref, low, high in ((one, 0, 1), (two, 1, 2), (four, 2, 4), (eight, 4, 8)):
 
         @pl.when((i >= low) & (i < high))
         def _():
-            out[...] = ref[...].astype(F32)
-
-
-def place(parts, info, order, first, rows, carry):
+            size = ref.shape[0] // count
+            for n, out in enumerate(outs):
+                out[...] = ref[n * size : (n + 1) * size].astype(F32)
+
+
+def place(parts, info, order, first, rows, carry, extra_rows):
     size, n = parts[0].shape
-    start = first // size
+    count = 2 if extra_rows else 1
+    half = size // count
+    start = first // half
     near = lambda at, many: pl.BlockSpec((size, n), lambda i, s: (jnp.clip(i - at, 0, many - 1), 0))
     in_specs = [near(0, 1), near(1, 1), near(2, 2), near(4, 4)]
     args = list(parts)
@@ -737,21 +748,22 @@
         in_specs.append(pl.BlockSpec(memory_space=pl.ANY))
         args.append(carry)
         alias = {5: 0}
-    spec = pltpu.PrefetchScalarGridSpec(
-        num_scalar_prefetch=1,
-        grid=(8,),
-        in_specs=in_specs,
-        out_specs=pl.BlockSpec((size, n), lambda i, s: (start + (slot_of(i, order) ^ s[0]), 0)),
-    )
-    return pl.pallas_call(
-        place_kernel,
+    out_specs = [pl.BlockSpec((half, n), lambda i, s: (start + (slot_of(i, order) ^ s[0]), 0))]
+    out_shape = [jax.ShapeDtypeStruct((rows, n), F32)]
+    if extra_rows:
+        out_specs.append(pl.BlockSpec((half, n), lambda i, s: (slot_of(i, order) ^ s[0], 0)))
+        out_shape.append(jax.ShapeDtypeStruct((8 * half, n), F32))
+    spec = pltpu.PrefetchScalarGridSpec(num_scalar_prefetch=1, grid=(8,), in_specs=in_specs, out_specs=out_specs)
+    out = pl.pallas_call(
+        functools.partial(place_kernel, count),
         grid_spec=spec,
-        out_shape=jax.ShapeDtypeStruct((rows, n), F32),
+        out_shape=out_shape,
         input_output_aliases=alias,
         compiler_params=params(),
         cost_estimate=cost(6.5),
         name="place",
     )(info, *args)
+    return (out[0], out[1][:extra_rows]) if extra_rows else out[0]
 
 
 def swap_dp(v, k):
@@ -759,9 +771,9 @@
 
 
 class CellSum:
-    def __init__(self, line, keep, send, info, order, rows, first=0):
+    def __init__(self, line, keep, send, info, order, rows, first=0, extra_rows=0):
         self.line, self.keep, self.info, self.order = line, keep, info, order
-        self.rows, self.first = rows, first
+        self.rows, self.first, self.extra_rows = rows, first, extra_rows
         self.stage = 0
         self.known = lax.axis_size("dp") == 8
         if not self.known:
@@ -791,7 +803,9 @@
 
     def finish(self, carry=None):
         return self.line(
-            lambda p, *c: place(p, self.info, self.order, self.first, self.rows, *(c or (None,))),
+            lambda p, *c: place(
+                p, self.info, self.order, self.first, self.rows, c[0] if c else None, self.extra_rows
+            ),
             self.parts,
             *([] if carry is None else [carry]),
         )
@@ -824,37 +838,42 @@
         self.send()
 
 
-def out_grad_kernel(count, info, *refs):
-    atts, y1gs, outs = refs[: count * SLOTS], refs[count * SLOTS : count * (SLOTS + 1)], refs[count * (SLOTS + 1) :]
-    for k in range(SLOTS):
-        total = None
-        for n in range(count):
-            part = dot(atts[n * SLOTS + k][...], y1gs[n][...], NT)
-            total = part if total is None else total + part
-        (outs[0], outs[2].at[0], outs[1], outs[2].at[1])[k][...] = total.astype(BF16)
-
-
-def out_grad_call(info, atts, y1g):
+def out_grad_kernel(chunks, info, *refs):
+    k = pl.program_id(0)
+    atts, y1gs, outs = refs[: chunks * SLOTS], refs[chunks * SLOTS : -SLOTS], refs[-SLOTS:]
+    dev = info[3 * y1gs[0].shape[1] * SLOTS // BLK]
+    for n in range(SLOTS):
+
+        @pl.when(k == n)
+        def _():
+            total = None
+            for c in range(chunks):
+                for s in range(SLOTS):
+                    at = pl.multiple_of((s ^ dev) * BLK, BLK)
+                    y1g = y1gs[s][:, c * BLK : (c + 1) * BLK]
+                    part = dot(atts[c * SLOTS + n][:, pl.ds(at, BLK)], y1g, NT)
+                    total = part if total is None else total + part
+            outs[n][...] = total.astype(BF16)
+
+
+def out_grad_call(info, atts, y1gs):
     rows = atts[0][0].shape[0]
-    d = y1g.shape[0]
-    count = len(atts)
-    dev = info.shape[0] - 1
-    in_specs = [pl.BlockSpec((rows, BLK), lambda i, s: (0, s[dev]))] * (count * SLOTS)
-    in_specs += [pl.BlockSpec((d, BLK), functools.partial(lambda at, i, s: (0, at), n)) for n in range(count)]
+    d = y1gs[0].shape[0]
+    arrays = [a for chunk in atts for a in chunk] + list(y1gs)
     spec = pltpu.PrefetchScalarGridSpec(
         num_scalar_prefetch=1,
-        grid=(1,),
-        in_specs=in_specs,
-        out_specs=[pl.BlockSpec((rows, d), lambda i, s: (0, 0))] * 2 + [pl.BlockSpec((2, rows, d), lambda i, s: (0, 0, 0))],
+        grid=(SLOTS,),
+        in_specs=[pl.BlockSpec(a.shape, lambda k, s: (0, 0), pipeline_mode=pl.Buffered(1)) for a in arrays],
+        out_specs=[pl.BlockSpec((rows, d), lambda k, s: (0, 0))] * SLOTS,
     )
     return pl.pallas_call(
-        functools.partial(out_grad_kernel, count),
+        functools.partial(out_grad_kernel, len(atts)),
         grid_spec=spec,
-        out_shape=[jax.ShapeDtypeStruct((rows, d), BF16)] * 2 + [jax.ShapeDtypeStruct((2, rows, d), BF16)],
-        compiler_params=params(),
-        cost_estimate=cost(5),
+        out_shape=[jax.ShapeDtypeStruct((rows, d), BF16)] * SLOTS,
+        compiler_params=params(),
+        cost_estimate=cost(12),
         name="out_grad_call",
-    )(info, *[a for chunk in atts for a in chunk], *[y1g] * count)
+    )(info, *arrays)
 
 
 def h1_grad_kernel(w_ref, dqkv_ref, x_ref, sum_ref, *outs):
@@ -879,7 +898,7 @@
         hg_s[m] = hg.astype(BF16)
         add_to(first, sum_ref, 0, m, fold(hg * n))
         add_to(first, sum_ref, 1, m, fold(hg))
-    to_slot(s, hg_s, outs[:3])
+    to_slot(s, hg_s, outs[:SLOTS])
 
 
 def h1_grad_call(w, dqkv, x):
@@ -888,7 +907,6 @@
     m = w.shape[1]
     at = lambda p, s: (0, p * SLOTS + s)
     mine = pl.BlockSpec((d, BLK), lambda p, s: (0, p))
-    side = pl.BlockSpec((2, d, BLK), lambda p, s: (0, 0, p))
     return pl.pallas_call(
         h1_grad_kernel,
         grid=(per, SLOTS),
@@ -897,10 +915,9 @@
             pl.BlockSpec((m, BLK), at),
             pl.BlockSpec((d, BLK), at),
         ],
-        out_specs=[pl.BlockSpec((2, d, 128), lambda p, s: (0, 0, 0)), mine, mine, side],
+        out_specs=[pl.BlockSpec((2, d, 128), lambda p, s: (0, 0, 0))] + [mine] * SLOTS,
         out_shape=[jax.ShapeDtypeStruct((2, d, 128), F32)]
-        + [jax.ShapeDtypeStruct((d, per * BLK), BF16)] * 2
-        + [jax.ShapeDtypeStruct((2, d, per * BLK), BF16)],
+        + [jax.ShapeDtypeStruct((d, per * BLK), BF16)] * SLOTS,
         scratch_shapes=[pltpu.VMEM((d, BLK), BF16)],
         compiler_params=params(),
         cost_estimate=cost(13),
@@ -908,26 +925,69 @@
     )(w, dqkv, x)
 
 
-def input_grad_kernel(x_ref, a_ref, b_ref, y1g_ref, gain_ref, out_ref):
+def input_grad_kernel(x_ref, a_ref, b_ref, c_ref, d_ref, y1g_ref, gain_ref, out_ref):
     n, root = normal(x_ref[...].astype(F32))
-    e = (a_ref[...] + b_ref[...].astype(F32)) * gain_ref[:, GAIN1 : GAIN1 + 1]
+    total = a_ref[...].astype(F32) + b_ref[...].astype(F32) + c_ref[...].astype(F32) + d_ref[...].astype(F32)
+    e = total * gain_ref[:, GAIN1 : GAIN1 + 1]
     e = root * (e - jnp.mean(e, axis=0, keepdims=True) - n * jnp.mean(e * n, axis=0, keepdims=True))
     out_ref[...] = (y1g_ref[...] + e).astype(BF16)
 
 
-def input_grad_call(x, a, b, y1g, gain):
+def input_grad_call(x, a, b, c, d4, y1g, gain):
     d, rows = x.shape
     block = pl.BlockSpec((d, 128), lambda i: (0, i))
     return pl.pallas_call(
         input_grad_kernel,
         grid=(rows // 128,),
-        in_specs=[block] * 4 + [pl.BlockSpec(gain.shape, lambda i: (0, 0))],
+        in_specs=[block] * 6 + [pl.BlockSpec(gain.shape, lambda i: (0, 0))],
         out_specs=block,
         out_shape=jax.ShapeDtypeStruct((d, rows), BF16),
         compiler_params=params(),
         cost_estimate=cost(6),
         name="input_grad_call",
-    )(x, a, b, y1g, gain)
+    )(x, a, b, c, d4, y1g, gain)
+
+
+def layer_kernel(own_ref, a_ref, b_ref, c_ref, vec_ref, out_ref):
+    total = a_ref[...].astype(F32) + b_ref[...].astype(F32) + c_ref[...].astype(F32)
+    out_ref[...] = (own_ref[...] + total + vec_ref[:, DOWN_BIAS : DOWN_BIAS + 1]).astype(BF16)
+
+
+def layer_call(own, a, b, c, vec):
+    d, rows = own.shape
+    block = pl.BlockSpec((d, 128), lambda i: (0, i))
+    return pl.pallas_call(
+        layer_kernel,
+        grid=(rows // 128,),
+        in_specs=[block] * 4 + [pl.BlockSpec(vec.shape, lambda i: (0, 0))],
+        out_specs=block,
+        out_shape=jax.ShapeDtypeStruct((d, rows), BF16),
+        compiler_params=params(),
+        cost_estimate=cost(3),
+        name="layer_call",
+    )(own, a, b, c, vec)
+
+
+def small_kernel(chunks, width, sum1_ref, *refs):
+    sums, ups, (qkv_ref, g_ref, out_ref) = refs[:chunks], refs[chunks : 2 * chunks], refs[2 * chunks :]
+    across = lambda v: jnp.sum(v, axis=1, keepdims=True)
+    columns = [across(sum1_ref[0]), across(sum1_ref[1])]
+    columns += [across(sum(ref[n] for ref in sums)) for n in range(3)]
+    columns += [across(g_ref[...].astype(F32)), across(sum(ref[0] for ref in ups))]
+    d = g_ref.shape[0]
+    qv = jnp.concatenate([qkv_ref[0:width], qkv_ref[2 * width : 3 * width]], 0)
+    qv = jnp.concatenate([across(qv), jnp.zeros((d - 2 * width, 1), F32)], 0)
+    out_ref[...] = jnp.concatenate([v.T for v in columns + [qv]], 0)
+
+
+def small_sums(sum1, sums, up_sums, qkv_sum, g):
+    return pl.pallas_call(
+        functools.partial(small_kernel, len(sums), qkv_sum.shape[0] // 3),
+        out_shape=jax.ShapeDtypeStruct((8, g.shape[0]), F32),
+        compiler_params=params(),
+        cost_estimate=cost(5),
+        name="small_sums",
+    )(sum1, *sums, *up_sums, qkv_sum, g)
 
 
 def swap(v, k):
@@ -1006,12 +1066,18 @@
     )(*args)
 
 
-def plus_second(a, pair):
-    return add(BF16, a, (pair, 1))
-
-
-def plus_first(a, pair, far, dtype=F32):
-    return add(dtype, a, (pair, 0), far)
+class GroupSum:
+    def __init__(self, line, parts):
+        self.line, self.parts = line, parts
+        self.side = swap(line.pin(parts[3]), 1)
+
+    def step(self):
+        self.far = swap(self.line(lambda a, b: add(BF16, a, b), self.parts[2], self.side), 2)
+        self.near = swap(self.line.pin(self.parts[1]), 1)
+        self.line.wait(self.near)
+
+    def terms(self):
+        return self.parts[0], self.near, self.far
 
 
 def stack_kernel(*refs):
@@ -1096,7 +1162,9 @@
     fronts, att_go = [], []
     for c in chunks:
         fronts.append(line(functools.partial(attend, c), info, start, qkv, kn))
-        att_go.append(Gather(fronts[c][0].reshape(width, SLOTS * BLK)))
+        if c == 0:
+            line.wait(g_go[0].across, g_go[0].side)
+        att_go.append(Gather(line.pin(fronts[c][0]).reshape(width, SLOTS * BLK)))
         if c == 0:
             wo_parts = wo_go.finish(line).all()
     wot = line(turn_pieces, *wo_parts)
@@ -1124,91 +1192,69 @@
             )
         )
     h2s, acts, pgs, gs, ns, roots, up_sums = zip(*[m[:7] for m in ahead])
-    own, layer0, layer2, layer13 = ahead[-1][7:]
-    layer_near = swap(layer13, 1)
+    own, *layer_parts = ahead[-1][7:]
     flat = lambda a, b: list(zip(a, b))
     y_first, z_first = (1, 2, 4), (2, 1, 4)
     f = down_weight.shape[0]
     down = CellSum(line, *line(lambda a, b: outer(flat(a, b), dp_info, y_first), acts, gs), dp_info, y_first, f)
-    layer_far = swap(line(plus_second, layer2, layer_near), 2)
     up = CellSum(line, *line(lambda a, b: outer(flat(a, b), dp_info, z_first), h2s, pgs), dp_info, z_first, d)
 
     back, attgs = [], []
     for c in chunks:
-        carry = back[-1][4:] if c else None
+        carry = back[-1][1 + SLOTS :] if c else None
         back.append(
             line(functools.partial(backward, c), info, pgs[c], ns[c], roots[c], g_own, up_weight, wo_parts, vec, carry)
         )
-        attg0, attg2, attg13 = back[c][1:4]
-        line.wait(attgs[-1][2] if c else layer_far)
-        near = swap(line.pin(attg13), 1)
-        (up if c else down).step()
-        attgs.append((attg0, near, swap(line(plus_second, attg2, near), 2)))
-    y1g0, y1g2, y1g13 = back[-1][4:]
-    y1_near = swap(line.pin(y1g13), 1)
-    down.step()
-    y1_far = swap(line(plus_second, y1g2, y1_near), 2)
-    do, stat = line(join, [a + tuple(f) for a, f in zip(attgs, fronts)])
-    dqkv = line(attend_back, info, start, qkv, kn, vn, do, stat).reshape(3 * width, total)
+        if c:
+            line.wait(attgs[-1].far, down.got, up.got)
+            up.step()
+        down.step()
+        attgs.append(GroupSum(line, back[c][1 : 1 + SLOTS]))
+        attgs[c].step()
+    y1g_parts = back[-1][1 + SLOTS :]
+    layer_sum = GroupSum(line, layer_parts)
+    out_parts = line(out_grad_call, info, atts, y1g_parts)
+    line.wait(attgs[-1].far, down.got, up.got, layer_sum.side)
+    out = GroupSum(line, out_parts)
+    do, stat = line(join, [a.terms() + tuple(f) for a, f in zip(attgs, fronts)])
+    out.step()
+    layer_sum.step()
     down.step()
     up.step()
-    line.wait(y1_far)
-    attn_parts = line(lambda a, b: outer([(a, b)], dp_info, y_first, with_sum=True), dqkv, h1)
-    attn = CellSum(line, *attn_parts[:2], dp_info, y_first, 3 * width)
+    dqkv = line(attend_back, info, start, qkv, kn, vn, do, stat).reshape(3 * width, total)
+    line.wait(down.got, up.got, out.far)
+
+    out_grad = line(lambda *v: add(BF16, *v), *out.terms())
+    y1g = GroupSum(line, y1g_parts)
+    up.step()
     down.step()
+    attn_grad, qkv_sum = line(attn_grad_call, dqkv, h1)
+    late = lax.psum((attn_grad, out_grad), "dp")
+    line.wait(up.got, down.got, layer_sum.far, y1g.side)
+    y1g.step()
     up.step()
-    sum1, h10, h12, h113 = line(h1_grad_call, w_back, dqkv, x_all)
-    h1_near = swap(line.pin(h113), 1)
     down.step()
+    sum1, *h1_parts = line(h1_grad_call, w_back, dqkv, x_all)
+    line.wait(y1g.far, up.got)
+    h1g = [h1_parts[0]] + [swap(line.pin(h1_parts[k]), k) for k in (1, 2, 3)]
     up.step()
-    h1_far = swap(line(plus_second, h12, h1_near), 2)
-    attn.step()
-    y1_grad = line(plus_first, y1g0, y1_near, y1_far)
-    out0, out2, out13 = line(lambda a, y: out_grad_call(info, a, y.astype(BF16)), atts, y1_grad)
-
-    def smalls(sum1, sums, up_sums, qkv_sum, g):
-        sum1 = jnp.sum(sum1, axis=2)
-        sum2 = jnp.sum(sum(sums), axis=2)
-        up_row = jnp.sum(sum(up_sums), axis=2)
-        qkv_sum = jnp.sum(qkv_sum[: 3 * width], axis=1).reshape(3, width)
-        down_row = jnp.sum(g.astype(F32), axis=1)
-        qv_row = jnp.pad(jnp.concatenate([qkv_sum[0], qkv_sum[2]]), (0, d - 2 * width))
-        return jnp.concatenate([sum1, sum2, down_row[None], up_row, qv_row[None]], 0)
-
-    small = line(smalls, sum1, [m[0] for m in back], up_sums, attn_parts[2], g_own)
-    up.step()
-    attn.step()
-    layer = line(
-        lambda own, a, near, far: (own + plus_first(a, near, far) + down_bias[:, None]).astype(BF16),
-        own,
-        layer0,
-        layer_near,
-        layer_far,
-    )
-    near = line(lambda a, b: add(F32, a, (b, 0)), h10, h1_near)
-    line.wait(h1_far, down.got)
-    out_near = swap(line.pin(out13), 1)
-    attn.step()
-    out_far = swap(line(plus_second, out2, out_near), 2)
+    y1_grad = line(lambda *v: add(F32, *v), *y1g.terms())
+    small = line(small_sums, sum1, [b[0] for b in back], up_sums, qkv_sum, g_own)
+    layer = line(layer_call, own, *layer_sum.terms(), vec)
+    line.wait(down.got)
     down_grad = down.finish()
-    line.wait(out_far)
+    line.wait(up.got)
+    up_grad = up.finish()
     small = Rounds(line, line.pin(small), True)
-    input_grad = line(input_grad_call, x_own, near, h1_far, y1_grad, vec)
-    attn.step()
     small.step()
-    line.wait(up.got)
-    out_sum = Rounds(line, line(lambda a, b, c: plus_first(a, b, c, BF16), out0, out_near, out_far))
+    line.wait(*h1g[1:])
+    input_grad = line(input_grad_call, x_own, *h1g, y1_grad, vec)
     small.step()
-    up_grad = up.finish()
-    out_sum.step()
-    attn.step()
     small.step()
-    out_sum.step()
     small.step()
-    out_sum.step()
     small.step()
-    out_grad = line(lambda v: v.astype(F32), out_sum.v)
-    attn_grad = attn.finish()
+    line.wait(late)
+    attn_grad, out_grad = (v.astype(F32) for v in line(lambda a, b: (a, b), *late))
     small, own_small = small.v, small.cells[6:]
     return (
         layer.T,

time: 561 us -> 494 us (0.88)
  waiting for transfers between devices: 126 us -> 87.1 us
  Pallas kernels: 324 us -> 308 us
  between operations: 1.52 us -> 14.9 us
  other arithmetic: 15 us -> 6.08 us
  starting transfers between devices: 50.3 us -> 42.5 us
  local copies, waits for them, and re-layouts: 34.1 us -> 26.5 us
    ppermute x24 -> x15, waiting for transfers between devices: 114 us -> 50.2 us  [swap_dp(): return lax.ppermute(v, 'dp', [(i, i ^ k) for i in range(8)])]
    pallas_call x4 -> x6, Pallas kernels: 25.1 us -> 46.7 us  [the longest x2 13.5 us: place(): pl.pallas_call(functools.partial(place_kernel, count), grid_spec=spec, ou...]
    pallas_call x21 -> x14, Pallas kernels: 45.9 us -> 28.8 us  [add(): pl.pallas_call(add_kernel, grid=(rows // size,), in_specs=in_specs, out_s...]
    ppermute x32 -> x38, waiting for transfers between devices: 12.4 us -> 25.6 us  [swap(): return lax.ppermute(v, 'tensor', [(i, i ^ k) for i in range(SLOTS)])]
    pallas_call x3 -> x2, Pallas kernels: 34.8 us -> 23.2 us  [outer(): pl.pallas_call(functools.partial(outer_kernel, len(pairs), order, with_su...]
    psum x0 -> x1, waiting for transfers between devices: none -> 11.3 us  [body(): late = lax.psum((attn_grad, out_grad), 'dp')]
    ppermute x24 -> x15, starting transfers between devices: 30.8 us -> 20 us  [swap_dp(): return lax.ppermute(v, 'dp', [(i, i ^ k) for i in range(8)])]
    unnamed x116 -> x118, local copies, waits for them, and re-layouts: 25.6 us -> 15.6 us
  transfers between devices with their start and end apart: 56 -> 54, of which waited for: 16 -> 25; matrix products, arithmetic and copies ran while one was open for 4% -> 3% of each run, Pallas kernels for 49% -> 52%
where the time goes in v3:
time: 494 us; the launch traced here: 485 us
  Pallas kernels  308 us (62%)
  waiting for transfers between devices  87.1 us (18%)
  starting transfers between devices  42.5 us (9%)
  local copies, waits for them, and re-layouts  26.5 us (5%)
  between operations  14.9 us (3%)
  other arithmetic  6.08 us (1%)
    pallas_call x2, Pallas kernels, forward(): pl.pallas_call(forward_kernel, grid_spec=spec, out_shape=[shape((d, wide)...  54 us
    ppermute x15, waiting for transfers between devices, swap_dp(): return lax.ppermute(v, 'dp', [(i, i ^ k) for i in range(8)])  50.2 us
    pallas_call x2, Pallas kernels, backward(): pl.pallas_call(backward_kernel, grid_spec=spec, out_shape=[shape((3, d, 1...  35 us
    pallas_call x14, Pallas kernels, add(): pl.pallas_call(add_kernel, grid=(rows // size,), in_specs=in_specs, out_s...  28.8 us
    ppermute x38, waiting for transfers between devices, swap(): return lax.ppermute(v, 'tensor', [(i, i ^ k) for i in range(SLOTS)])  25.6 us
    pallas_call x2, Pallas kernels, outer(): pl.pallas_call(functools.partial(outer_kernel, len(pairs), order, with_su...  23.2 us
    pallas_call x1, Pallas kernels, attend_back(): pl.pallas_call(functools.partial(attend_back_kernel, heads, nb, per), gri...  22.6 us
    ppermute x38, starting transfers between devices, swap(): return lax.ppermute(v, 'tensor', [(i, i ^ k) for i in range(SLOTS)])  22.5 us
  transfers between devices with their start and end apart: 54, of which 25 were waited for; matrix products, arithmetic and copies ran while one was open for 3% of the time, Pallas kernels for 52%

profile of v3, /device:TPU:0, one launch (start us, length us, event | category | flops | bytes accessed | tf_op | source)
XLA Modules:
  0.0 485.2 jit_solution(6635901995161419911)
XLA Ops:
  7.7 2.6 collective-permute-start
  16.7 9.2 %turn.1 = (bf16[1120,1120]{1,0:T(8,128)(2,1)}, bf16[1120,1120]{1,0:T(8,128)(2,1)}, bf16[1120,840]{1,0:T(8,128)(2,1)}, f32[1120,8]{1,0:T(8,128)}, f32[280,8]{1,0:...) custom-call(bf16[1120,1120]{1,0:T(8,128)(2,1)} %up.1, bf16[1120,1120]{1,0:T(8,128)(2,1)} %refs_10_.1, ...), custom_call_target="tpu_custom_call" | custom-call | flops 1 | bytes 1 | tf_op jit(solution)/shard_map/turn/pallas_call | solution.py:83
  27.0 8.3 %qkv_call.2 = (bf16[1120,2048]{1,0:T(8,128)(2,1)}, bf16[1120,2048]{1,0:T(8,128)(2,1)}, bf16[15,56,2048]{2,1,0:T(8,128)(2,1)}, bf16[5,2048,56]{2,1,0:T(8,128)(2,1)}, bf16[5,2048,56]{2,1,0:T(8,128)(2,1)}) custom-call(bf16[1120,512]{1,0:T(8,128)(2,1)} %bitcast.45, bf16[1120,512]{1,0:T(8,128)(2,1)} %copy-done.24, bf16[3,280,1120]{2,1,0:T(8,128)(2,1)} %bitcast.33, ...), custom_call_target="tpu_custom_call" | custom-call | flops 1 | bytes 1 | tf_op jit(solution)/shard_map/qkv_call/pallas_call | solution.py:177
  39.3 8.2 %qkv_call.3 = (bf16[1120,2048]{1,0:T(8,128)(2,1)}, bf16[1120,2048]{1,0:T(8,128)(2,1)}, bf16[15,56,2048]{2,1,0:T(8,128)(2,1)}, bf16[5,2048,56]{2,1,0:T(8,128)(2,1)}, bf16[5,2048,56]{2,1,0:T(8,128)(2,1)}) custom-call(bf16[1120,512]{1,0:T(8,128)(2,1)} %copy-done.27, ...), custom_call_target="tpu_custom_call", output_to_operand_aliasing={{0}: (5, {}), {1}: (6, {}), {2}: (7, {}), {3}: (8, {}), {4}... | custom-call | flops 1 | bytes 1 | tf_op jit(solution)/shard_map/qkv_call/pallas_call | solution.py:177
  50.9 11.4 %attend.2 = (bf16[5,56,1024]{2,1,0:T(8,128)(2,1)}, f32[8,1024]{1,0:T(8,128)}) custom-call(s32[25]{0:T(128)} %pad_add_fusion.info, s32[1,2048]{1,0:T(1,128)} %compare_select_fusion.start_ref, bf16[15,56,2048]{2,1,0:T(8,128)(2,1)} %get-tuple-element.598.q_ref.v_ref.k_ref, bf16[5,2048,56]{2,1,0:T(8,128)(2,1)} %get-tuple-element.599.kn_ref, ...), custom_call_target="tpu_custom_call" | custom-call | flops 1 | bytes 1 | tf_op jit(solution)/shard_map/attend/pallas_call | solution.py:256
  62.3 3.7 collective-permute-done.3.refs_6_
  68.8 10.0 %attend.3 = (bf16[5,56,1024]{2,1,0:T(8,128)(2,1)}, f32[8,1024]{1,0:T(8,128)}) custom-call(s32[25]{0:T(128)} %pad_add_fusion.info, s32[1,2048]{1,0:T(1,128)} %compare_select_fusion.start_ref, bf16[15,56,2048]{2,1,0:T(8,128)(2,1)} %get-tuple-element.598.q_ref.v_ref.k_ref, bf16[5,2048,56]{2,1,0:T(8,128)(2,1)} %get-tuple-element.599.kn_ref, ...), custom_call_target="tpu_custom_call" | custom-call | flops 1 | bytes 1 | tf_op jit(solution)/shard_map/attend/pallas_call | solution.py:256
  79.8 5.3 %turn_pieces.1.refs_8_ = bf16[1120,1120]{1,0:T(8,128)(2,1)} custom-call(bf16[280,1120]{1,0:T(8,128)(2,1)} %refs_0_.3, bf16[280,1120]{1,0:T(8,128)(2,1)} %copy-done.2, bf16[280,1120]{1,0:T(8,128)(2,1)} %copy-done.1, bf16[280,1120]{1,0:T(8,128)(2,1)} %copy-done.3), custom_call_target="tpu_custom_call" | custom-call | flops 1 | bytes 1 | tf_op jit(solution)/shard_map/turn_pieces/pallas_call | solution.py:101
  88.7 27.1 %forward.2 = (bf16[1120,1024]{1,0:T(8,128)(2,1)}, bf16[1120,1024]{1,0:T(8,128)(2,1)}, bf16[1120,1024]{1,0:T(8,128)(2,1)}, bf16[1120,1024]{1,0:T(8,128)(2,1)}, bf...) custom-call(s32[25]{0:T(128)} %pad_add_fusion.info, ...), custom_call_target="tpu_custom_call" | custom-call | flops 1 | bytes 1 | tf_op jit(solution)/shard_map/forward/pallas_call | solution.py:513
  119.8 26.9 %forward.3 = (bf16[1120,1024]{1,0:T(8,128)(2,1)}, bf16[1120,1024]{1,0:T(8,128)(2,1)}, bf16[1120,1024]{1,0:T(8,128)(2,1)}, bf16[1120,1024]{1,0:T(8,128)(2,1)}, bf...) custom-call(s32[25]{0:T(128)} %pad_add_fusion.info, ...), custom_call_target="tpu_custom_call", output_to_operand_aliasing={{7}: (15, {}), {8}: (16, {}), {9}: (17, {}), {10}: (18, {})... | custom-call | flops 1 | bytes 1 | tf_op jit(solution)/shard_map/forward/pallas_call | solution.py:513
  146.7 11.6 %outer.2 = (bf16[576,1120]{1,0:T(8,128)(2,1)}, bf16[576,1120]{1,0:T(8,128)(2,1)}) custom-call(s32[1]{0:T(128)} %bitcast.10.info, bf16[1120,1024]{1,0:T(8,128)(2,1)} %get-tuple-element.477.refs_0_, bf16[1120,1024]{1,0:T(8,128)(2,1)} %get-tuple-element.478.refs_1_, bf16[1120,1024]{1,0:T(8,128)(2,1)} %get-tuple-element.479.refs_2_, ...), custom_call_target="tpu_custom_call" | custom-call | flops 1 | bytes 1 | tf_op jit(solution)/shard_map/outer/pallas_call | solution.py:659
  160.5 11.6 %outer.3 = (bf16[576,1120]{1,0:T(8,128)(2,1)}, bf16[576,1120]{1,0:T(8,128)(2,1)}) custom-call(s32[1]{0:T(128)} %bitcast.10.info, bf16[1120,1024]{1,0:T(8,128)(2,1)} %get-tuple-element.483.refs_0_, bf16[1120,1024]{1,0:T(8,128)(2,1)} %get-tuple-element.490.refs_1_.pg_ref, bf16[1120,1024]{1,0:T(8,128)(2,1)} %get-tuple-element.485.refs_2_, ...), custom_call_target="tpu_custom_call" | custom-call | flops 1 | bytes 1 | tf_op jit(solution)/shard_map/outer/pallas_call | solution.py:659
  172.0 3.9 collective-permute-start.22
  176.0 17.8 %backward.2 = (f32[3,1120,128]{2,1,0:T(8,128)}, bf16[280,1024]{1,0:T(8,128)(2,1)}, bf16[280,1024]{1,0:T(8,128)(2,1)}, bf16[280,1024]{1,0:T(8,128)(2,1)}, bf16[28...) custom-call(s32[25]{0:T(128)} %pad_add_fusion.info, ...), custom_call_target="tpu_custom_call" | custom-call | flops 1 | bytes 1 | tf_op jit(solution)/shard_map/backward/pallas_call | solution.py:596
  194.8 3.1 halve.4
  205.1 17.3 %backward.3 = (f32[3,1120,128]{2,1,0:T(8,128)}, bf16[280,1024]{1,0:T(8,128)(2,1)}, bf16[280,1024]{1,0:T(8,128)(2,1)}, bf16[280,1024]{1,0:T(8,128)(2,1)}, bf16[28...) custom-call(s32[25]{0:T(128)} %pad_add_fusion.info, ...), custom_call_target="tpu_custom_call", output_to_operand_aliasing={{5}: (11, {}), {6}: (12, {}), {7}: (13, {}), {8}: (14, {})} | custom-call | flops 1 | bytes 1 | tf_op jit(solution)/shard_map/backward/pallas_call | solution.py:596
  223.5 3.1 halve.5
  226.6 2.4 halve.6
  237.9 13.0 %out_grad_call.1 = (bf16[280,1120]{1,0:T(8,128)(2,1)}, bf16[280,1120]{1,0:T(8,128)(2,1)}, bf16[280,1120]{1,0:T(8,128)(2,1)}, bf16[280,1120]{1,0:T(8,128)(2,1)}) custom-call(s32[25]{0:T(128)} %pad_add_fusion.info, bf16[280,1024]{1,0:T(8,128)(2,1)} %bitcast.38, bf16[280,1024]{1,0:T(8,128)(2,1)} %copy-done.14, bf16[280,1024]{1,0:T(8,128)(2,1)} %copy-done.13, ...), custom_call_target="tpu_custom_call" | custom-call | flops 1 | bytes 1 | tf_op jit(solution)/shard_map/out_grad_call/pallas_call | solution.py:869
  250.9 3.9 collective-permute-done.28.refs_1_
  255.7 5.3 %join.1 = (bf16[5,56,2048]{2,1,0:T(8,128)(2,1)}, f32[16,2048]{1,0:T(8,128)}) custom-call(bf16[5,56,1024]{2,1,0:T(8,128)(2,1)} %bitcast.50, bf16[5,56,1024]{2,1,0:T(8,128)(2,1)} %bitcast.51, bf16[5,56,1024]{2,1,0:T(8,128)(2,1)} %bitcast.52, bf16[5,56,1024]{2,1,0:T(8,128)(2,1)} %get-tuple-element.575.refs_3_, f32[8,1024]{1,0:T(8,128)} %get-tuple-element.576.refs_4_, ...), custom_call_target="tpu_custom_call" | custom-call | flops 1 | bytes 1 | tf_op jit(solution)/shard_map/join/pallas_call | solution.py:398
  266.4 2.8 add.77
  276.3 2.9 collective-permute-start.34
  280.7 22.6 %attend_back.1 = bf16[15,56,2048]{2,1,0:T(8,128)(2,1)} custom-call(s32[25]{0:T(128)} %pad_add_fusion.info, s32[1,2048]{1,0:T(1,128)} %compare_select_fusion.start_ref, bf16[15,56,2048]{2,1,0:T(8,128)(2,1)} %get-tuple-element.598.q_ref.v_ref.k_ref, bf16[15,56,2048]{2,1,0:T(8,128)(2,1)} %get-tuple-element.598.q_ref.v_ref.k_ref, ...), custom_call_target="tpu_custom_call" | custom-call | flops 1 | bytes 1 | tf_op jit(solution)/shard_map/attend_back/pallas_call | solution.py:352
  303.3 4.4 collective-permute-done.34.refs_1_.two
  307.7 2.7 add.79
  314.4 2.6 collective-permute-start.38
  317.0 8.8 %attn_grad_call.1 = (bf16[840,1120]{1,0:T(8,128)(2,1)}, f32[840,128]{1,0:T(8,128)}) custom-call(bf16[840,2048]{1,0:T(8,128)(2,1)} %bitcast.26, bf16[1120,2048]{1,0:T(8,128)(2,1)} %get-tuple-element.612.b_ref), custom_call_target="tpu_custom_call" | custom-call | flops 1 | bytes 1 | tf_op jit(solution)/shard_map/attn_grad_call/pallas_call | solution.py:679
  325.8 11.0 %collective-permute-done.38.refs_1_.two = bf16[144,1120]{1,0:T(8,128)(2,1)S(1)} collective-permute-done((bf16[144,1120]{1,0:T(8,128)(2,1)S(1)}, bf16[144,1120]{1,0:T(8,128)(2,1)S(1)}, u32[]{:S(2)}, u32[]{:S(2)}) %collective-permute-start.38) | collective-permute-done | bytes 322592 | tf_op jit(solution)/shard_map/ppermute | solution.py:770
  339.0 2.8 add.81
  347.9 2.5 stack.38
  351.5 13.7 %h1_grad_call.1 = (f32[2,1120,128]{2,1,0:T(8,128)}, bf16[1120,512]{1,0:T(8,128)(2,1)}, bf16[1120,512]{1,0:T(8,128)(2,1)}, bf16[1120,512]{1,0:T(8,128)(2,1)}, bf16[1120,512]{1,0:T(8,128)(2,1)}) custom-call(bf16[1120,840]{1,0:T(8,128)(2,1)} %get-tuple-element.623.w_ref, bf16[840,2048]{1,0:T(8,128)(2,1)} %bitcast.27, bf16[1120,2048]{1,0:T(8,128)(2,1)} %get-tuple-element.625.x_ref), custom_call_target="tpu_custom_call" | custom-call | flops 1 | bytes 1 | tf_op jit(solution)/shard_map/h1_grad_call/pallas_call | solution.py:910
  365.1 4.6 collective-permute-done.41.refs_2_
  369.8 3.3 collective-permute-done.42.refs_2_.four
  374.0 2.4 stack.39
  379.6 3.2 add.82.y1g_ref
  382.8 6.1 %small_sums.1.refs_0_ = f32[8,1120]{1,0:T(8,128)} custom-call(f32[2,1120,128]{2,1,0:T(8,128)} %get-tuple-element.637.sum1_ref, f32[3,1120,128]{2,1,0:T(8,128)} %get-tuple-element.638.refs_0_, f32[3,1120,128]{2,1,0:T(8,128)} %get-tuple-element.639.refs_1_, f32[1,1120,128]{2,1,0:T(8,128)} %get-tuple-element.640.refs_2_, ...), custom_call_target="tpu_custom_call" | custom-call | flops 1 | bytes 1 | tf_op jit(solution)/shard_map/small_sums/pallas_call | solution.py:984
  388.8 5.3 %layer_call.1 = bf16[1120,512]{1,0:T(8,128)(2,1)} custom-call(f32[1120,512]{1,0:T(8,128)} %get-tuple-element.644.own_ref, bf16[1120,512]{1,0:T(8,128)(2,1)} %get-tuple-element.645.a_ref, bf16[1120,512]{1,0:T(8,128)(2,1)} %collective-permute-done.32.b_ref, bf16[1120,512]{1,0:T(8,128)(2,1)} %collective-permute-done.33.c_ref, ...), custom_call_target="tpu_custom_call" | custom-call | flops 1 | bytes 1 | tf_op jit(solution)/shard_map/layer_call/pallas_call | solution.py:959
  394.1 11.9 %collective-permute-done.47.eight = bf16[576,1120]{1,0:T(8,128)(2,1)S(1)} collective-permute-done((bf16[576,1120]{1,0:T(8,128)(2,1)}, bf16[576,1120]{1,0:T(8,128)(2,1)S(1)}, u32[]{:S(2)}, u32[]{:S(2)}) %collective-permute-start.47) | collective-permute-done | bytes 1290272 | tf_op jit(solution)/shard_map/ppermute | solution.py:770
  407.1 6.7 %place.2 = f32[1120,1120]{1,0:T(8,128)} custom-call(s32[1]{0:T(128)} %bitcast.10.info, bf16[144,1120]{1,0:T(8,128)(2,1)} %add.78.refs_0_.one, bf16[144,1120]{1,0:T(8,128)(2,1)} %copy-done.9, bf16[288,1120]{1,0:T(8,128)(2,1)} %copy-done.11, bf16[576,1120]{1,0:T(8,128)(2,1)} %copy-done.22), custom_call_target="tpu_custom_call" | custom-call | flops 1 | bytes 1 | tf_op jit(solution)/shard_map/place/pallas_call | solution.py:757
  413.8 4.5 collective-permute-done.46.eight
  419.4 6.8 %place.3 = f32[1120,1120]{1,0:T(8,128)} custom-call(s32[1]{0:T(128)} %bitcast.10.info, bf16[144,1120]{1,0:T(8,128)(2,1)} %add.80.refs_0_.one, bf16[144,1120]{1,0:T(8,128)(2,1)} %copy-done.10, bf16[288,1120]{1,0:T(8,128)(2,1)} %copy-done.12, bf16[576,1120]{1,0:T(8,128)(2,1)} %copy-done.23), custom_call_target="tpu_custom_call" | custom-call | flops 1 | bytes 1 | tf_op jit(solution)/shard_map/place/pallas_call | solution.py:757
  426.2 3.9 collective-permute-done.48.refs_1_
  432.1 6.8 %input_grad_call.1 = bf16[1120,512]{1,0:T(8,128)(2,1)} custom-call(bf16[1120,512]{1,0:T(8,128)(2,1)} %bitcast.46, bf16[1120,512]{1,0:T(8,128)(2,1)} %get-tuple-element.664.a_ref, bf16[1120,512]{1,0:T(8,128)(2,1)} %collective-permute-done.43.b_ref, bf16[1120,512]{1,0:T(8,128)(2,1)} %collective-permute-done.44.c_ref, ...), custom_call_target="tpu_custom_call" | custom-call | flops 1 | bytes 1 | tf_op jit(solution)/shard_map/input_grad_call/pallas_call | solution.py:939
  441.0 3.0 collective-permute-start.50
  444.0 4.9 %collective-permute-done.50.refs_1_ = f32[8,1120]{1,0:T(8,128)S(1)} collective-permute-done((f32[8,1120]{1,0:T(8,128)}, f32[8,1120]{1,0:T(8,128)S(1)}, u32[]{:S(2)}, u32[]{:S(2)}) %collective-permute-start.50) | collective-permute-done | bytes 35872 | tf_op jit(solution)/shard_map/ppermute | solution.py:770
  462.3 11.3 %all-reduce.4.cloned.1.call-done = (bf16[840,1120]{1,0:T(8,128)(2,1)}, bf16[280,1120]{1,0:T(8,128)(2,1)}) async-done(((bf16[840,1120]{1,0:T(8,128)(2,1)}, bf16[280,1120]{1,0:T(8,128)(2,1)}), (bf16[840,1120]{1,0:T(8,128)(2,1)}, bf16[280,1120]{1,0:T(8,128)(2,1)})) %all-reduce.4.cloned.1.call-update) | async-done | bytes 2508816 | tf_op jit(solution)/shard_map/psum | solution.py:1232
  473.6 2.4 convert_element_type.4
  (249 shorter events, 101.0 us)
Async XLA Ops:
  7.2 466.4 %all-reduce.4.cloned.1.call-start = ((), (), s32[]{:S(2)}) async-start(), calls=%async_computation | async-start | bytes 5160960 | tf_op jit(solution)/shard_map/psum | solution.py:1232
  7.2 18.8 %collective-permute-start.1 = (bf16[1120,512]{1,0:T(8,128)(2,1)}, bf16[1120,512]{1,0:T(8,128)(2,1)S(1)}, u32[]{:S(2)}, u32[]{:S(2)}) collective-permute-start(bf16[1120,512]{1,0:T(8,128)(2,1)} %bitcast.43), channel_id=1, source_target_pairs={{0,1},{1,0},{2,3},{3,2},{4,5},{5,4},{6,7},{7,6},{8,9},{9,8},{10,11... | collective-permute-start | bytes 3440648 | tf_op jit(solution)/shard_map/ppermute | solution.py:994
  7.7 28.6 %collective-permute-start = (bf16[1120,512]{1,0:T(8,128)(2,1)}, bf16[1120,512]{1,0:T(8,128)(2,1)S(1)}, u32[]{:S(2)}, u32[]{:S(2)}) collective-permute-start(bf16[1120,512]{1,0:T(8,128)(2,1)} %bitcast.44), channel_id=1, source_target_pairs={{0,2},{1,3},{2,0},{3,1},{4,6},{5,7},{6,4},{7,5},{8,10},{9,11},{10,... | collective-permute-start | bytes 3440648 | tf_op jit(solution)/shard_map/ppermute | solution.py:994
  36.4 2.9 collective-permute-start.2
  36.7 25.6 %collective-permute-start.10 = (bf16[280,1120]{1,0:T(8,128)(2,1)S(1)}, bf16[280,1120]{1,0:T(8,128)(2,1)S(1)}, u32[]{:S(2)}, u32[]{:S(2)}) collective-permute-start(bf16[280,1120]{1,0:T(8,128)(2,1)S(1)} %copy-done), channel_id=1, source_target_pairs={{0,2},{1,3},{2,0},{3,1},{4,6},{5,7},{6,4},{7,5},{8,10},{9,11},{10,... | collective-permute-start | bytes 1881608 | tf_op jit(solution)/shard_map/ppermute | solution.py:994
  47.5 14.8 %collective-permute-start.4 = (bf16[1120,256]{1,0:T(8,128)(2,1)S(1)}, bf16[1120,256]{1,0:T(8,128)(2,1)S(1)}, u32[]{:S(2)}, u32[]{:S(2)}) collective-permute-start(bf16[1120,256]{1,0:T(8,128)(2,1)S(1)} %copy-done.36), channel_id=1, source_target_pairs={{0,1},{1,0},{2,3},{3,2},{4,5},{5,4},{6,7},{7,6},{8,9},{9,8},{10,11... | collective-permute-start | bytes 1720328 | tf_op jit(solution)/shard_map/ppermute | solution.py:994
  47.7 18.2 %collective-permute-start.3 = (bf16[1120,256]{1,0:T(8,128)(2,1)S(1)}, bf16[1120,256]{1,0:T(8,128)(2,1)S(1)}, u32[]{:S(2)}, u32[]{:S(2)}) collective-permute-start(bf16[1120,256]{1,0:T(8,128)(2,1)S(1)} %copy-done.36), channel_id=1, source_target_pairs={{0,2},{1,3},{2,0},{3,1},{4,6},{5,7},{6,4},{7,5},{8,10},{9,11},{10,... | collective-permute-start | bytes 1720328 | tf_op jit(solution)/shard_map/ppermute | solution.py:994
  50.8 27.9 %collective-permute-start.9 = (bf16[280,1120]{1,0:T(8,128)(2,1)S(1)}, bf16[280,1120]{1,0:T(8,128)(2,1)S(1)}, u32[]{:S(2)}, u32[]{:S(2)}) collective-permute-start(bf16[280,1120]{1,0:T(8,128)(2,1)S(1)} %copy-done), channel_id=1, source_target_pairs={{0,1},{1,0},{2,3},{3,2},{4,5},{5,4},{6,7},{7,6},{8,9},{9,8},{10,11... | collective-permute-start | bytes 1881608 | tf_op jit(solution)/shard_map/ppermute | solution.py:994
  66.8 12.0 %collective-permute-start.11 = (bf16[280,1120]{1,0:T(8,128)(2,1)S(1)}, bf16[280,1120]{1,0:T(8,128)(2,1)S(1)}, u32[]{:S(2)}, u32[]{:S(2)}) collective-permute-start(bf16[280,1120]{1,0:T(8,128)(2,1)S(1)} %collective-permute-done.10.refs_2_), channel_id=1, source_target_pairs={{0,1},{1,0},{2,3},{3,2},{4,5},{5,4},{6,7},{7,6},{8,9},{9,8},{10,11... | collective-permute-start | bytes 1881608 | tf_op jit(solution)/shard_map/ppermute | solution.py:994
  66.8 18.3 %collective-permute-start.8 = (bf16[280,1024]{1,0:T(8,128)(2,1)}, bf16[280,1024]{1,0:T(8,128)(2,1)S(1)}, u32[]{:S(2)}, u32[]{:S(2)}) collective-permute-start(bf16[280,1024]{1,0:T(8,128)(2,1)} %bitcast.35), channel_id=1, source_target_pairs={{0,2},{1,3},{2,0},{3,1},{4,6},{5,7},{6,4},{7,5},{8,10},{9,11},{10,... | collective-permute-start | bytes 1720328 | tf_op jit(solution)/shard_map/ppermute | solution.py:994
  68.6 19.2 %collective-permute-start.7 = (bf16[280,1024]{1,0:T(8,128)(2,1)}, bf16[280,1024]{1,0:T(8,128)(2,1)S(1)}, u32[]{:S(2)}, u32[]{:S(2)}) collective-permute-start(bf16[280,1024]{1,0:T(8,128)(2,1)} %bitcast.36), channel_id=1, source_target_pairs={{0,1},{1,0},{2,3},{3,2},{4,5},{5,4},{6,7},{7,6},{8,9},{9,8},{10,11... | collective-permute-start | bytes 1720328 | tf_op jit(solution)/shard_map/ppermute | solution.py:994
  85.1 2.6 collective-permute-start.12
  85.5 2.8 collective-permute-start.13
  85.7 30.2 %collective-permute-start.16 = (bf16[1120,256]{1,0:T(8,128)(2,1)}, bf16[1120,256]{1,0:T(8,128)(2,1)}, u32[]{:S(2)}, u32[]{:S(2)}) collective-permute-start(bf16[1120,256]{1,0:T(8,128)(2,1)} %get-tuple-element.451.refs_4_), channel_id=1, source_target_pairs={{0,2},{1,3},{2,0},{3,1},{4,6},{5,7},{6,4},{7,5},{8,10},{9,11},{10,... | collective-permute-start | bytes 1720328 | tf_op jit(solution)/shard_map/ppermute | solution.py:994
  86.0 29.9 %collective-permute-start.6 = (bf16[280,1024]{1,0:T(8,128)(2,1)S(1)}, bf16[280,1024]{1,0:T(8,128)(2,1)S(1)}, u32[]{:S(2)}, u32[]{:S(2)}) collective-permute-start(bf16[280,1024]{1,0:T(8,128)(2,1)S(1)} %bitcast.41), channel_id=1, source_target_pairs={{0,2},{1,3},{2,0},{3,1},{4,6},{5,7},{6,4},{7,5},{8,10},{9,11},{10,... | collective-permute-start | bytes 1720328 | tf_op jit(solution)/shard_map/ppermute | solution.py:994
  87.7 28.8 %collective-permute-start.5 = (bf16[280,1024]{1,0:T(8,128)(2,1)S(1)}, bf16[280,1024]{1,0:T(8,128)(2,1)S(1)}, u32[]{:S(2)}, u32[]{:S(2)}) collective-permute-start(bf16[280,1024]{1,0:T(8,128)(2,1)S(1)} %bitcast.42), channel_id=1, source_target_pairs={{0,1},{1,0},{2,3},{3,2},{4,5},{5,4},{6,7},{7,6},{8,9},{9,8},{10,11... | collective-permute-start | bytes 1720328 | tf_op jit(solution)/shard_map/ppermute | solution.py:994
  87.8 28.7 %collective-permute-start.15 = (bf16[1120,256]{1,0:T(8,128)(2,1)}, bf16[1120,256]{1,0:T(8,128)(2,1)}, u32[]{:S(2)}, u32[]{:S(2)}) collective-permute-start(bf16[1120,256]{1,0:T(8,128)(2,1)} %get-tuple-element.451.refs_4_), channel_id=1, source_target_pairs={{0,1},{1,0},{2,3},{3,2},{4,5},{5,4},{6,7},{7,6},{8,9},{9,8},{10,11... | collective-permute-start | bytes 1720328 | tf_op jit(solution)/shard_map/ppermute | solution.py:994
  116.3 2.7 collective-permute-start.17
  158.3 35.5 %collective-permute-start.18 = (bf16[576,1120]{1,0:T(8,128)(2,1)}, bf16[576,1120]{1,0:T(8,128)(2,1)S(1)}, u32[]{:S(2)}, u32[]{:S(2)}) collective-permute-start(bf16[576,1120]{1,0:T(8,128)(2,1)} %get-tuple-element.482), channel_id=1, source_target_pairs={{0,4},{4,0},{8,12},{12,8},{16,20},{20,16},{24,28},{28,24},{1,5},{5... | collective-permute-start | bytes 3870728 | tf_op jit(solution)/shard_map/ppermute | solution.py:770
  172.0 50.4 %collective-permute-start.22 = (bf16[576,1120]{1,0:T(8,128)(2,1)}, bf16[576,1120]{1,0:T(8,128)(2,1)S(1)}, u32[]{:S(2)}, u32[]{:S(2)}) collective-permute-start(bf16[576,1120]{1,0:T(8,128)(2,1)} %get-tuple-element.488), channel_id=1, source_target_pairs={{0,8},{4,12},{8,0},{12,4},{16,24},{20,28},{24,16},{28,20},{1,9},{5... | collective-permute-start | bytes 3870728 | tf_op jit(solution)/shard_map/ppermute | solution.py:770
  197.9 24.5 %collective-permute-start.21 = (bf16[288,1120]{1,0:T(8,128)(2,1)}, bf16[288,1120]{1,0:T(8,128)(2,1)S(1)}, u32[]{:S(2)}, u32[]{:S(2)}) collective-permute-start(bf16[288,1120]{1,0:T(8,128)(2,1)} %get-tuple-element.512), channel_id=1, source_target_pairs={{0,8},{4,12},{8,0},{12,4},{16,24},{20,28},{24,16},{28,20},{1,9},{5... | collective-permute-start | bytes 1935368 | tf_op jit(solution)/shard_map/ppermute | solution.py:770
  203.1 19.4 %collective-permute-start.23 = (bf16[280,1024]{1,0:T(8,128)(2,1)}, bf16[280,1024]{1,0:T(8,128)(2,1)S(1)}, u32[]{:S(2)}, u32[]{:S(2)}) collective-permute-start(bf16[280,1024]{1,0:T(8,128)(2,1)} %add.74), channel_id=1, source_target_pairs={{0,2},{1,3},{2,0},{3,1},{4,6},{5,7},{6,4},{7,5},{8,10},{9,11},{10,... | collective-permute-start | bytes 1720328 | tf_op jit(solution)/shard_map/ppermute | solution.py:994
  236.0 18.9 %collective-permute-start.26 = (bf16[1120,512]{1,0:T(8,128)(2,1)S(1)}, bf16[1120,512]{1,0:T(8,128)(2,1)S(1)}, u32[]{:S(2)}, u32[]{:S(2)}) collective-permute-start(bf16[1120,512]{1,0:T(8,128)(2,1)S(1)} %copy-done.29), channel_id=1, source_target_pairs={{0,1},{1,0},{2,3},{3,2},{4,5},{5,4},{6,7},{7,6},{8,9},{9,8},{10,11... | collective-permute-start | bytes 3440648 | tf_op jit(solution)/shard_map/ppermute | solution.py:994
  236.2 18.7 %collective-permute-start.29 = (bf16[288,1120]{1,0:T(8,128)(2,1)}, bf16[288,1120]{1,0:T(8,128)(2,1)S(1)}, u32[]{:S(2)}, u32[]{:S(2)}) collective-permute-start(bf16[288,1120]{1,0:T(8,128)(2,1)} %get-tuple-element.544), channel_id=1, source_target_pairs={{0,4},{4,0},{8,12},{12,8},{16,20},{20,16},{24,28},{28,24},{1,5},{5... | collective-permute-start | bytes 1935368 | tf_op jit(solution)/shard_map/ppermute | solution.py:770
  236.5 18.4 %collective-permute-start.27 = (bf16[280,1024]{1,0:T(8,128)(2,1)}, bf16[280,1024]{1,0:T(8,128)(2,1)S(1)}, u32[]{:S(2)}, u32[]{:S(2)}) collective-permute-start(bf16[280,1024]{1,0:T(8,128)(2,1)} %add.75), channel_id=1, source_target_pairs={{0,2},{1,3},{2,0},{3,1},{4,6},{5,7},{6,4},{7,5},{8,10},{9,11},{10,... | collective-permute-start | bytes 1720328 | tf_op jit(solution)/shard_map/ppermute | solution.py:994
  237.0 17.8 %collective-permute-start.28 = (bf16[144,1120]{1,0:T(8,128)(2,1)}, bf16[144,1120]{1,0:T(8,128)(2,1)}, u32[]{:S(2)}, u32[]{:S(2)}) collective-permute-start(bf16[144,1120]{1,0:T(8,128)(2,1)} %get-tuple-element.548), channel_id=1, source_target_pairs={{0,16},{4,20},{8,24},{12,28},{16,0},{20,4},{24,8},{28,12},{1,17},{... | collective-permute-start | bytes 967688 | tf_op jit(solution)/shard_map/ppermute | solution.py:770
  254.9 6.1 %collective-permute-start.30 = (bf16[280,1120]{1,0:T(8,128)(2,1)}, bf16[280,1120]{1,0:T(8,128)(2,1)S(1)}, u32[]{:S(2)}, u32[]{:S(2)}) collective-permute-start(bf16[280,1120]{1,0:T(8,128)(2,1)} %get-tuple-element.571), channel_id=1, source_target_pairs={{0,1},{1,0},{2,3},{3,2},{4,5},{5,4},{6,7},{7,6},{8,9},{9,8},{10,11... | collective-permute-start | bytes 1881608 | tf_op jit(solution)/shard_map/ppermute | solution.py:994
  264.1 2.3 collective-permute-start.31
  269.2 3.0 collective-permute-start.32
  269.4 33.9 %collective-permute-start.36 = (bf16[280,1120]{1,0:T(8,128)(2,1)S(1)}, bf16[280,1120]{1,0:T(8,128)(2,1)S(1)}, u32[]{:S(2)}, u32[]{:S(2)}) collective-permute-start(bf16[280,1120]{1,0:T(8,128)(2,1)S(1)} %copy-done.34), channel_id=1, source_target_pairs={{0,2},{1,3},{2,0},{3,1},{4,6},{5,7},{6,4},{7,5},{8,10},{9,11},{10,... | collective-permute-start | bytes 1881608 | tf_op jit(solution)/shard_map/ppermute | solution.py:994
  276.3 27.0 %collective-permute-start.35 = (bf16[144,1120]{1,0:T(8,128)(2,1)}, bf16[144,1120]{1,0:T(8,128)(2,1)S(1)}, u32[]{:S(2)}, u32[]{:S(2)}) collective-permute-start(bf16[144,1120]{1,0:T(8,128)(2,1)} %get-tuple-element.595), channel_id=1, source_target_pairs={{0,16},{4,20},{8,24},{12,28},{16,0},{20,4},{24,8},{28,12},{1,17},{... | collective-permute-start | bytes 967688 | tf_op jit(solution)/shard_map/ppermute | solution.py:770
  276.3 31.4 %collective-permute-start.34 = (bf16[144,1120]{1,0:T(8,128)(2,1)S(1)}, bf16[144,1120]{1,0:T(8,128)(2,1)S(1)}, u32[]{:S(2)}, u32[]{:S(2)}) collective-permute-start(bf16[144,1120]{1,0:T(8,128)(2,1)S(1)} %copy-done.4), channel_id=1, source_target_pairs={{0,16},{4,20},{8,24},{12,28},{16,0},{20,4},{24,8},{28,12},{1,17},{... | collective-permute-start | bytes 967688 | tf_op jit(solution)/shard_map/ppermute | solution.py:770
  279.3 46.5 %collective-permute-start.33 = (bf16[1120,512]{1,0:T(8,128)(2,1)}, bf16[1120,512]{1,0:T(8,128)(2,1)}, u32[]{:S(2)}, u32[]{:S(2)}) collective-permute-start(bf16[1120,512]{1,0:T(8,128)(2,1)} %add.77), channel_id=1, source_target_pairs={{0,2},{1,3},{2,0},{3,1},{4,6},{5,7},{6,4},{7,5},{8,10},{9,11},{10,... | collective-permute-start | bytes 3440648 | tf_op jit(solution)/shard_map/ppermute | solution.py:994
  310.4 28.6 %collective-permute-start.39 = (bf16[1120,512]{1,0:T(8,128)(2,1)S(1)}, bf16[1120,512]{1,0:T(8,128)(2,1)}, u32[]{:S(2)}, u32[]{:S(2)}) collective-permute-start(bf16[1120,512]{1,0:T(8,128)(2,1)S(1)} %copy-done.8), channel_id=1, source_target_pairs={{0,1},{1,0},{2,3},{3,2},{4,5},{5,4},{6,7},{7,6},{8,9},{9,8},{10,11... | collective-permute-start | bytes 3440648 | tf_op jit(solution)/shard_map/ppermute | solution.py:994
  314.4 24.6 %collective-permute-start.37 = (bf16[288,1120]{1,0:T(8,128)(2,1)}, bf16[288,1120]{1,0:T(8,128)(2,1)S(1)}, u32[]{:S(2)}, u32[]{:S(2)}) collective-permute-start(bf16[288,1120]{1,0:T(8,128)(2,1)} %stack.36), channel_id=1, source_target_pairs={{0,8},{4,12},{8,0},{12,4},{16,24},{20,28},{24,16},{28,20},{1,9},{5... | collective-permute-start | bytes 1935368 | tf_op jit(solution)/shard_map/ppermute | solution.py:770
  314.4 22.4 %collective-permute-start.38 = (bf16[144,1120]{1,0:T(8,128)(2,1)S(1)}, bf16[144,1120]{1,0:T(8,128)(2,1)S(1)}, u32[]{:S(2)}, u32[]{:S(2)}) collective-permute-start(bf16[144,1120]{1,0:T(8,128)(2,1)S(1)} %copy-done.5), channel_id=1, source_target_pairs={{0,16},{4,20},{8,24},{12,28},{16,0},{20,4},{24,8},{28,12},{1,17},{... | collective-permute-start | bytes 967688 | tf_op jit(solution)/shard_map/ppermute | solution.py:770
  341.8 3.0 collective-permute-start.40
  341.9 27.9 %collective-permute-start.41 = (bf16[1120,512]{1,0:T(8,128)(2,1)}, bf16[1120,512]{1,0:T(8,128)(2,1)S(1)}, u32[]{:S(2)}, u32[]{:S(2)}) collective-permute-start(bf16[1120,512]{1,0:T(8,128)(2,1)} %add.81), channel_id=1, source_target_pairs={{0,2},{1,3},{2,0},{3,1},{4,6},{5,7},{6,4},{7,5},{8,10},{9,11},{10,... | collective-permute-start | bytes 3440648 | tf_op jit(solution)/shard_map/ppermute | solution.py:994
  346.7 26.4 %collective-permute-start.42 = (bf16[288,1120]{1,0:T(8,128)(2,1)}, bf16[288,1120]{1,0:T(8,128)(2,1)S(1)}, u32[]{:S(2)}, u32[]{:S(2)}) collective-permute-start(bf16[288,1120]{1,0:T(8,128)(2,1)} %stack.37), channel_id=1, source_target_pairs={{0,4},{4,0},{8,12},{12,8},{16,20},{20,16},{24,28},{28,24},{1,5},{5... | collective-permute-start | bytes 1935368 | tf_op jit(solution)/shard_map/ppermute | solution.py:770
  350.4 55.6 %collective-permute-start.47 = (bf16[576,1120]{1,0:T(8,128)(2,1)}, bf16[576,1120]{1,0:T(8,128)(2,1)S(1)}, u32[]{:S(2)}, u32[]{:S(2)}) collective-permute-start(bf16[576,1120]{1,0:T(8,128)(2,1)} %stack.38), channel_id=1, source_target_pairs={{0,4},{4,0},{8,12},{12,8},{16,20},{20,16},{24,28},{28,24},{1,5},{5... | collective-permute-start | bytes 3870728 | tf_op jit(solution)/shard_map/ppermute | solution.py:770
  376.4 41.9 %collective-permute-start.46 = (bf16[576,1120]{1,0:T(8,128)(2,1)}, bf16[576,1120]{1,0:T(8,128)(2,1)S(1)}, u32[]{:S(2)}, u32[]{:S(2)}) collective-permute-start(bf16[576,1120]{1,0:T(8,128)(2,1)} %stack.39), channel_id=1, source_target_pairs={{0,8},{4,12},{8,0},{12,4},{16,24},{20,28},{24,16},{28,20},{1,9},{5... | collective-permute-start | bytes 3870728 | tf_op jit(solution)/shard_map/ppermute | solution.py:770
  377.8 54.4 %collective-permute-start.43 = (bf16[1120,512]{1,0:T(8,128)(2,1)}, bf16[1120,512]{1,0:T(8,128)(2,1)}, u32[]{:S(2)}, u32[]{:S(2)}) collective-permute-start(bf16[1120,512]{1,0:T(8,128)(2,1)} %get-tuple-element.649), channel_id=1, source_target_pairs={{0,1},{1,0},{2,3},{3,2},{4,5},{5,4},{6,7},{7,6},{8,9},{9,8},{10,11... | collective-permute-start | bytes 3440648 | tf_op jit(solution)/shard_map/ppermute | solution.py:994
  377.8 54.4 %collective-permute-start.44 = (bf16[1120,512]{1,0:T(8,128)(2,1)}, bf16[1120,512]{1,0:T(8,128)(2,1)}, u32[]{:S(2)}, u32[]{:S(2)}) collective-permute-start(bf16[1120,512]{1,0:T(8,128)(2,1)} %get-tuple-element.650), channel_id=1, source_target_pairs={{0,2},{1,3},{2,0},{3,1},{4,6},{5,7},{6,4},{7,5},{8,10},{9,11},{10,... | collective-permute-start | bytes 3440648 | tf_op jit(solution)/shard_map/ppermute | solution.py:994
  379.2 52.9 %collective-permute-start.45 = (bf16[1120,512]{1,0:T(8,128)(2,1)}, bf16[1120,512]{1,0:T(8,128)(2,1)}, u32[]{:S(2)}, u32[]{:S(2)}) collective-permute-start(bf16[1120,512]{1,0:T(8,128)(2,1)} %get-tuple-element.651), channel_id=1, source_target_pairs={{0,3},{1,2},{2,1},{3,0},{4,7},{5,6},{6,5},{7,4},{8,11},{9,10},{10,... | collective-permute-start | bytes 3440648 | tf_op jit(solution)/shard_map/ppermute | solution.py:994
  426.1 4.0 collective-permute-start.48
  432.1 6.8 %collective-permute-start.49 = (f32[8,1120]{1,0:T(8,128)}, f32[8,1120]{1,0:T(8,128)S(1)}, u32[]{:S(2)}, u32[]{:S(2)}) collective-permute-start(f32[8,1120]{1,0:T(8,128)} %add.83.refs_0_), channel_id=1, source_target_pairs={{0,8},{4,12},{8,0},{12,4},{16,24},{20,28},{24,16},{28,20},{1,9},{5... | collective-permute-start | bytes 107528 | tf_op jit(solution)/shard_map/ppermute | solution.py:770
  441.0 7.9 %collective-permute-start.50 = (f32[8,1120]{1,0:T(8,128)}, f32[8,1120]{1,0:T(8,128)S(1)}, u32[]{:S(2)}, u32[]{:S(2)}) collective-permute-start(f32[8,1120]{1,0:T(8,128)} %add.84.refs_0_), channel_id=1, source_target_pairs={{0,16},{4,20},{8,24},{12,28},{16,0},{20,4},{24,8},{28,12},{1,17},{... | collective-permute-start | bytes 107528 | tf_op jit(solution)/shard_map/ppermute | solution.py:770
  454.4 4.2 collective-permute-start.52
  (65 other events, 252.9 us)
Sparse Core Ops, SparseCore 0:
  343.6 130.0 all-reduce.3
